TPU v7x, 32 devices: a whole 2x2x4 slice. The times are simulated.
32 devices in a mesh: ctx: 8 (over z, y), ch: 4 (over x, core).
Axes of the slice: x: 2, y: 2, z: 4, core: 2. Of those that a mesh axis runs over, the one named last changes fastest.
Arguments:
- gate_medium: bfloat16 [2048, 8192], P('ctx', 'ch'), may hold values from -6 to 6
- key_medium: bfloat16 [2048, 8192], P('ctx', 'ch'), may hold values from -6 to 6
- value_medium: bfloat16 [2048, 8192], P('ctx', 'ch'), may hold values from -16 to 16
- short_medium: float32 [3, 3, 8192], P(None, None, 'ch'), may hold values from -3.5 to 3.5
- filter_medium: float32 [128, 8192], P(None, 'ch'), may hold values from -2 to 2
- skip_medium: float32 [8192], P('ch'), may hold values from -4 to 4
- norm_gain: float32 [8192], P('ch'), may hold values from 0.5 to 1.5
- gate_long: bfloat16 [2048, 8192], P('ctx', 'ch'), may hold values from -6 to 6
- key_long: bfloat16 [2048, 8192], P('ctx', 'ch'), may hold values from -6 to 6
- short_long: float32 [3, 3, 8192], P(None, None, 'ch'), may hold values from -3.5 to 3.5
- decay_rates: float32 [16, 8192], P(None, 'ch'), may hold values from 4.8828125e-06 to 0.0625
- residues: float32 [16, 8192], P(None, 'ch'), may hold values from -1.5 to 1.5
- skip_long: float32 [8192], P('ch'), may hold values from -4 to 4
Outputs:
- mixed_medium: bfloat16 [2048, 8192], P('ctx', 'ch')
- mixed_long: bfloat16 [2048, 8192], P('ctx', 'ch')
All inputs are finite; a program needn't handle non-finite values.
Results may differ from a plain program's by a relative error of at most 0.0095.
Values may be sent and summed in bfloat16 or wider, within the bound.
No kernel may reach another device: no remote copies, remote signals or barrier semaphores. Data moves between devices by JAX's collectives and lax.ppermute only.
A program may use at most 64 MiB of HBM per device.

v0:
```python
import jax
import jax.numpy as jnp
import ml_dtypes
import numpy as np
from jax import lax
from jax.experimental import pallas as pl
from jax.experimental.pallas import tpu as pltpu
from jax.sharding import PartitionSpec as P

F32 = jnp.float32
BF16 = jnp.bfloat16
BLOCK = 128
HALF = BLOCK // 2
TILE = 8
LANES = 128
WIDTH = 1024


RIM = 2 * TILE
EARLY = BLOCK + RIM


def split_np(values):
    high = values.astype(ml_dtypes.bfloat16)
    low = (values - high.astype(np.float64)).astype(ml_dtypes.bfloat16)
    return high, low


def angles(times):
    order = np.concatenate([np.arange(0, BLOCK, 2), np.arange(1, BLOCK, 2)])
    return np.pi * (order[:, None] + 0.5) * times[None, :] / BLOCK


def transforms():
    angle = angles(np.arange(BLOCK))
    forward = np.concatenate([np.cos(angle), -np.sin(angle)], 0)
    high, low = split_np(forward)
    exact_rows = np.concatenate([high, low], 1)
    split_rows = np.concatenate([high, high, low], 1)
    backward = np.concatenate(split_np(forward.T / BLOCK), 0)
    times = np.arange(-RIM, EARLY) + BLOCK - 2
    angle = angles(times)
    late = np.concatenate([np.cos(angle), -np.sin(angle)], 0).T / BLOCK
    late = late * ((times >= BLOCK - 4) & (times < 2 * BLOCK - 1))[:, None]
    return exact_rows, split_rows, backward, np.concatenate(split_np(late), 0)


def dot(a, b):
    return jnp.dot(a, b, preferred_element_type=F32)


def split(values):
    high = values.astype(BF16)
    return high, (values - high.astype(F32)).astype(BF16)


def forward_exact(matrix, block):
    return dot(matrix, jnp.concatenate([block, block], 0))


def forward_split(matrix, block):
    high, low = split(block)
    return dot(matrix, jnp.concatenate([high, low, high], 0))


def backward_split(matrix, spectrum):
    high, low = split(spectrum)
    rows = matrix.shape[0] // 2
    both = dot(matrix, high)
    return both[:rows] + both[rows:] + dot(matrix[:rows], low)


def turned(spectrum):
    even_re, odd_re, even_im, odd_im = (spectrum[i * HALF : (i + 1) * HALF] for i in range(4))
    return jnp.concatenate([-even_im, odd_im, even_re, -odd_re], 0)


def times(a, b):
    a_re, a_im, b_re, b_im = a[:BLOCK], a[BLOCK:], b[:BLOCK], b[BLOCK:]
    return jnp.concatenate([a_re * b_re - a_im * b_im, a_re * b_im + a_im * b_re], 0)


def shifted_filter(frame, weights):
    return (
        weights[0:1] * frame
        + weights[1:2] * pltpu.roll(frame, 1, 0)
        + weights[2:3] * pltpu.roll(frame, 2, 0)
    )


def rows_of(shape):
    return lax.broadcasted_iota(jnp.int32, shape, 0)


def over_channels(width, step):
    def one(i, _):
        step(pl.ds(pl.multiple_of(i * WIDTH, WIDTH), WIDTH), i * WIDTH)
        return 0

    lax.fori_loop(0, width // WIDTH, one, 0)


def sublane_sum(values):
    return jnp.sum(values, axis=0, keepdims=True)


def lane_parts(values):
    total = values[:, :LANES]
    for tile in range(1, values.shape[1] // LANES):
        total = total + values[:, tile * LANES : (tile + 1) * LANES]
    return total


def pack_kernel(key_top, key_low, value_top, value_low, gate, gate_long, key_long, short, out):
    key = jnp.concatenate([key_top[...], key_low[...]], 0).astype(F32)
    value = jnp.concatenate([value_top[...], value_low[...]], 0).astype(F32)
    product = shifted_filter(key, short[1]) * shifted_filter(value, short[2])
    product = pltpu.roll(product, product.shape[0] - 2, 0)
    row = rows_of((TILE, key.shape[1]))
    key_end, value_end = key[-TILE:], value[-TILE:]
    gate_end = gate[...].astype(F32)[TILE:]
    gate_long_end = gate_long[...].astype(F32)[TILE:]
    key_long_end = key_long[...].astype(F32)[TILE:]
    first = jnp.where(
        row < 2, pltpu.roll(key_end, 2, 0), jnp.where(row < 4, pltpu.roll(value_end, 4, 0), gate_end)
    )
    second = jnp.where(
        row < 2,
        pltpu.roll(gate_long_end, 2, 0),
        jnp.where(row < 4, pltpu.roll(key_long_end, 4, 0), product[TILE:RIM]),
    )
    out[...] = jnp.concatenate([first, second, product[RIM:]], 0).astype(BF16)


def mode_tables(rates, mode, lanes, offset, sign):
    rate = jnp.broadcast_to(rates[mode : mode + 1, lanes], (TILE, LANES))
    row = rows_of((TILE, LANES)).astype(F32)
    return jnp.exp(-rate * (offset + sign * row)), jnp.exp(-TILE * rate)


def response(starts, steps, count, emit):
    parts = list(starts)
    for i in range(count):
        level = parts
        while len(level) > 1:
            level = [a + b for a, b in zip(level[::2], level[1::2])]
        emit(i, level[0])
        if i + 1 < count:
            parts = [part * step for part, step in zip(parts, steps)]


def lane_tiles(base):
    return [
        pl.ds(pl.multiple_of(base + tile * LANES, LANES), LANES) for tile in range(WIDTH // LANES)
    ]


def impulse_kernel(count, place, rates, weights, split_rows, long_hat, carry, impulse):
    modes, width = rates.shape
    rows = impulse.shape[0]
    for i, weight in enumerate(carry_weights(place[0], count, rows, rates[...])):
        carry[i] = weight

    def step(here, base):
        for tile, lanes in enumerate(lane_tiles(base)):
            starts, steps = [], []
            for mode in range(modes):
                lead, decay = mode_tables(rates, mode, lanes, 0.0, 1.0)
                starts.append(lead * weights[mode : mode + 1, lanes])
                steps.append(decay)

            def emit(i, total):
                impulse[i * TILE : (i + 1) * TILE, tile * LANES : (tile + 1) * LANES] = total

            response(starts, steps, rows // TILE, emit)
        for block in range(rows // BLOCK):
            long_hat[block, :, here] = forward_split(
                split_rows[...], impulse[block * BLOCK : (block + 1) * BLOCK]
            )
        for block in reversed(range(1, rows // BLOCK)):
            long_hat[block, :, here] = long_hat[block, :, here] + turned(
                long_hat[block - 1, :, here]
            )

    over_channels(width, step)


def own_kernel(
    gate, key, value, key_long, short, short_long, skip, taps, split_rows, exact_rows, backward,
    conv_early, gate_early, mixed_late, squares_late, key_feat, taps_hat, heads,
):
    rows = gate.shape[0]

    @pl.when(pl.program_id(0) == 0)
    def _():
        squares_late[...] = jnp.zeros(squares_late.shape, F32)

    taps_hat[...] = forward_split(split_rows[...], taps[...])
    keys, values, gates = (ref[...].astype(F32) for ref in (key, value, gate))
    keys_long = key_long[...].astype(F32)
    heads[...] = jnp.concatenate(
        [part[:TILE] for part in (keys, values, gates, keys_long)] + [taps[BLOCK - TILE :]], 0
    )
    product = shifted_filter(keys, short[1]) * shifted_filter(values, short[2])
    row = rows_of((TILE, WIDTH))
    product = jnp.concatenate(
        [jnp.where(row < 2, 0.0, product[:TILE]), product[TILE:]], 0
    ).astype(BF16)
    before = None
    conv = []
    for block in range(rows // BLOCK):
        now = forward_exact(exact_rows[...], product[block * BLOCK : (block + 1) * BLOCK])
        window = now if before is None else now + turned(before)
        conv.append(backward_split(backward[...], times(taps_hat[...], window)))
        before = now
    total = jnp.concatenate(conv, 0) + skip[...] * product.astype(F32)
    feat = shifted_filter(gates, short[0])
    conv_early[...] = total[:EARLY]
    gate_early[...] = feat[:EARLY]
    mixed = (feat[EARLY:] * total[EARLY:]).astype(BF16)
    mixed_late[...] = mixed
    kept = mixed.astype(F32)
    squares_late[...] = squares_late[...] + lane_parts(kept * kept)
    key_feat[...] = shifted_filter(keys_long, short_long[1])


def medium_kernel(
    halo, heads, short, skip, taps_hat, exact_rows, backward,
    conv_early, gate_early, mixed_late, squares_late, _,
    mixed, mixed_rim, squares, rim_long, total,
):
    width = halo.shape[1]
    total[...] = jnp.zeros(total.shape, F32)

    def step(here, base):
        halo_part = halo[:, here].astype(F32)
        rim, rim_late = halo_part[:TILE], halo_part[TILE:RIM]
        rim_long[:, here] = rim_late
        row = rows_of((TILE, WIDTH))
        key_part, value_part, gate_part, _, tail = (
            heads[i * TILE : (i + 1) * TILE, here] for i in range(5)
        )
        keys = jnp.where(row >= 6, pltpu.roll(key_part, 6, 0), pltpu.roll(rim, 4, 0))
        values = jnp.where(row >= 6, pltpu.roll(value_part, 6, 0), pltpu.roll(rim, 2, 0))
        start = shifted_filter(keys, short[1, :, here]) * shifted_filter(values, short[2, :, here])
        start = start.astype(BF16).astype(F32)
        end = jnp.where(row >= 6, start, halo_part[-TILE:])
        window = jnp.concatenate([halo_part[RIM:-TILE], end], 0).astype(BF16)
        spectrum = times(taps_hat[:, here], forward_exact(exact_rows[...], window))
        late = backward_split(backward[...], spectrum)
        tap_a, tap_b, tap_c = (tail[i : i + 1] for i in (7, 6, 5))
        far_a, far_b, far_c = (rim_late[i : i + 1] for i in (5, 6, 7))
        skip_part = skip[:, here]
        rim_conv = late[TILE:RIM] + skip_part * pltpu.roll(end, 2, 0)
        rim_conv = rim_conv + jnp.where(
            row == 6, tap_a * far_a + tap_b * far_b + tap_c * far_c, tap_a * far_b + tap_b * far_c
        )
        rim_conv = jnp.where(row >= 6, rim_conv, 0.0)
        early = conv_early[:, here] + late[RIM:]
        extra = skip_part * jnp.where(row < 2, pltpu.roll(start, 2, 0), 0.0)
        extra = extra + jnp.where(row == 0, tap_a * far_c, 0.0)
        gates = shifted_filter(jnp.concatenate([rim, gate_part], 0), short[0, :, here])
        conv = jnp.concatenate([rim_conv, early[:TILE] + extra, early[TILE:]], 0)
        feat = jnp.concatenate([gates, gate_early[TILE:, here]], 0)
        result = (feat * conv).astype(BF16)
        mixed[:EARLY, here] = result[TILE:]
        mixed[EARLY:, here] = mixed_late[:, here]
        kept = result.astype(F32)
        mixed_rim[:, here] = kept[:TILE]
        total[...] = total[...] + lane_parts(kept * kept)

    over_channels(width, step)
    squares[...] = lax.dot_general(
        jnp.ones((TILE, LANES), F32),
        jnp.concatenate([total[...], squares_late[...]], 0),
        (((1,), (1,)), ((), ())),
        precision=lax.Precision.HIGHEST,
        preferred_element_type=F32,
    )


def state_kernel(
    all_width, mixed, mixed_rim, squares, gain, key_feat, heads, rim_long, short, rates,
    product_out, state, inverse,
):
    rows, width = mixed.shape
    modes = rates.shape[0]
    total = lax.dot_general(
        squares[...] * (1.0 / TILE),
        jnp.ones((TILE, LANES), F32),
        (((0,), (0,)), ((), ())),
        precision=lax.Precision.HIGHEST,
        preferred_element_type=F32,
    )
    inverse[...] = lax.rsqrt(total / all_width + 1e-06)

    def step(here, base):
        scale = jnp.concatenate([inverse[...]] * (WIDTH // LANES), 1)
        frame = jnp.concatenate([mixed_rim[:, here], mixed[:, here].astype(F32)], 0) * scale
        feat = shifted_filter(frame, short[2, :, here] * gain[:, here])[TILE:]
        keys = shifted_filter(
            jnp.concatenate(
                [pltpu.roll(rim_long[:, here], 4, 0), heads[3 * TILE : 4 * TILE, here]], 0
            ),
            short[1, :, here],
        )[TILE:]
        keys = jnp.concatenate([keys, key_feat[TILE:, here]], 0)
        rounded = (keys * feat).astype(BF16)
        product_out[:, here] = rounded
        values = rounded.astype(F32)
        for tile, lanes in enumerate(lane_tiles(base)):
            part_lanes = slice(tile * LANES, (tile + 1) * LANES)
            tails, steps = [], []
            for mode in range(modes):
                tail, decay = mode_tables(rates, mode, lanes, TILE - 1.0, -1.0)
                tails.append(tail)
                steps.append(decay)
            parts = [values[:TILE, part_lanes]] * modes
            for i in range(1, rows // TILE):
                piece = values[i * TILE : (i + 1) * TILE, part_lanes]
                parts = [part * decay + piece for part, decay in zip(parts, steps)]
            for mode in range(modes):
                state[mode : mode + 1, lanes] = sublane_sum(parts[mode] * tails[mode])

    over_channels(width, step)


def local_kernel(
    product, long_hat, skip, exact_rows, backward, gate_long, rim_long, short, mixed,
    out, gate_feat, mixed_out, done,
):
    rows, width = product.shape
    done[...] = jnp.zeros(done.shape, F32)

    def step(here, base):
        mixed_out[:, here] = mixed[:, here]
        gates = jnp.concatenate(
            [pltpu.roll(rim_long[:, here], 6, 0), gate_long[:, here].astype(F32)], 0
        )
        feat = shifted_filter(gates, short[0, :, here])[TILE:]
        gate_feat[:, here] = feat
        spectra = []
        for block in range(rows // BLOCK):
            part = slice(block * BLOCK, (block + 1) * BLOCK)
            piece = product[part, here]
            spectra.append(forward_exact(exact_rows[...], piece))
            total = times(long_hat[0, :, here], spectra[block])
            for lag in range(1, block + 1):
                total = total + times(long_hat[lag, :, here], spectra[block - lag])
            conv = backward_split(backward[...], total) + skip[:, here] * piece.astype(F32)
            out[part, here] = feat[part] * conv

    over_channels(width, step)


def finish_kernel(state, rates, weights, local, gate_feat, out):
    rows, width = local.shape
    modes = rates.shape[0]

    def step(here, base):
        for lanes in lane_tiles(base):
            starts, steps = [], []
            for mode in range(modes):
                lead, decay = mode_tables(rates, mode, lanes, 1.0, 1.0)
                starts.append(
                    lead * (weights[mode : mode + 1, lanes] * state[mode : mode + 1, lanes])
                )
                steps.append(decay)
            held = []

            def emit(i, total):
                part = slice(i * TILE, (i + 1) * TILE)
                held.append(local[part, lanes] + gate_feat[part, lanes] * total)
                if i % 2 == 1:
                    out[(i - 1) * TILE : (i + 1) * TILE, lanes] = jnp.concatenate(
                        held[-2:], 0
                    ).astype(BF16)

            response(starts, steps, rows // TILE, emit)

    over_channels(width, step)


def columns(rows, row_block=0):
    return pl.BlockSpec((rows, WIDTH), lambda j: (row_block, j))


def stacked(count, rows):
    return pl.BlockSpec((count, rows, WIDTH), lambda j: (0, 0, j))


def whole(*shape):
    return pl.BlockSpec(shape, lambda j: (0,) * len(shape))


KEPT = pl.BlockSpec(memory_space=pltpu.VMEM)
MIB = 1024 * 1024


def call(kernel, name, in_specs, out_shape, scratch=(), out_specs=None, steps=0, flops=0, moved=0, room=10):
    if out_specs is None:
        out_specs = jax.tree.map(lambda _: KEPT, out_shape)
    return pl.pallas_call(
        kernel,
        grid=(steps,) if steps else (),
        in_specs=in_specs,
        out_specs=out_specs,
        out_shape=out_shape,
        scratch_shapes=list(scratch),
        compiler_params=pltpu.CompilerParams(vmem_limit_bytes=room * MIB),
        name=name,
        cost_estimate=pl.CostEstimate(flops=flops, bytes_accessed=moved, transcendentals=0),
    )


def in_hbm(value):
    return pltpu.with_memory_space_constraint(value, pltpu.HBM)


def arr(shape, dtype):
    return jax.ShapeDtypeStruct(shape, dtype)


def passed_along(value, axis, steps):
    count = lax.axis_size(axis)
    return lax.ppermute(value, axis, [(source, source + steps) for source in range(count - steps)])


def exchanged(value, axis, flip):
    count = lax.axis_size(axis)
    return lax.ppermute(value, axis, [(source, source ^ flip) for source in range(count)])


def stages(count):
    group = 1
    while group < count:
        radix = 4 if count // group >= 4 else 2
        yield group, radix
        group *= radix


def carry_weights(place, count, row_count, rates):
    for group, radix in stages(count):
        digit = (place // group) % radix
        within = (place % group).astype(F32)
        for turn in range(radix):
            member = digit ^ turn
            behind = (digit - 1 - member).astype(F32) * group + within
            decay = jnp.exp(-rates * (row_count * jnp.maximum(behind, 0.0)))
            yield jnp.where(member < digit, decay, 0.0)
            left = ((radix - 1 - member) * group).astype(F32)
            yield jnp.exp(-rates * (row_count * left))


def carried_state(state, weights, beside):
    count = lax.axis_size("ctx")
    incoming = jnp.zeros_like(state)
    at = 0
    for group, radix in stages(count):
        if group > 1 and group * radix == count:
            state = state + beside
        sent = state.astype(BF16)
        got = [state]
        for turn in range(1, radix):
            got.append(exchanged(sent, "ctx", turn * group).astype(F32))
        for turn in range(radix):
            incoming = incoming + weights[at + 2 * turn] * got[turn]
        state = sum(weights[at + 2 * turn + 1] * got[turn] for turn in range(radix))
        at += 2 * radix
    return incoming


def body(
    gate_medium,
    key_medium,
    value_medium,
    short_medium,
    filter_medium,
    skip_medium,
    norm_gain,
    gate_long,
    key_long,
    short_long,
    decay_rates,
    residues,
    skip_long,
):
    rows, width = gate_medium.shape
    modes = decay_rates.shape[0]
    blocks = rows // BLOCK
    frame = rows + TILE
    count = lax.axis_size("ctx")
    all_width = width * lax.axis_size("ch")
    exact_rows, split_rows, backward, backward_late = (jnp.asarray(m) for m in transforms())
    gate_long_kept, short_kept = gate_long, short_medium
    gate_medium, key_medium, value_medium, gate_long, key_long, filter_medium, short_medium = (
        in_hbm(value)
        for value in (
            gate_medium, key_medium, value_medium, gate_long, key_long, filter_medium, short_medium
        )
    )
    steps = width // WIDTH
    end = rows // RIM - 1
    lower, upper = columns(BLOCK, blocks - 1), columns(RIM, end - BLOCK // RIM)
    last = columns(RIM, end)
    pack = call(
        pack_kernel, "pack",
        [upper, lower, upper, lower, last, last, last, stacked(3, 3)],
        arr((EARLY, width), BF16), out_specs=columns(EARLY), steps=steps,
    )(key_medium, key_medium, value_medium, value_medium, gate_medium, gate_long, key_long, short_medium)
    halo = passed_along(pack, "ctx", 1)

    skip_row = skip_medium[None]
    conv_early, gate_early, mixed_late, squares_late, key_feat, taps_hat, heads = call(
        own_kernel, "own",
        [
            columns(rows), columns(rows), columns(rows), columns(rows), stacked(3, 3),
            stacked(3, 3), columns(1), columns(BLOCK), whole(*split_rows.shape),
            whole(*exact_rows.shape), whole(*backward.shape),
        ],
        [
            arr((EARLY, width), F32), arr((EARLY, width), F32),
            arr((rows - EARLY, width), BF16), arr((rows - EARLY, LANES), F32),
            arr((rows, width), F32), arr((2 * BLOCK, width), F32), arr((5 * TILE, width), F32),
        ],
        out_specs=[
            columns(EARLY), columns(EARLY), columns(rows - EARLY), whole(rows - EARLY, LANES),
            columns(rows), columns(2 * BLOCK), columns(5 * TILE),
        ],
        steps=steps, flops=2000 * rows * width, moved=10 * rows * width, room=24,
    )(
        gate_medium, key_medium, value_medium, key_long, short_medium, short_long, skip_row,
        filter_medium, split_rows, exact_rows, backward,
    )

    mode_weight = residues * jnp.sqrt(-jnp.expm1(-2.0 * decay_rates))
    place = lax.axis_index("ctx").astype(jnp.int32).reshape(1)
    turns = sum(2 * radix for _, radix in stages(count))
    long_hat, carry = call(
        lambda *refs: impulse_kernel(count, *refs), "impulse",
        [pl.BlockSpec(memory_space=pltpu.SMEM)] + [KEPT] * 3,
        [arr((blocks, 2 * BLOCK, width), F32), arr((turns, modes, width), F32)],
        [pltpu.VMEM((rows, WIDTH), F32)],
        flops=2000 * rows * width, moved=10 * rows * width,
    )(place, decay_rates, mode_weight, split_rows)

    mixed_medium, mixed_rim, squares, rim_long = call(
        medium_kernel, "medium", [KEPT] * 12,
        [
            arr((rows, width), BF16), arr((TILE, width), F32), arr((TILE, frame), F32),
            arr((TILE, width), F32),
        ],
        [pltpu.VMEM((EARLY + TILE, LANES), F32)],
        flops=1000 * rows * width, moved=10 * rows * width,
    )(
        halo, heads, short_kept, skip_row, taps_hat, exact_rows, backward_late,
        conv_early, gate_early, mixed_late, squares_late, carry,
    )

    parts = [exchanged(squares, "ch", turn) for turn in range(1, lax.axis_size("ch"))]
    total_squares = squares
    for part in parts:
        total_squares = total_squares + part

    product_long, state = call(
        lambda *refs: state_kernel(all_width, *refs), "state", [KEPT] * 9,
        [arr((rows, width), BF16), arr((modes, width), F32)],
        [pltpu.VMEM((frame, LANES), F32)],
        flops=100 * rows * width, moved=10 * rows * width,
    )(
        mixed_medium, mixed_rim, total_squares, norm_gain[None], key_feat, heads, rim_long,
        short_long, decay_rates,
    )

    local, gate_feat, mixed_out, done = call(
        local_kernel, "local", [KEPT] * 9,
        [
            arr((rows, width), F32), arr((rows, width), F32), arr((rows, width), BF16),
            arr((1, width), F32),
        ],
        flops=2000 * rows * width, moved=14 * rows * width,
    )(
        product_long, long_hat, skip_long[None], exact_rows, backward, gate_long_kept, rim_long,
        short_long, mixed_medium,
    )
    incoming = carried_state(state, carry, done)
    mixed_long = call(
        finish_kernel, "finish", [KEPT] * 5, arr((rows, width), BF16),
        flops=100 * rows * width, moved=8 * rows * width,
    )(incoming, decay_rates, mode_weight, local, gate_feat)
    return (mixed_out, mixed_long)


def solution(mesh):
    placed = (
        P("ctx", "ch"),
        P("ctx", "ch"),
        P("ctx", "ch"),
        P(None, None, "ch"),
        P(None, "ch"),
        P("ch"),
        P("ch"),
        P("ctx", "ch"),
        P("ctx", "ch"),
        P(None, None, "ch"),
        P(None, "ch"),
        P(None, "ch"),
        P("ch"),
    )
    return jax.shard_map(
        body,
        mesh=mesh,
        in_specs=placed,
        out_specs=(P("ctx", "ch"), P("ctx", "ch")),
        check_vma=False,
    )
```

profile of v0, /device:TPU:0, one launch (start us, length us, event | category | flops | bytes accessed | tf_op | source)
XLA Modules:
  0.0 50.6 jit_solution(8712159164217251136)
XLA Ops:
  0.6 0.0 copy-start.6
  0.7 2.4 %pack.1 = bf16[144,2048]{1,0:T(8,128)(2,1)S(1)} custom-call(bf16[256,2048]{1,0:T(8,128)(2,1)} %key.1, bf16[256,2048]{1,0:T(8,128)(2,1)} %key.1, bf16[256,2048]{1,0:T(8,128)(2,1)} %value.1, bf16[256,2048]{1,0:T(8,128)(2,1)} %value.1, bf16[256,2048]{1,0:T(8,128)(2,1)} %gate.3, bf16[256,2048]{1,0:T(8,128)(2,1)} %gate_long.3, bf16[256,2048]{1,0:T(8,128)(2,1)} %key_long.3, ...), custom_call_target="tpu_custom_call" | custom-call | tf_op jit(solution)/shard_map/pack/pallas_call | solution.py:506
  3.1 4.9 %collective-permute-start = (bf16[144,2048]{1,0:T(8,128)(2,1)S(1)}, bf16[144,2048]{1,0:T(8,128)(2,1)S(1)}, u32[]{:S(2)}, u32[]{:S(2)}) collective-permute-start(bf16[144,2048]{1,0:T(8,128)(2,1)S(1)} %pack.1), channel_id=1, source_target_pairs={{0,4},{4,8},{8,12},{12,16},{16,20},{20,24},{24,28},{1,5},{5,9},{9,... | collective-permute-start | bytes 1769480 | tf_op jit(solution)/shard_map/ppermute | solution.py:426
  8.0 0.0 copy-start.1
  8.1 0.1 sqrt_multiply_fusion.refs_2_.weights
  8.2 3.9 %impulse.1 = (f32[2,256,2048]{2,1,0:T(8,128)S(1)}, f32[12,16,2048]{2,1,0:T(8,128)S(1)}) custom-call(s32[1]{0:T(128)} %bitcast.1.refs_0_, f32[16,2048]{1,0:T(8,128)S(1)} %copy-done.2, f32[16,2048]{1,0:T(8,128)S(1)} %sqrt_multiply_fusion.refs_2_.weights, bf16[256,384]{1,0:T(8,128)(2,1)S(1)} %copy-done.6), custom_call_target="tpu_custom_call" | custom-call | flops 1048576000 | bytes 5242880 | tf_op jit(solution)/shard_map/impulse/pallas_call | solution.py:539
  12.1 0.0 copy-start.7
  12.1 8.8 %own.1 = (f32[144,2048]{1,0:T(8,128)S(1)}, f32[144,2048]{1,0:T(8,128)S(1)}, bf16[112,2048]{1,0:T(8,128)(2,1)S(1)}, f32[112,128]{1,0:T(8,128)S(1)}, f32[256,2048]...) custom-call(bf16[256,2048]{1,0:T(8,128)(2,1)} %gate.3, bf16[256,2048]{1,0:T(8,128)(2,1)} %key.1, ...), custom_call_target="tpu_custom_call" | custom-call | flops 1048576000 | bytes 5242880 | tf_op jit(solution)/shard_map/own/pallas_call | solution.py:514
  21.0 1.9 %medium.1 = (bf16[256,2048]{1,0:T(8,128)(2,1)S(1)}, f32[8,2048]{1,0:T(8,128)S(1)}, f32[8,264]{1,0:T(8,128)S(1)}, f32[8,2048]{1,0:T(8,128)S(1)}) custom-call(bf16[144,2048]{1,0:T(8,128)(2,1)S(1)} %collective-permute-done.halo, f32[40,2048]{1,0:T(8,128)S(1)} %get-tuple-element.21.heads.refs_5_, f32[3,3,2048]{2,1,0:T(4,128)S(1)} %copy-done.3, ...), custom_call_target="tpu_custom_call" | custom-call | flops 524288000 | bytes 5242880 | tf_op jit(solution)/shard_map/medium/pallas_call | solution.py:547
  22.9 0.7 %collective-permute-start.3 = (f32[8,264]{1,0:T(8,128)S(1)}, f32[8,264]{1,0:T(8,128)S(1)}, u32[]{:S(2)}, u32[]{:S(2)}) collective-permute-start(f32[8,264]{1,0:T(8,128)S(1)} %get-tuple-element.30), channel_id=1, source_target_pairs={{0,3},{1,2},{2,1},{3,0},{4,7},{5,6},{6,5},{7,4},{8,11},{9,10},{10,... | collective-permute-start | bytes 25352 | tf_op jit(solution)/shard_map/ppermute | solution.py:431
  23.6 0.9 %collective-permute-start.2 = (f32[8,264]{1,0:T(8,128)S(1)}, f32[8,264]{1,0:T(8,128)S(1)}, u32[]{:S(2)}, u32[]{:S(2)}) collective-permute-start(f32[8,264]{1,0:T(8,128)S(1)} %get-tuple-element.30), channel_id=1, source_target_pairs={{0,2},{1,3},{2,0},{3,1},{4,6},{5,7},{6,4},{7,5},{8,10},{9,11},{10,... | collective-permute-start | bytes 25352 | tf_op jit(solution)/shard_map/ppermute | solution.py:431
  24.5 0.3 collective-permute-start.1
  24.8 1.3 %collective-permute-done.3 = f32[8,264]{1,0:T(8,128)S(1)} collective-permute-done((f32[8,264]{1,0:T(8,128)S(1)}, f32[8,264]{1,0:T(8,128)S(1)}, u32[]{:S(2)}, u32[]{:S(2)}) %collective-permute-start.3) | collective-permute-done | bytes 8480 | tf_op jit(solution)/shard_map/ppermute | solution.py:431
  26.1 1.3 %collective-permute-done.2 = f32[8,264]{1,0:T(8,128)S(1)} collective-permute-done((f32[8,264]{1,0:T(8,128)S(1)}, f32[8,264]{1,0:T(8,128)S(1)}, u32[]{:S(2)}, u32[]{:S(2)}) %collective-permute-start.2) | collective-permute-done | bytes 8480 | tf_op jit(solution)/shard_map/ppermute | solution.py:431
  27.4 4.9 %state.1 = (bf16[256,2048]{1,0:T(8,128)(2,1)S(1)}, f32[16,2048]{1,0:T(8,128)S(1)}) custom-call(bf16[256,2048]{1,0:T(8,128)(2,1)S(1)} %get-tuple-element.28.refs_0_.mixed, f32[8,2048]{1,0:T(8,128)S(1)} %get-tuple-element.29.refs_1_, f32[8,264]{1,0:T(8,128)S(1)} %add_add_fusion.refs_2_, f32[1,2048]{1,0:T(1,128)S(1)} %bitcast.39, ...), custom_call_target="tpu_custom_call" | custom-call | flops 52428800 | bytes 5242880 | tf_op jit(solution)/shard_map/state/pallas_call | solution.py:565
  32.3 2.4 %collective-permute-start.6 = (bf16[16,2048]{1,0:T(8,128)(2,1)S(1)}, bf16[16,2048]{1,0:T(8,128)(2,1)S(1)}, u32[]{:S(2)}, u32[]{:S(2)}) collective-permute-start(bf16[16,2048]{1,0:T(8,128)(2,1)S(1)} %convert_element_type.18), channel_id=1, source_target_pairs={{0,12},{4,8},{8,4},{12,0},{16,28},{20,24},{24,20},{28,16},{1,13},{... | collective-permute-start | bytes 196616 | tf_op jit(solution)/shard_map/ppermute | solution.py:431
  34.7 0.4 collective-permute-start.5
  35.2 1.0 %collective-permute-start.4 = (bf16[16,2048]{1,0:T(8,128)(2,1)S(1)}, bf16[16,2048]{1,0:T(8,128)(2,1)S(1)}, u32[]{:S(2)}, u32[]{:S(2)}) collective-permute-start(bf16[16,2048]{1,0:T(8,128)(2,1)S(1)} %convert_element_type.18), channel_id=1, source_target_pairs={{0,4},{4,0},{8,12},{12,8},{16,20},{20,16},{24,28},{28,24},{1,5},{5... | collective-permute-start | bytes 196616 | tf_op jit(solution)/shard_map/ppermute | solution.py:431
  36.2 4.5 %local.1 = (f32[256,2048]{1,0:T(8,128)S(1)}, f32[256,2048]{1,0:T(8,128)S(1)}, bf16[256,2048]{1,0:T(8,128)(2,1)}, f32[1,2048]{1,0:T(1,128)S(1)}) custom-call(bf16[256,2048]{1,0:T(8,128)(2,1)S(1)} %get-tuple-element.33.product, f32[2,256,2048]{2,1,0:T(8,128)S(1)} %get-tuple-element.34.long_hat, f32[1,2048]{1,0:T(1,128)S(1)} %bitcast.40, ...), custom_call_target="tpu_custom_call" | custom-call | flops 1048576000 | bytes 7340032 | tf_op jit(solution)/shard_map/local/pallas_call | solution.py:575
  40.7 0.1 fusion.9
  40.8 3.1 %collective-permute-start.7 = (bf16[16,2048]{1,0:T(8,128)(2,1)S(1)}, bf16[16,2048]{1,0:T(8,128)(2,1)S(1)}, u32[]{:S(2)}, u32[]{:S(2)}) collective-permute-start(bf16[16,2048]{1,0:T(8,128)(2,1)S(1)} %get-tuple-element.40), channel_id=1, source_target_pairs={{0,16},{4,20},{8,24},{12,28},{16,0},{20,4},{24,8},{28,12},{1,17},{... | collective-permute-start | bytes 196616 | tf_op jit(solution)/shard_map/ppermute | solution.py:431
  43.9 2.8 %collective-permute-done.7 = bf16[16,2048]{1,0:T(8,128)(2,1)S(1)} collective-permute-done((bf16[16,2048]{1,0:T(8,128)(2,1)S(1)}, bf16[16,2048]{1,0:T(8,128)(2,1)S(1)}, u32[]{:S(2)}, u32[]{:S(2)}) %collective-permute-start.7) | collective-permute-done | bytes 65568 | tf_op jit(solution)/shard_map/ppermute | solution.py:431
  46.7 0.1 fusion.4.state
  46.8 3.8 %finish.1 = bf16[256,2048]{1,0:T(8,128)(2,1)} custom-call(f32[16,2048]{1,0:T(8,128)S(1)} %fusion.4.state, f32[16,2048]{1,0:T(8,128)S(1)} %copy-done.2, f32[16,2048]{1,0:T(8,128)S(1)} %sqrt_multiply_fusion.refs_2_.weights, f32[256,2048]{1,0:T(8,128)S(1)} %get-tuple-element.38.local, f32[256,2048]{1,0:T(8,128)S(1)} %get-tuple-element.39.gate_feat), custom_call_target="tpu_custom_call" | custom-call | flops 52428800 | bytes 4194304 | tf_op jit(solution)/shard_map/finish/pallas_call | solution.py:587
  (28 shorter events, 0.1 us)
Async XLA Ops:
  0.6 7.5 %copy-start.6 = (bf16[256,384]{1,0:T(8,128)(2,1)S(1)}, bf16[256,384]{1,0:T(8,128)(2,1)}, u32[]{:S(2)}) copy-start(bf16[256,384]{1,0:T(8,128)(2,1)} %constant.17.clone.split_rows.refs_3_) | copy-start | bytes 589828
  0.6 7.4 %copy-start.2 = (f32[16,2048]{1,0:T(8,128)S(1)}, f32[16,2048]{1,0:T(8,128)}, u32[]{:S(2)}) copy-start(f32[16,2048]{1,0:T(8,128)} %rates.1) | copy-start | bytes 393220
  0.7 7.4 %copy-start.11 = (f32[16,2048]{1,0:T(8,128)S(1)}, f32[16,2048]{1,0:T(8,128)}, u32[]{:S(2)}) copy-start(f32[16,2048]{1,0:T(8,128)} %param.28) | copy-start | bytes 393220
  3.1 17.9 %collective-permute-start = (bf16[144,2048]{1,0:T(8,128)(2,1)S(1)}, bf16[144,2048]{1,0:T(8,128)(2,1)S(1)}, u32[]{:S(2)}, u32[]{:S(2)}) collective-permute-start(bf16[144,2048]{1,0:T(8,128)(2,1)S(1)} %pack.1), channel_id=1, source_target_pairs={{0,4},{4,8},{8,12},{12,16},{16,20},{20,24},{24,28},{1,5},{5,9},{9,... | collective-permute-start | bytes 1769480 | tf_op jit(solution)/shard_map/ppermute | solution.py:426
  8.0 4.0 %copy-start.1 = (bf16[256,256]{1,0:T(8,128)(2,1)S(1)}, bf16[256,256]{1,0:T(8,128)(2,1)}, u32[]{:S(2)}) copy-start(bf16[256,256]{1,0:T(8,128)(2,1)} %constant.16.clone.exact_rows) | copy-start | bytes 393220
  8.0 4.0 %copy-start.4 = (f32[3,3,2048]{2,1,0:T(4,128)S(1)}, f32[3,3,2048]{2,1,0:T(4,128)}, u32[]{:S(2)}) copy-start(f32[3,3,2048]{2,1,0:T(4,128)} %short.7) | copy-start | bytes 221188
  8.0 4.0 %copy-start.5 = (bf16[256,256]{1,0:T(8,128)(2,1)S(1)}, bf16[256,256]{1,0:T(8,128)(2,1)}, u32[]{:S(2)}) copy-start(bf16[256,256]{1,0:T(8,128)(2,1)} %constant.18.clone.backward) | copy-start | bytes 393220
  8.1 4.0 %copy-start.8 = (f32[2048]{0:T(1024)S(1)}, f32[2048]{0:T(1024)}, u32[]{:S(2)}) copy-start(f32[2048]{0:T(1024)} %param.22) | copy-start | bytes 24580
  12.1 8.9 %copy-start.3 = (f32[3,3,2048]{2,1,0:T(4,128)S(1)}, f32[3,3,2048]{2,1,0:T(4,128)}, u32[]{:S(2)}) copy-start(f32[3,3,2048]{2,1,0:T(4,128)} %short.6) | copy-start | bytes 221188
  12.1 8.9 %copy-start.7 = (bf16[320,256]{1,0:T(8,128)(2,1)S(1)}, bf16[320,256]{1,0:T(8,128)(2,1)}, u32[]{:S(2)}) copy-start(bf16[320,256]{1,0:T(8,128)(2,1)} %constant.19.clone.backward) | copy-start | bytes 491524
  21.0 6.4 %copy-start.9 = (f32[2048]{0:T(1024)S(1)}, f32[2048]{0:T(1024)}, u32[]{:S(2)}) copy-start(f32[2048]{0:T(1024)} %param.23) | copy-start | bytes 24580
  22.9 13.3 %copy-start = (bf16[256,2048]{1,0:T(8,128)(2,1)S(1)}, bf16[256,2048]{1,0:T(8,128)(2,1)}, u32[]{:S(2)}) copy-start(bf16[256,2048]{1,0:T(8,128)(2,1)} %gate_long.3) | copy-start | bytes 3145732
  22.9 13.3 %copy-start.10 = (f32[2048]{0:T(1024)S(1)}, f32[2048]{0:T(1024)}, u32[]{:S(2)}) copy-start(f32[2048]{0:T(1024)} %param.29) | copy-start | bytes 24580
  22.9 3.2 %collective-permute-start.3 = (f32[8,264]{1,0:T(8,128)S(1)}, f32[8,264]{1,0:T(8,128)S(1)}, u32[]{:S(2)}, u32[]{:S(2)}) collective-permute-start(f32[8,264]{1,0:T(8,128)S(1)} %get-tuple-element.30), channel_id=1, source_target_pairs={{0,3},{1,2},{2,1},{3,0},{4,7},{5,6},{6,5},{7,4},{8,11},{9,10},{10,... | collective-permute-start | bytes 25352 | tf_op jit(solution)/shard_map/ppermute | solution.py:431
  23.6 3.8 %collective-permute-start.2 = (f32[8,264]{1,0:T(8,128)S(1)}, f32[8,264]{1,0:T(8,128)S(1)}, u32[]{:S(2)}, u32[]{:S(2)}) collective-permute-start(f32[8,264]{1,0:T(8,128)S(1)} %get-tuple-element.30), channel_id=1, source_target_pairs={{0,2},{1,3},{2,0},{3,1},{4,6},{5,7},{6,4},{7,5},{8,10},{9,11},{10,... | collective-permute-start | bytes 25352 | tf_op jit(solution)/shard_map/ppermute | solution.py:431
  24.5 2.9 %collective-permute-start.1 = (f32[8,264]{1,0:T(8,128)S(1)}, f32[8,264]{1,0:T(8,128)S(1)}, u32[]{:S(2)}, u32[]{:S(2)}) collective-permute-start(f32[8,264]{1,0:T(8,128)S(1)} %get-tuple-element.30), channel_id=1, source_target_pairs={{0,1},{1,0},{2,3},{3,2},{4,5},{5,4},{6,7},{7,6},{8,9},{9,8},{10,11... | collective-permute-start | bytes 25352 | tf_op jit(solution)/shard_map/ppermute | solution.py:431
  32.3 8.4 %collective-permute-start.6 = (bf16[16,2048]{1,0:T(8,128)(2,1)S(1)}, bf16[16,2048]{1,0:T(8,128)(2,1)S(1)}, u32[]{:S(2)}, u32[]{:S(2)}) collective-permute-start(bf16[16,2048]{1,0:T(8,128)(2,1)S(1)} %convert_element_type.18), channel_id=1, source_target_pairs={{0,12},{4,8},{8,4},{12,0},{16,28},{20,24},{24,20},{28,16},{1,13},{... | collective-permute-start | bytes 196616 | tf_op jit(solution)/shard_map/ppermute | solution.py:431
  34.7 6.0 %collective-permute-start.5 = (bf16[16,2048]{1,0:T(8,128)(2,1)S(1)}, bf16[16,2048]{1,0:T(8,128)(2,1)S(1)}, u32[]{:S(2)}, u32[]{:S(2)}) collective-permute-start(bf16[16,2048]{1,0:T(8,128)(2,1)S(1)} %convert_element_type.18), channel_id=1, source_target_pairs={{0,8},{4,12},{8,0},{12,4},{16,24},{20,28},{24,16},{28,20},{1,9},{5... | collective-permute-start | bytes 196616 | tf_op jit(solution)/shard_map/ppermute | solution.py:431
  35.2 5.5 %collective-permute-start.4 = (bf16[16,2048]{1,0:T(8,128)(2,1)S(1)}, bf16[16,2048]{1,0:T(8,128)(2,1)S(1)}, u32[]{:S(2)}, u32[]{:S(2)}) collective-permute-start(bf16[16,2048]{1,0:T(8,128)(2,1)S(1)} %convert_element_type.18), channel_id=1, source_target_pairs={{0,4},{4,0},{8,12},{12,8},{16,20},{20,16},{24,28},{28,24},{1,5},{5... | collective-permute-start | bytes 196616 | tf_op jit(solution)/shard_map/ppermute | solution.py:431
  40.8 5.9 %collective-permute-start.7 = (bf16[16,2048]{1,0:T(8,128)(2,1)S(1)}, bf16[16,2048]{1,0:T(8,128)(2,1)S(1)}, u32[]{:S(2)}, u32[]{:S(2)}) collective-permute-start(bf16[16,2048]{1,0:T(8,128)(2,1)S(1)} %get-tuple-element.40), channel_id=1, source_target_pairs={{0,16},{4,20},{8,24},{12,28},{16,0},{20,4},{24,8},{28,12},{1,17},{... | collective-permute-start | bytes 196616 | tf_op jit(solution)/shard_map/ppermute | solution.py:431
where the time goes:
time: 50.8 us; the launch traced here: 50.6 us
  Pallas kernels  30.2 us (59%)
  starting transfers between devices  13.7 us (27%)
  waiting for transfers between devices  5.45 us (11%)
  between operations  0.87 us (2%)
    ppermute x7, starting transfers between devices, exchanged(): lax.ppermute(value, axis, [(source, source ^ flip) for source in range(co...  8.83 us
    pallas_call x1, Pallas kernels, body(): call(own_kernel, 'own', [columns(rows), columns(rows), columns(rows), col...  8.83 us
    ppermute x7, waiting for transfers between devices, exchanged(): lax.ppermute(value, axis, [(source, source ^ flip) for source in range(co...  5.45 us
    ppermute x1, starting transfers between devices, passed_along(): lax.ppermute(value, axis, [(source, source + steps) for source in range(c...  4.91 us
    pallas_call x1, Pallas kernels, body(): call(lambda *refs: state_kernel(all_width, *refs), 'state', [KEPT] * 9, [...  4.87 us
    pallas_call x1, Pallas kernels, body(): call(local_kernel, 'local', [KEPT] * 9, [arr((rows, width), F32), arr((ro...  4.55 us
    pallas_call x1, Pallas kernels, body(): call(lambda *refs: impulse_kernel(count, *refs), 'impulse', [pl.BlockSpec...  3.85 us
    pallas_call x1, Pallas kernels, body(): call(finish_kernel, 'finish', [KEPT] * 5, arr((rows, width), BF16), flops...  3.84 us
  transfers between devices with their start and end apart: 8, of which 3 were waited for; matrix products, arithmetic and copies ran while one was open for 0% of the time, Pallas kernels for 34%

commit v1 on v0

v1 whole, which is shorter than its diff:
```python
import jax
import jax.numpy as jnp
import ml_dtypes
import numpy as np
from jax import lax
from jax.experimental import pallas as pl
from jax.experimental.pallas import tpu as pltpu
from jax.sharding import PartitionSpec as P

F32 = jnp.float32
BF16 = jnp.bfloat16
BLOCK = 128
HALF = BLOCK // 2
TILE = 8
LANES = 128
WIDTH = 1024
PART = 512


RIM = 2 * TILE
EARLY = BLOCK + RIM


def split_np(values):
    high = values.astype(ml_dtypes.bfloat16)
    low = (values - high.astype(np.float64)).astype(ml_dtypes.bfloat16)
    return high, low


def angles(times):
    order = np.concatenate([np.arange(0, BLOCK, 2), np.arange(1, BLOCK, 2)])
    return np.pi * (order[:, None] + 0.5) * times[None, :] / BLOCK


def transforms():
    angle = angles(np.arange(BLOCK))
    forward = np.concatenate([np.cos(angle), -np.sin(angle)], 0)
    high, low = split_np(forward)
    exact_rows = np.concatenate([high, low], 1)
    split_rows = np.concatenate([high, high, low], 1)
    backward = np.concatenate(split_np(forward.T / BLOCK), 0)
    times = np.arange(-RIM, EARLY) + BLOCK - 2
    angle = angles(times)
    late = np.concatenate([np.cos(angle), -np.sin(angle)], 0).T / BLOCK
    late = late * ((times >= BLOCK - 4) & (times < 2 * BLOCK - 1))[:, None]
    return exact_rows, split_rows, backward, np.concatenate(split_np(late), 0)


def dot(a, b):
    return jnp.dot(a, b, preferred_element_type=F32)


def split(values):
    high = values.astype(BF16)
    return high, (values - high.astype(F32)).astype(BF16)


def forward_exact(matrix, block):
    return dot(matrix, jnp.concatenate([block, block], 0))


def forward_split(matrix, block):
    high, low = split(block)
    return dot(matrix, jnp.concatenate([high, low, high], 0))


def backward_exact(matrix, spectrum):
    rows = matrix.shape[0] // 2
    both = dot(matrix, spectrum.astype(BF16))
    return both[:rows] + both[rows:]


def turned(spectrum):
    even_re, odd_re, even_im, odd_im = (spectrum[i * HALF : (i + 1) * HALF] for i in range(4))
    return jnp.concatenate([-even_im, odd_im, even_re, -odd_re], 0)


def times(a, b):
    a_re, a_im, b_re, b_im = a[:BLOCK], a[BLOCK:], b[:BLOCK], b[BLOCK:]
    return jnp.concatenate([a_re * b_re - a_im * b_im, a_re * b_im + a_im * b_re], 0)


def shifted_filter(frame, weights):
    return (
        weights[0:1] * frame
        + weights[1:2] * pltpu.roll(frame, 1, 0)
        + weights[2:3] * pltpu.roll(frame, 2, 0)
    )


def ahead_filter(frame, weights):
    rows = frame.shape[0]
    return (
        weights[0:1] * pltpu.roll(frame, rows - 2, 0)
        + weights[1:2] * pltpu.roll(frame, rows - 1, 0)
        + weights[2:3] * frame
    )


def rows_of(shape):
    return lax.broadcasted_iota(jnp.int32, shape, 0)


def over_channels(width, step):
    def one(i, _):
        step(pl.ds(pl.multiple_of(i * WIDTH, WIDTH), WIDTH), i * WIDTH)
        return 0

    lax.fori_loop(0, width // WIDTH, one, 0)


def sublane_sum(values):
    return jnp.sum(values, axis=0, keepdims=True)


def lane_parts(values):
    total = values[:, :LANES]
    for tile in range(1, values.shape[1] // LANES):
        total = total + values[:, tile * LANES : (tile + 1) * LANES]
    return total


def pack_kernel(
    key, value, gate, gate_long, key_long, short, out, tops, ends, taps, arrived
):
    rows, width = key.shape
    copies = []
    for chunk in range(width // WIDTH):
        here = pl.ds(chunk * WIDTH, WIDTH)
        pairs = [(short.at[1:3, :, here], taps.at[:, :, here])]
        for i, ref in enumerate((key, value)):
            pairs.append((ref.at[rows - EARLY :, here], tops.at[i, :, here]))
        for i, ref in enumerate((gate, gate_long, key_long)):
            pairs.append((ref.at[rows - RIM :, here], ends.at[i, :, here]))
        copies.append(
            [
                pltpu.make_async_copy(source, target, arrived.at[chunk, i])
                for i, (source, target) in enumerate(pairs)
            ]
        )
    for group in copies:
        for copy in group:
            copy.start()
    for chunk in range(width // WIDTH):
        here = pl.ds(chunk * WIDTH, WIDTH)
        for copy in copies[chunk]:
            copy.wait()
        key_part, value_part = tops[0, :, here].astype(F32), tops[1, :, here].astype(F32)
        product = ahead_filter(key_part, taps[0, :, here]) * ahead_filter(
            value_part, taps[1, :, here]
        )
        row = rows_of((TILE, WIDTH))
        key_end, value_end = key_part[-TILE:], value_part[-TILE:]
        gate_end, gate_long_end, key_long_end = (
            ends[i, :, here].astype(F32)[TILE:] for i in range(3)
        )
        first = jnp.where(
            row < 2,
            pltpu.roll(key_end, 2, 0),
            jnp.where(row < 4, pltpu.roll(value_end, 4, 0), gate_end),
        )
        second = jnp.where(
            row < 2,
            pltpu.roll(gate_long_end, 2, 0),
            jnp.where(row < 4, pltpu.roll(key_long_end, 4, 0), product[TILE:RIM]),
        )
        out[:, here] = jnp.concatenate([first, second, product[RIM:]], 0).astype(BF16)


def mode_tables(rates, mode, lanes, offset, sign):
    rate = jnp.broadcast_to(rates[mode : mode + 1, lanes], (TILE, LANES))
    row = rows_of((TILE, LANES)).astype(F32)
    return jnp.exp(-rate * (offset + sign * row)), jnp.exp(-TILE * rate)


def response(starts, steps, count, emit):
    parts = list(starts)
    for i in range(count):
        level = parts
        while len(level) > 1:
            level = [a + b for a, b in zip(level[::2], level[1::2])]
        emit(i, level[0])
        if i + 1 < count:
            parts = [part * step for part, step in zip(parts, steps)]


def lane_tiles(base):
    return [
        pl.ds(pl.multiple_of(base + tile * LANES, LANES), LANES) for tile in range(WIDTH // LANES)
    ]


def impulse_kernel(count, place, rates, weights, split_rows, long_hat, carry, leads, decays, impulse):
    modes, width = rates.shape
    rows = impulse.shape[0]
    for i, weight in enumerate(carry_weights(place[0], count, rows, rates[...])):
        carry[i] = weight

    def step(here, base):
        for tile, lanes in enumerate(lane_tiles(base)):
            starts, steps = [], []
            for mode in range(modes):
                lead, decay = mode_tables(rates, mode, lanes, 0.0, 1.0)
                start = lead * weights[mode : mode + 1, lanes]
                leads[mode, :, lanes] = start * jnp.exp(-rates[mode : mode + 1, lanes])
                decays[mode, :, lanes] = decay
                starts.append(start)
                steps.append(decay)

            def emit(i, total):
                impulse[i * TILE : (i + 1) * TILE, tile * LANES : (tile + 1) * LANES] = total

            response(starts, steps, rows // TILE, emit)
        for block in range(rows // BLOCK):
            long_hat[block, :, here] = forward_split(
                split_rows[...], impulse[block * BLOCK : (block + 1) * BLOCK]
            )
        for block in reversed(range(1, rows // BLOCK)):
            long_hat[block, :, here] = long_hat[block, :, here] + turned(
                long_hat[block - 1, :, here]
            )

    over_channels(width, step)


def own_kernel(
    gate, key, value, key_long, short, short_long, skip, taps, split_rows, exact_rows, backward, _,
    conv_early, gate_early, mixed_late, squares_late, key_feat, taps_hat, heads,
):
    rows, width = gate.shape
    squares_late[...] = jnp.zeros(squares_late.shape, F32)

    def step(here, base):
        hat = forward_split(split_rows[...], taps[:, here])
        taps_hat[:, here] = hat
        keys, values, gates, keys_long = (
            ref[:, here].astype(F32) for ref in (key, value, gate, key_long)
        )
        heads[:, here] = jnp.concatenate(
            [part[:TILE] for part in (keys, values, gates, keys_long)]
            + [taps[BLOCK - TILE :, here]],
            0,
        )
        product = shifted_filter(keys, short[1, :, here]) * shifted_filter(
            values, short[2, :, here]
        )
        row = rows_of((TILE, WIDTH))
        product = jnp.concatenate(
            [jnp.where(row < 2, 0.0, product[:TILE]), product[TILE:]], 0
        ).astype(BF16)
        before = None
        conv = []
        for block in range(rows // BLOCK):
            now = forward_exact(exact_rows[...], product[block * BLOCK : (block + 1) * BLOCK])
            window = now if before is None else now + turned(before)
            conv.append(backward_exact(backward[...], times(hat, window)))
            before = now
        total = jnp.concatenate(conv, 0) + skip[:, here] * product.astype(F32)
        feat = shifted_filter(gates, short[0, :, here])
        conv_early[:, here] = total[:EARLY]
        gate_early[:, here] = feat[:EARLY]
        mixed = (feat[EARLY:] * total[EARLY:]).astype(BF16)
        mixed_late[:, here] = mixed
        kept = mixed.astype(F32)
        squares_late[...] = squares_late[...] + lane_parts(kept * kept)
        key_feat[:, here] = shifted_filter(keys_long, short_long[1, :, here])

    over_channels(width, step)


def medium_kernel(
    halo, heads, short, skip, taps_hat, exact_rows, backward,
    conv_early, gate_early, mixed_late, squares_late,
    mixed, mixed_rim, squares, rim_long, total,
):
    width = halo.shape[1]
    total[...] = jnp.zeros(total.shape, F32)

    def step(here, base):
        halo_part = halo[:, here].astype(F32)
        rim, rim_late = halo_part[:TILE], halo_part[TILE:RIM]
        rim_long[:, here] = rim_late
        row = rows_of((TILE, WIDTH))
        key_part, value_part, gate_part, _, tail = (
            heads[i * TILE : (i + 1) * TILE, here] for i in range(5)
        )
        keys = jnp.where(row >= 6, pltpu.roll(key_part, 6, 0), pltpu.roll(rim, 4, 0))
        values = jnp.where(row >= 6, pltpu.roll(value_part, 6, 0), pltpu.roll(rim, 2, 0))
        start = shifted_filter(keys, short[1, :, here]) * shifted_filter(values, short[2, :, here])
        start = start.astype(BF16).astype(F32)
        end = jnp.where(row >= 6, start, halo_part[-TILE:])
        window = jnp.concatenate([halo_part[RIM:-TILE], end], 0).astype(BF16)
        spectrum = times(taps_hat[:, here], forward_exact(exact_rows[...], window))
        late = backward_exact(backward[...], spectrum)
        tap_a, tap_b, tap_c = (tail[i : i + 1] for i in (7, 6, 5))
        far_a, far_b, far_c = (rim_late[i : i + 1] for i in (5, 6, 7))
        skip_part = skip[:, here]
        rim_conv = late[TILE:RIM] + skip_part * pltpu.roll(end, 2, 0)
        rim_conv = rim_conv + jnp.where(
            row == 6, tap_a * far_a + tap_b * far_b + tap_c * far_c, tap_a * far_b + tap_b * far_c
        )
        rim_conv = jnp.where(row >= 6, rim_conv, 0.0)
        early = conv_early[:, here] + late[RIM:]
        extra = skip_part * jnp.where(row < 2, pltpu.roll(start, 2, 0), 0.0)
        extra = extra + jnp.where(row == 0, tap_a * far_c, 0.0)
        gates = shifted_filter(jnp.concatenate([rim, gate_part], 0), short[0, :, here])
        conv = jnp.concatenate([rim_conv, early[:TILE] + extra, early[TILE:]], 0)
        feat = jnp.concatenate([gates, gate_early[TILE:, here]], 0)
        kept = (feat * conv).astype(BF16).astype(F32)
        mixed[:EARLY, here] = kept[TILE:].astype(BF16)
        mixed[EARLY:, here] = mixed_late[:, here]
        mixed_rim[:, here] = kept[:TILE]
        total[...] = total[...] + lane_parts(kept * kept)

    over_channels(width, step)
    squares[...] = lax.dot_general(
        jnp.ones((TILE, LANES), F32),
        jnp.concatenate([total[...], squares_late[...]], 0),
        (((1,), (1,)), ((), ())),
        precision=lax.Precision.HIGHEST,
        preferred_element_type=F32,
    )


def value_kernel(mixed, mixed_rim, gain, key_feat, heads, rim_long, short, rates, parts, tails):
    rows, width = mixed.shape
    modes = rates.shape[0]

    def step(here, base):
        frame = jnp.concatenate([mixed_rim[:, here], mixed[:, here].astype(F32)], 0)
        keys = shifted_filter(
            jnp.concatenate(
                [pltpu.roll(rim_long[:, here], 4, 0), heads[3 * TILE : 4 * TILE, here]], 0
            ),
            short[1, :, here],
        )[TILE:]
        keys = jnp.concatenate([keys, key_feat[TILE:, here]], 0)
        weights = short[2, :, here] * gain[:, here]
        for j in range(3):
            moved = frame if j == 0 else pltpu.roll(frame, j, 0)
            parts[j, :, here] = keys * (weights[j : j + 1] * moved[TILE:])
        for lanes in lane_tiles(base):
            for mode in range(modes):
                tails[mode, :, lanes] = mode_tables(rates, mode, lanes, TILE - 1.0, -1.0)[0]

    over_channels(width, step)


def state_kernel(all_width, squares, parts, tails, decays, product_out, state, factors):
    rows, width = product_out.shape
    modes = decays.shape[0]
    factor = lax.rsqrt(squares[...] / all_width + 1e-06)
    high, rest = split(factor)
    low = (factor - high.astype(F32) - rest.astype(F32)).astype(BF16)
    row = rows_of(factor.shape)
    stack = jnp.where(row == 0, high.astype(F32), jnp.where(row == 1, rest.astype(F32), 0.0))
    stack = jnp.where(row == 2, low.astype(F32), stack)
    stack = jnp.concatenate([stack, jnp.zeros_like(stack)], 0).astype(BF16)
    inverse = lax.dot_general(
        stack,
        jnp.ones((RIM, LANES), BF16),
        (((0,), (0,)), ((), ())),
        preferred_element_type=F32,
    )
    factors[0] = inverse[TILE:]
    factors[1] = pltpu.roll(inverse, 1, 0)[TILE:]
    factors[2] = pltpu.roll(inverse, 2, 0)[TILE:]

    def step(here, base):
        for lanes in lane_tiles(base):
            steps = [decays[mode, :, lanes] for mode in range(modes)]
            held = None
            for i in range(0, rows, 2 * TILE):
                part = slice(i, i + 2 * TILE)
                product = (
                    parts[0, part, lanes] * factors[0, part]
                    + parts[1, part, lanes] * factors[1, part]
                    + parts[2, part, lanes] * factors[2, part]
                )
                product_out[part, lanes] = product.astype(BF16)
                for piece in (product[:TILE], product[TILE:]):
                    if held is None:
                        held = [piece] * modes
                    else:
                        held = [old * decay + piece for old, decay in zip(held, steps)]
            for mode in range(modes):
                state[mode : mode + 1, lanes] = sublane_sum(held[mode] * tails[mode, :, lanes])

    over_channels(width, step)


def local_kernel(product, long_hat, skip, exact_rows, backward, out, done):
    rows, width = product.shape
    done[...] = jnp.zeros(done.shape, F32)

    def step(here, base):
        spectra = []
        for block in range(rows // BLOCK):
            part = slice(block * BLOCK, (block + 1) * BLOCK)
            piece = product[part, here]
            spectra.append(forward_exact(exact_rows[...], piece))
            total = times(long_hat[0, :, here], spectra[block])
            for lag in range(1, block + 1):
                total = total + times(long_hat[lag, :, here], spectra[block - lag])
            out[part, here] = backward_exact(backward[...], total) + skip[:, here] * piece.astype(
                F32
            )

    over_channels(width, step)


def gate_kernel(gate_long, rim_long, short, mixed, _, gate_feat, mixed_out):
    width = gate_long.shape[1]

    def step(here, base):
        gates = jnp.concatenate(
            [pltpu.roll(rim_long[:, here], 6, 0), gate_long[:, here].astype(F32)], 0
        )
        gate_feat[:, here] = shifted_filter(gates, short[0, :, here])[TILE:]
        mixed_out[:, here] = mixed[:, here]

    over_channels(width, step)


def finish_kernel(state, decays, leads, local, gate_feat, out, held_out, sent):
    rows, width = local.shape
    modes = decays.shape[0]
    copies = []
    for chunk in range(width // PART):
        for tile in range(PART // LANES):
            lanes = slice(chunk * PART + tile * LANES, chunk * PART + (tile + 1) * LANES)
            starts = [
                leads[mode, :, lanes] * state[mode : mode + 1, lanes] for mode in range(modes)
            ]
            steps = [decays[mode, :, lanes] for mode in range(modes)]
            held = []

            def emit(i, total):
                part = slice(i * TILE, (i + 1) * TILE)
                held.append(gate_feat[part, lanes] * (local[part, lanes] + total))
                if i % 2 == 1:
                    held_out[(i - 1) * TILE : (i + 1) * TILE, lanes] = jnp.concatenate(
                        held[-2:], 0
                    ).astype(BF16)

            response(starts, steps, rows // TILE, emit)
        here = pl.ds(chunk * PART, PART)
        copy = pltpu.make_async_copy(held_out.at[:, here], out.at[:, here], sent.at[chunk])
        copy.start()
        copies.append(copy)
    for copy in copies:
        copy.wait()


SCALAR = pl.BlockSpec(memory_space=pltpu.SMEM)
KEPT = pl.BlockSpec(memory_space=pltpu.VMEM)
FAR = pl.BlockSpec(memory_space=pl.ANY)
MIB = 1024 * 1024


def call(kernel, name, in_specs, out_shape, scratch=(), flops=0, moved=0, room=12, out_specs=None):
    return pl.pallas_call(
        kernel,
        in_specs=in_specs,
        out_specs=out_specs or jax.tree.map(lambda _: KEPT, out_shape),
        out_shape=out_shape,
        scratch_shapes=list(scratch),
        compiler_params=pltpu.CompilerParams(vmem_limit_bytes=room * MIB),
        name=name,
        cost_estimate=pl.CostEstimate(flops=flops, bytes_accessed=moved, transcendentals=0),
    )


def in_hbm(value):
    return pltpu.with_memory_space_constraint(value, pltpu.HBM)


def arr(shape, dtype):
    return jax.ShapeDtypeStruct(shape, dtype)


def passed_along(value, axis, steps):
    count = lax.axis_size(axis)
    return lax.ppermute(value, axis, [(source, source + steps) for source in range(count - steps)])


def exchanged(value, axis, flip):
    count = lax.axis_size(axis)
    return lax.ppermute(value, axis, [(source, source ^ flip) for source in range(count)])


def stages(count):
    group = 1
    while group < count:
        radix = 4 if count // group >= 4 else 2
        yield group, radix
        group *= radix


def carry_weights(place, count, row_count, rates):
    for group, radix in stages(count):
        digit = (place // group) % radix
        within = (place % group).astype(F32)
        for turn in range(radix):
            member = digit ^ turn
            behind = (digit - 1 - member).astype(F32) * group + within
            decay = jnp.exp(-rates * (row_count * jnp.maximum(behind, 0.0)))
            yield jnp.where(member < digit, decay, 0.0)
            left = ((radix - 1 - member) * group).astype(F32)
            yield jnp.exp(-rates * (row_count * left))


def carried_state(state, weights, beside):
    count = lax.axis_size("ctx")
    incoming = jnp.zeros_like(state)
    sent = incoming
    at = 0
    for group, radix in stages(count):
        if group > 1 and group * radix == count:
            state = state + beside
        sent = state.astype(BF16)
        got = [state]
        for turn in range(1, radix):
            got.append(exchanged(sent, "ctx", turn * group).astype(F32))
        for turn in range(radix):
            incoming = incoming + weights[at + 2 * turn] * got[turn]
        state = sum(weights[at + 2 * turn + 1] * got[turn] for turn in range(radix))
        at += 2 * radix
    return incoming, sent


def body(
    gate_medium,
    key_medium,
    value_medium,
    short_medium,
    filter_medium,
    skip_medium,
    norm_gain,
    gate_long,
    key_long,
    short_long,
    decay_rates,
    residues,
    skip_long,
):
    rows, width = gate_medium.shape
    modes = decay_rates.shape[0]
    blocks = rows // BLOCK
    frame = rows + TILE
    count = lax.axis_size("ctx")
    all_width = width * lax.axis_size("ch")
    exact_rows, split_rows, backward, backward_late = (jnp.asarray(m) for m in transforms())
    far = [
        in_hbm(value)
        for value in (key_medium, value_medium, gate_medium, gate_long, key_long, short_medium)
    ]
    pack = call(
        pack_kernel, "pack", [FAR] * 6, arr((EARLY, width), BF16),
        [
            pltpu.VMEM((2, EARLY, width), BF16), pltpu.VMEM((3, RIM, width), BF16),
            pltpu.VMEM((2, 3, width), F32), pltpu.SemaphoreType.DMA((width // WIDTH, 6)),
        ],
    )(*far)
    halo = passed_along(pack, "ctx", 1)

    skip_row = skip_medium[None]
    mode_weight = residues * jnp.sqrt(-jnp.expm1(-2.0 * decay_rates))
    place = lax.axis_index("ctx").astype(jnp.int32).reshape(1)
    turns = sum(2 * radix for _, radix in stages(count)) or 1
    long_hat, carry, leads, decays = call(
        lambda *refs: impulse_kernel(count, *refs), "impulse",
        [SCALAR] + [KEPT] * 3,
        [
            arr((blocks, 2 * BLOCK, width), F32), arr((turns, modes, width), F32),
            arr((modes, TILE, width), F32), arr((modes, TILE, width), F32),
        ],
        [pltpu.VMEM((rows, WIDTH), F32)],
        flops=2000 * rows * width, moved=10 * rows * width,
    )(place, decay_rates, mode_weight, split_rows)

    conv_early, gate_early, mixed_late, squares_late, key_feat, taps_hat, heads = call(
        own_kernel, "own", [KEPT] * 12,
        [
            arr((EARLY, width), F32), arr((EARLY, width), F32),
            arr((rows - EARLY, width), BF16), arr((rows - EARLY, LANES), F32),
            arr((rows, width), F32), arr((2 * BLOCK, width), F32), arr((5 * TILE, width), F32),
        ],
        flops=2000 * rows * width, moved=10 * rows * width, room=16,
    )(
        gate_medium, key_medium, value_medium, key_long, short_medium, short_long, skip_row,
        filter_medium, split_rows, exact_rows, backward, carry,
    )

    mixed_medium, mixed_rim, squares, rim_long = call(
        medium_kernel, "medium", [KEPT] * 11,
        [
            arr((rows, width), BF16), arr((TILE, width), F32), arr((TILE, frame), F32),
            arr((TILE, width), F32),
        ],
        [pltpu.VMEM((EARLY + TILE, LANES), F32)],
        flops=1000 * rows * width, moved=10 * rows * width,
    )(
        halo, heads, short_medium, skip_row, taps_hat, exact_rows, backward_late,
        conv_early, gate_early, mixed_late, squares_late,
    )

    parts = [exchanged(squares, "ch", turn) for turn in range(1, lax.axis_size("ch"))]
    total_squares = squares
    for part in parts:
        total_squares = total_squares + part

    long_parts, tails = call(
        value_kernel, "value", [KEPT] * 8,
        [arr((3, rows, width), F32), arr((modes, TILE, width), F32)],
        flops=1000 * rows * width, moved=10 * rows * width,
    )(
        mixed_medium, mixed_rim, norm_gain[None], key_feat, heads, rim_long, short_long,
        decay_rates,
    )
    product_long, state = call(
        lambda *refs: state_kernel(all_width, *refs), "state", [KEPT] * 4,
        [arr((rows, width), BF16), arr((modes, width), F32)],
        [pltpu.VMEM((3, rows, LANES), F32)],
        flops=100 * rows * width, moved=10 * rows * width,
    )(total_squares, long_parts, tails, decays)

    local, done = call(
        local_kernel, "local", [KEPT] * 5, [arr((rows, width), F32), arr((1, width), F32)],
        flops=2000 * rows * width, moved=14 * rows * width,
    )(product_long, long_hat, skip_long[None], exact_rows, backward)
    incoming, last_sent = carried_state(state, carry, done)
    gate_feat, mixed_out = call(
        gate_kernel, "gate", [KEPT] * 5, [arr((rows, width), F32), arr((rows, width), BF16)],
        flops=1000 * rows * width, moved=14 * rows * width,
    )(gate_long, rim_long, short_long, mixed_medium, last_sent)
    mixed_long = call(
        finish_kernel, "finish", [KEPT] * 5, arr((rows, width), BF16),
        [pltpu.VMEM((rows, width), BF16), pltpu.SemaphoreType.DMA((width // PART,))], out_specs=FAR,
        flops=100 * rows * width, moved=8 * rows * width,
    )(incoming, decays, leads, local, gate_feat)
    return (mixed_out, mixed_long)


def solution(mesh):
    placed = (
        P("ctx", "ch"),
        P("ctx", "ch"),
        P("ctx", "ch"),
        P(None, None, "ch"),
        P(None, "ch"),
        P("ch"),
        P("ch"),
        P("ctx", "ch"),
        P("ctx", "ch"),
        P(None, None, "ch"),
        P(None, "ch"),
        P(None, "ch"),
        P("ch"),
    )
    return jax.shard_map(
        body,
        mesh=mesh,
        in_specs=placed,
        out_specs=(P("ctx", "ch"), P("ctx", "ch")),
        check_vma=False,
    )
```

time: 50.8 us -> 47.2 us (0.929)
  Pallas kernels: 30.2 us -> 25.7 us
  starting transfers between devices: 13.7 us -> 14.8 us
    pallas_call x7 -> x9, Pallas kernels: 30.2 us -> 25.7 us  [the longest x1 5.97 us: body(): call(own_kernel, 'own', [KEPT] * 12, [arr((EARLY, width), F32), arr((EARL...]
    ppermute x7, waiting for transfers between devices: 5.45 us -> 3.01 us  [exchanged(): lax.ppermute(value, axis, [(source, source ^ flip) for source in range(co...]
    ppermute x1, waiting for transfers between devices: 0.01 us -> 2.08 us  [passed_along(): lax.ppermute(value, axis, [(source, source + steps) for source in range(c...]
    ppermute x7, starting transfers between devices: 8.83 us -> 9.91 us  [exchanged(): lax.ppermute(value, axis, [(source, source ^ flip) for source in range(co...]
  transfers between devices with their start and end apart: 8 -> 8, of which waited for: 3 -> 6; matrix products, arithmetic and copies ran while one was open for 0% -> 0% of each run, Pallas kernels for 34% -> 32%
where the time goes in v1:
time: 47.2 us; the launch traced here: 47.1 us
  Pallas kernels  25.7 us (54%)
  starting transfers between devices  14.8 us (31%)
  waiting for transfers between devices  5.09 us (11%)
  between operations  1.11 us (2%)
    ppermute x7, starting transfers between devices, exchanged(): lax.ppermute(value, axis, [(source, source ^ flip) for source in range(co...  9.91 us
    pallas_call x1, Pallas kernels, body(): call(own_kernel, 'own', [KEPT] * 12, [arr((EARLY, width), F32), arr((EARL...  5.97 us
    ppermute x1, starting transfers between devices, passed_along(): lax.ppermute(value, axis, [(source, source + steps) for source in range(c...  4.91 us
    pallas_call x1, Pallas kernels, body(): call(lambda *refs: impulse_kernel(count, *refs), 'impulse', [SCALAR] + [K...  4.16 us
    pallas_call x1, Pallas kernels, body(): call(lambda *refs: state_kernel(all_width, *refs), 'state', [KEPT] * 4, [...  3.46 us
    pallas_call x1, Pallas kernels, body(): call(finish_kernel, 'finish', [KEPT] * 5, arr((rows, width), BF16), [pltp...  3.12 us
    ppermute x7, waiting for transfers between devices, exchanged(): lax.ppermute(value, axis, [(source, source ^ flip) for source in range(co...  3.01 us
    pallas_call x1, Pallas kernels, body(): call(pack_kernel, 'pack', [FAR] * 6, arr((EARLY, width), BF16), [pltpu.VM...  2.29 us
  transfers between devices with their start and end apart: 8, of which 6 were waited for; matrix products, arithmetic and copies ran while one was open for 0% of the time, Pallas kernels for 32%

profile of v1, /device:TPU:0, one launch (start us, length us, event | category | flops | bytes accessed | tf_op | source)
XLA Modules:
  0.0 47.1 jit_solution(7328188880577693270)
XLA Ops:
  0.7 2.3 %pack.1 = bf16[144,2048]{1,0:T(8,128)(2,1)S(1)} custom-call(bf16[256,2048]{1,0:T(8,128)(2,1)} %key.3, bf16[256,2048]{1,0:T(8,128)(2,1)} %value.4, bf16[256,2048]{1,0:T(8,128)(2,1)} %gate.4, bf16[256,2048]{1,0:T(8,128)(2,1)} %gate_long.3, bf16[256,2048]{1,0:T(8,128)(2,1)} %key_long.3, f32[3,3,2048]{2,1,0:T(4,128)} %short.7), custom_call_target="tpu_custom_call" | custom-call | tf_op jit(solution)/shard_map/pack/pallas_call | solution.py:558
  3.0 4.9 %collective-permute-start = (bf16[144,2048]{1,0:T(8,128)(2,1)S(1)}, bf16[144,2048]{1,0:T(8,128)(2,1)S(1)}, u32[]{:S(2)}, u32[]{:S(2)}) collective-permute-start(bf16[144,2048]{1,0:T(8,128)(2,1)S(1)} %pack.1), channel_id=1, source_target_pairs={{0,4},{4,8},{8,12},{12,16},{16,20},{20,24},{24,28},{1,5},{5,9},{9,... | collective-permute-start | bytes 1769480 | tf_op jit(solution)/shard_map/ppermute | solution.py:484
  8.0 0.1 sqrt_multiply_fusion.refs_2_
  8.1 4.2 %impulse.1 = (f32[2,256,2048]{2,1,0:T(8,128)S(1)}, f32[12,16,2048]{2,1,0:T(8,128)S(1)}, f32[16,8,2048]{2,1,0:T(8,128)S(1)}, f32[16,8,2048]{2,1,0:T(8,128)S(1)}) custom-call(s32[1]{0:T(128)} %bitcast.1.refs_0_, f32[16,2048]{1,0:T(8,128)S(1)} %copy-done.10, f32[16,2048]{1,0:T(8,128)S(1)} %sqrt_multiply_fusion.refs_2_, bf16[256,384]{1,0:T(8,128)(2,1)S(1)} %copy-done.11), custom_call_target="tpu_custom_call" | custom-call | flops 1048576000 | bytes 5242880 | tf_op jit(solution)/shard_map/impulse/pallas_call | solution.py:571
  12.4 6.0 %own.1 = (f32[144,2048]{1,0:T(8,128)S(1)}, f32[144,2048]{1,0:T(8,128)S(1)}, bf16[112,2048]{1,0:T(8,128)(2,1)S(1)}, f32[112,128]{1,0:T(8,128)S(1)}, f32[256,2048]...) custom-call(bf16[256,2048]{1,0:T(8,128)(2,1)S(1)} %copy-done.3, bf16[256,2048]{1,0:T(8,128)(2,1)S(1)} %copy-done.1, ...), custom_call_target="tpu_custom_call" | custom-call | flops 1048576000 | bytes 5242880 | tf_op jit(solution)/shard_map/own/pallas_call | solution.py:582
  18.4 2.1 %collective-permute-done.halo = bf16[144,2048]{1,0:T(8,128)(2,1)S(1)} collective-permute-done((bf16[144,2048]{1,0:T(8,128)(2,1)S(1)}, bf16[144,2048]{1,0:T(8,128)(2,1)S(1)}, u32[]{:S(2)}, u32[]{:S(2)}) %collective-permute-start) | collective-permute-done | bytes 589856 | tf_op jit(solution)/shard_map/ppermute | solution.py:484
  20.5 1.6 %medium.1 = (bf16[256,2048]{1,0:T(8,128)(2,1)S(1)}, f32[8,2048]{1,0:T(8,128)S(1)}, f32[8,264]{1,0:T(8,128)S(1)}, f32[8,2048]{1,0:T(8,128)S(1)}) custom-call(bf16[144,2048]{1,0:T(8,128)(2,1)S(1)} %collective-permute-done.halo, f32[40,2048]{1,0:T(8,128)S(1)} %get-tuple-element.26.heads, f32[3,3,2048]{2,1,0:T(4,128)S(1)} %copy-done.7, f32[1,2048]{1,0:T(1,128)S(1)} %bitcast.38, ...), custom_call_target="tpu_custom_call" | custom-call | flops 524288000 | bytes 5242880 | tf_op jit(solution)/shard_map/medium/pallas_call | solution.py:595
  22.2 1.5 %collective-permute-start.2 = (f32[8,264]{1,0:T(8,128)S(1)}, f32[8,264]{1,0:T(8,128)S(1)}, u32[]{:S(2)}, u32[]{:S(2)}) collective-permute-start(f32[8,264]{1,0:T(8,128)S(1)} %get-tuple-element.34), channel_id=1, source_target_pairs={{0,2},{1,3},{2,0},{3,1},{4,6},{5,7},{6,4},{7,5},{8,10},{9,11},{10,... | collective-permute-start | bytes 25352 | tf_op jit(solution)/shard_map/ppermute | solution.py:489
  23.6 0.3 collective-permute-start.1
  24.0 1.1 %value.5 = (f32[3,256,2048]{2,1,0:T(8,128)S(1)}, f32[16,8,2048]{2,1,0:T(8,128)S(1)}) custom-call(bf16[256,2048]{1,0:T(8,128)(2,1)S(1)} %get-tuple-element.33.mixed, f32[8,2048]{1,0:T(8,128)S(1)} %get-tuple-element.35.mixed_rim, f32[1,2048]{1,0:T(1,128)S(1)} %bitcast.39, f32[256,2048]{1,0:T(8,128)S(1)} %get-tuple-element.36.key_feat, ...), custom_call_target="tpu_custom_call" | custom-call | flops 524288000 | bytes 5242880 | tf_op jit(solution)/shard_map/value/pallas_call | solution.py:613
  25.1 0.2 collective-permute-done.3
  25.3 0.5 %collective-permute-done.2 = f32[8,264]{1,0:T(8,128)S(1)} collective-permute-done((f32[8,264]{1,0:T(8,128)S(1)}, f32[8,264]{1,0:T(8,128)S(1)}, u32[]{:S(2)}, u32[]{:S(2)}) %collective-permute-start.2) | collective-permute-done | bytes 8480 | tf_op jit(solution)/shard_map/ppermute | solution.py:489
  25.9 3.5 %state.1 = (bf16[256,2048]{1,0:T(8,128)(2,1)S(1)}, f32[16,2048]{1,0:T(8,128)S(1)}) custom-call(f32[8,264]{1,0:T(8,128)S(1)} %add_add_fusion.refs_0_, f32[3,256,2048]{2,1,0:T(8,128)S(1)} %get-tuple-element.37.refs_1_, f32[16,8,2048]{2,1,0:T(8,128)S(1)} %get-tuple-element.38.refs_2_, f32[16,8,2048]{2,1,0:T(8,128)S(1)} %get-tuple-element.39.refs_3_.decays), custom_call_target="tpu_custom_call" | custom-call | flops 52428800 | bytes 5242880 | tf_op jit(solution)/shard_map/state/pallas_call | solution.py:621
  29.4 3.6 %collective-permute-start.6 = (bf16[16,2048]{1,0:T(8,128)(2,1)S(1)}, bf16[16,2048]{1,0:T(8,128)(2,1)S(1)}, u32[]{:S(2)}, u32[]{:S(2)}) collective-permute-start(bf16[16,2048]{1,0:T(8,128)(2,1)S(1)} %convert_element_type.18), channel_id=1, source_target_pairs={{0,12},{4,8},{8,4},{12,0},{16,28},{20,24},{24,20},{28,16},{1,13},{... | collective-permute-start | bytes 196616 | tf_op jit(solution)/shard_map/ppermute | solution.py:489
  32.9 0.4 collective-permute-start.5
  33.4 1.0 %collective-permute-start.4 = (bf16[16,2048]{1,0:T(8,128)(2,1)S(1)}, bf16[16,2048]{1,0:T(8,128)(2,1)S(1)}, u32[]{:S(2)}, u32[]{:S(2)}) collective-permute-start(bf16[16,2048]{1,0:T(8,128)(2,1)S(1)} %convert_element_type.18), channel_id=1, source_target_pairs={{0,4},{4,0},{8,12},{12,8},{16,20},{20,16},{24,28},{28,24},{1,5},{5... | collective-permute-start | bytes 196616 | tf_op jit(solution)/shard_map/ppermute | solution.py:489
  34.4 2.3 %local.1 = (f32[256,2048]{1,0:T(8,128)S(1)}, f32[1,2048]{1,0:T(1,128)S(1)}) custom-call(bf16[256,2048]{1,0:T(8,128)(2,1)S(1)} %get-tuple-element.41.product, f32[2,256,2048]{2,1,0:T(8,128)S(1)} %get-tuple-element.42.long_hat, f32[1,2048]{1,0:T(1,128)S(1)} %bitcast.40, bf16[256,256]{1,0:T(8,128)(2,1)S(1)} %copy-done.5, bf16[256,256]{1,0:T(8,128)(2,1)S(1)} %copy-done.9), custom_call_target="tpu_custom_call" | custom-call | flops 1048576000 | bytes 7340032 | tf_op jit(solution)/shard_map/local/pallas_call | solution.py:628
  36.7 0.5 %collective-permute-done.5 = bf16[16,2048]{1,0:T(8,128)(2,1)S(1)} collective-permute-done((bf16[16,2048]{1,0:T(8,128)(2,1)S(1)}, bf16[16,2048]{1,0:T(8,128)(2,1)S(1)}, u32[]{:S(2)}, u32[]{:S(2)}) %collective-permute-start.5) | collective-permute-done | bytes 65568 | tf_op jit(solution)/shard_map/ppermute | solution.py:489
  37.2 0.4 collective-permute-done.4
  37.7 3.0 %collective-permute-start.7 = (bf16[16,2048]{1,0:T(8,128)(2,1)S(1)}, bf16[16,2048]{1,0:T(8,128)(2,1)S(1)}, u32[]{:S(2)}, u32[]{:S(2)}) collective-permute-start(bf16[16,2048]{1,0:T(8,128)(2,1)S(1)} %get-tuple-element.48._), channel_id=1, source_target_pairs={{0,16},{4,20},{8,24},{12,28},{16,0},{20,4},{24,8},{28,12},{1,17},{... | collective-permute-start | bytes 196616 | tf_op jit(solution)/shard_map/ppermute | solution.py:489
  40.7 1.7 %gate.5 = (f32[256,2048]{1,0:T(8,128)S(1)}, bf16[256,2048]{1,0:T(8,128)(2,1)}) custom-call(bf16[256,2048]{1,0:T(8,128)(2,1)S(1)} %copy-done, f32[8,2048]{1,0:T(8,128)S(1)} %get-tuple-element.32.rim_long, f32[3,3,2048]{2,1,0:T(4,128)S(1)} %copy-done.8, bf16[256,2048]{1,0:T(8,128)(2,1)S(1)} %get-tuple-element.33.mixed, bf16[16,2048]{1,0:T(8,128)(2,1)S(1)} %get-tuple-element.48._), custom_call_target="tpu_custom_call" | custom-call | flops 524288000 | bytes 7340032 | tf_op jit(solution)/shard_map/gate/pallas_call | solution.py:633
  42.4 1.3 %collective-permute-done.7 = bf16[16,2048]{1,0:T(8,128)(2,1)S(1)} collective-permute-done((bf16[16,2048]{1,0:T(8,128)(2,1)S(1)}, bf16[16,2048]{1,0:T(8,128)(2,1)S(1)}, u32[]{:S(2)}, u32[]{:S(2)}) %collective-permute-start.7) | collective-permute-done | bytes 65568 | tf_op jit(solution)/shard_map/ppermute | solution.py:489
  43.7 0.1 fusion.8.state
  43.8 3.1 %finish.1 = bf16[256,2048]{1,0:T(8,128)(2,1)} custom-call(f32[16,2048]{1,0:T(8,128)S(1)} %fusion.8.state, f32[16,8,2048]{2,1,0:T(8,128)S(1)} %get-tuple-element.39.refs_3_.decays, f32[16,8,2048]{2,1,0:T(8,128)S(1)} %get-tuple-element.45.leads, f32[256,2048]{1,0:T(8,128)S(1)} %get-tuple-element.46.local, f32[256,2048]{1,0:T(8,128)S(1)} %get-tuple-element.47.gate_feat), custom_call_target="tpu_custom_call" | custom-call | flops 52428800 | bytes 4194304 | tf_op jit(solution)/shard_map/finish/pallas_call | solution.py:637
  (40 shorter events, 0.3 us)
Async XLA Ops:
  0.6 7.5 %copy-start.11 = (bf16[256,384]{1,0:T(8,128)(2,1)S(1)}, bf16[256,384]{1,0:T(8,128)(2,1)}, u32[]{:S(2)}) copy-start(bf16[256,384]{1,0:T(8,128)(2,1)} %constant.17.clone.refs_3_.split_rows) | copy-start | bytes 589828
  0.6 7.3 %copy-start.10 = (f32[16,2048]{1,0:T(8,128)S(1)}, f32[16,2048]{1,0:T(8,128)}, u32[]{:S(2)}) copy-start(f32[16,2048]{1,0:T(8,128)} %rates.1) | copy-start | bytes 393220
  0.7 7.3 %copy-start.16 = (f32[16,2048]{1,0:T(8,128)S(1)}, f32[16,2048]{1,0:T(8,128)}, u32[]{:S(2)}) copy-start(f32[16,2048]{1,0:T(8,128)} %param.28) | copy-start | bytes 393220
  0.7 11.6 %copy-start.5 = (bf16[256,256]{1,0:T(8,128)(2,1)S(1)}, bf16[256,256]{1,0:T(8,128)(2,1)}, u32[]{:S(2)}) copy-start(bf16[256,256]{1,0:T(8,128)(2,1)} %constant.16.clone.exact_rows) | copy-start | bytes 393220
  0.7 11.6 %copy-start.6 = (f32[128,2048]{1,0:T(8,128)S(1)}, f32[128,2048]{1,0:T(8,128)}, u32[]{:S(2)}) copy-start(f32[128,2048]{1,0:T(8,128)} %taps.1) | copy-start | bytes 3145732
  0.7 11.6 %copy-start.7 = (f32[3,3,2048]{2,1,0:T(4,128)S(1)}, f32[3,3,2048]{2,1,0:T(4,128)}, u32[]{:S(2)}) copy-start(f32[3,3,2048]{2,1,0:T(4,128)} %short.7) | copy-start | bytes 221188
  0.7 11.6 %copy-start.8 = (f32[3,3,2048]{2,1,0:T(4,128)S(1)}, f32[3,3,2048]{2,1,0:T(4,128)}, u32[]{:S(2)}) copy-start(f32[3,3,2048]{2,1,0:T(4,128)} %short.9) | copy-start | bytes 221188
  0.7 11.6 %copy-start.9 = (bf16[256,256]{1,0:T(8,128)(2,1)S(1)}, bf16[256,256]{1,0:T(8,128)(2,1)}, u32[]{:S(2)}) copy-start(bf16[256,256]{1,0:T(8,128)(2,1)} %constant.18.clone.backward) | copy-start | bytes 393220
  3.0 17.4 %collective-permute-start = (bf16[144,2048]{1,0:T(8,128)(2,1)S(1)}, bf16[144,2048]{1,0:T(8,128)(2,1)S(1)}, u32[]{:S(2)}, u32[]{:S(2)}) collective-permute-start(bf16[144,2048]{1,0:T(8,128)(2,1)S(1)} %pack.1), channel_id=1, source_target_pairs={{0,4},{4,8},{8,12},{12,16},{16,20},{20,24},{24,28},{1,5},{5,9},{9,... | collective-permute-start | bytes 1769480 | tf_op jit(solution)/shard_map/ppermute | solution.py:484
  8.0 4.4 %copy-start.1 = (bf16[256,2048]{1,0:T(8,128)(2,1)S(1)}, bf16[256,2048]{1,0:T(8,128)(2,1)}, u32[]{:S(2)}) copy-start(bf16[256,2048]{1,0:T(8,128)(2,1)} %key.3) | copy-start | bytes 3145732
  8.0 4.4 %copy-start.2 = (bf16[256,2048]{1,0:T(8,128)(2,1)S(1)}, bf16[256,2048]{1,0:T(8,128)(2,1)}, u32[]{:S(2)}) copy-start(bf16[256,2048]{1,0:T(8,128)(2,1)} %value.4) | copy-start | bytes 3145732
  8.0 4.4 %copy-start.3 = (bf16[256,2048]{1,0:T(8,128)(2,1)S(1)}, bf16[256,2048]{1,0:T(8,128)(2,1)}, u32[]{:S(2)}) copy-start(bf16[256,2048]{1,0:T(8,128)(2,1)} %gate.4) | copy-start | bytes 3145732
  8.0 4.4 %copy-start.4 = (bf16[256,2048]{1,0:T(8,128)(2,1)S(1)}, bf16[256,2048]{1,0:T(8,128)(2,1)}, u32[]{:S(2)}) copy-start(bf16[256,2048]{1,0:T(8,128)(2,1)} %key_long.3) | copy-start | bytes 3145732
  8.0 4.4 %copy-start.13 = (f32[2048]{0:T(1024)S(1)}, f32[2048]{0:T(1024)}, u32[]{:S(2)}) copy-start(f32[2048]{0:T(1024)} %param.22) | copy-start | bytes 24580
  12.4 8.1 %copy-start.12 = (bf16[320,256]{1,0:T(8,128)(2,1)S(1)}, bf16[320,256]{1,0:T(8,128)(2,1)}, u32[]{:S(2)}) copy-start(bf16[320,256]{1,0:T(8,128)(2,1)} %constant.19.clone.backward) | copy-start | bytes 491524
  22.1 3.2 %collective-permute-start.3 = (f32[8,264]{1,0:T(8,128)S(1)}, f32[8,264]{1,0:T(8,128)S(1)}, u32[]{:S(2)}, u32[]{:S(2)}) collective-permute-start(f32[8,264]{1,0:T(8,128)S(1)} %get-tuple-element.34), channel_id=1, source_target_pairs={{0,3},{1,2},{2,1},{3,0},{4,7},{5,6},{6,5},{7,4},{8,11},{9,10},{10,... | collective-permute-start | bytes 25352 | tf_op jit(solution)/shard_map/ppermute | solution.py:489
  22.2 3.7 %collective-permute-start.2 = (f32[8,264]{1,0:T(8,128)S(1)}, f32[8,264]{1,0:T(8,128)S(1)}, u32[]{:S(2)}, u32[]{:S(2)}) collective-permute-start(f32[8,264]{1,0:T(8,128)S(1)} %get-tuple-element.34), channel_id=1, source_target_pairs={{0,2},{1,3},{2,0},{3,1},{4,6},{5,7},{6,4},{7,5},{8,10},{9,11},{10,... | collective-permute-start | bytes 25352 | tf_op jit(solution)/shard_map/ppermute | solution.py:489
  23.6 2.2 %collective-permute-start.1 = (f32[8,264]{1,0:T(8,128)S(1)}, f32[8,264]{1,0:T(8,128)S(1)}, u32[]{:S(2)}, u32[]{:S(2)}) collective-permute-start(f32[8,264]{1,0:T(8,128)S(1)} %get-tuple-element.34), channel_id=1, source_target_pairs={{0,1},{1,0},{2,3},{3,2},{4,5},{5,4},{6,7},{7,6},{8,9},{9,8},{10,11... | collective-permute-start | bytes 25352 | tf_op jit(solution)/shard_map/ppermute | solution.py:489
  25.9 8.5 %copy-start.15 = (f32[2048]{0:T(1024)S(1)}, f32[2048]{0:T(1024)}, u32[]{:S(2)}) copy-start(f32[2048]{0:T(1024)} %param.29) | copy-start | bytes 24580
  29.4 7.3 %collective-permute-start.6 = (bf16[16,2048]{1,0:T(8,128)(2,1)S(1)}, bf16[16,2048]{1,0:T(8,128)(2,1)S(1)}, u32[]{:S(2)}, u32[]{:S(2)}) collective-permute-start(bf16[16,2048]{1,0:T(8,128)(2,1)S(1)} %convert_element_type.18), channel_id=1, source_target_pairs={{0,12},{4,8},{8,4},{12,0},{16,28},{20,24},{24,20},{28,16},{1,13},{... | collective-permute-start | bytes 196616 | tf_op jit(solution)/shard_map/ppermute | solution.py:489
  32.9 4.3 %collective-permute-start.5 = (bf16[16,2048]{1,0:T(8,128)(2,1)S(1)}, bf16[16,2048]{1,0:T(8,128)(2,1)S(1)}, u32[]{:S(2)}, u32[]{:S(2)}) collective-permute-start(bf16[16,2048]{1,0:T(8,128)(2,1)S(1)} %convert_element_type.18), channel_id=1, source_target_pairs={{0,8},{4,12},{8,0},{12,4},{16,24},{20,28},{24,16},{28,20},{1,9},{5... | collective-permute-start | bytes 196616 | tf_op jit(solution)/shard_map/ppermute | solution.py:489
  33.4 4.3 %collective-permute-start.4 = (bf16[16,2048]{1,0:T(8,128)(2,1)S(1)}, bf16[16,2048]{1,0:T(8,128)(2,1)S(1)}, u32[]{:S(2)}, u32[]{:S(2)}) collective-permute-start(bf16[16,2048]{1,0:T(8,128)(2,1)S(1)} %convert_element_type.18), channel_id=1, source_target_pairs={{0,4},{4,0},{8,12},{12,8},{16,20},{20,16},{24,28},{28,24},{1,5},{5... | collective-permute-start | bytes 196616 | tf_op jit(solution)/shard_map/ppermute | solution.py:489
  34.4 6.4 %copy-start = (bf16[256,2048]{1,0:T(8,128)(2,1)S(1)}, bf16[256,2048]{1,0:T(8,128)(2,1)}, u32[]{:S(2)}) copy-start(bf16[256,2048]{1,0:T(8,128)(2,1)} %gate_long.3) | copy-start | bytes 3145732
  37.7 6.0 %collective-permute-start.7 = (bf16[16,2048]{1,0:T(8,128)(2,1)S(1)}, bf16[16,2048]{1,0:T(8,128)(2,1)S(1)}, u32[]{:S(2)}, u32[]{:S(2)}) collective-permute-start(bf16[16,2048]{1,0:T(8,128)(2,1)S(1)} %get-tuple-element.48._), channel_id=1, source_target_pairs={{0,16},{4,20},{8,24},{12,28},{16,0},{20,4},{24,8},{28,12},{1,17},{... | collective-permute-start | bytes 196616 | tf_op jit(solution)/shard_map/ppermute | solution.py:489
  (1 other events, 3.5 us)

commit v2 on v1

--- a/solution.py
+++ b/solution.py
@@ -101,7 +101,12 @@
     return lax.broadcasted_iota(jnp.int32, shape, 0)
 
 
-def over_channels(width, step):
+def over_channels(width, step, unrolled=False):
+    if unrolled:
+        for i in range(width // WIDTH):
+            step(pl.ds(i * WIDTH, WIDTH), i * WIDTH)
+        return
+
     def one(i, _):
         step(pl.ds(pl.multiple_of(i * WIDTH, WIDTH), WIDTH), i * WIDTH)
         return 0
@@ -185,12 +190,13 @@
 
 
 def lane_tiles(base):
-    return [
-        pl.ds(pl.multiple_of(base + tile * LANES, LANES), LANES) for tile in range(WIDTH // LANES)
-    ]
-
-
-def impulse_kernel(count, place, rates, weights, split_rows, long_hat, carry, leads, decays, impulse):
+    starts = [base + tile * LANES for tile in range(WIDTH // LANES)]
+    if isinstance(base, int):
+        return [pl.ds(start, LANES) for start in starts]
+    return [pl.ds(pl.multiple_of(start, LANES), LANES) for start in starts]
+
+
+def impulse_kernel(count, place, rates, weights, exact_rows, long_hat, carry, leads, decays, impulse):
     modes, width = rates.shape
     rows = impulse.shape[0]
     for i, weight in enumerate(carry_weights(place[0], count, rows, rates[...])):
@@ -212,8 +218,8 @@
 
             response(starts, steps, rows // TILE, emit)
         for block in range(rows // BLOCK):
-            long_hat[block, :, here] = forward_split(
-                split_rows[...], impulse[block * BLOCK : (block + 1) * BLOCK]
+            long_hat[block, :, here] = forward_exact(
+                exact_rows[...], impulse[block * BLOCK : (block + 1) * BLOCK].astype(BF16)
             )
         for block in reversed(range(1, rows // BLOCK)):
             long_hat[block, :, here] = long_hat[block, :, here] + turned(
@@ -312,7 +318,7 @@
         mixed_rim[:, here] = kept[:TILE]
         total[...] = total[...] + lane_parts(kept * kept)
 
-    over_channels(width, step)
+    over_channels(width, step, unrolled=True)
     squares[...] = lax.dot_general(
         jnp.ones((TILE, LANES), F32),
         jnp.concatenate([total[...], squares_late[...]], 0),
@@ -343,7 +349,7 @@
             for mode in range(modes):
                 tails[mode, :, lanes] = mode_tables(rates, mode, lanes, TILE - 1.0, -1.0)[0]
 
-    over_channels(width, step)
+    over_channels(width, step, unrolled=True)
 
 
 def state_kernel(all_width, squares, parts, tails, decays, product_out, state, factors):
@@ -386,7 +392,7 @@
             for mode in range(modes):
                 state[mode : mode + 1, lanes] = sublane_sum(held[mode] * tails[mode, :, lanes])
 
-    over_channels(width, step)
+    over_channels(width, step, unrolled=True)
 
 
 def local_kernel(product, long_hat, skip, exact_rows, backward, out, done):
@@ -406,45 +412,68 @@
                 F32
             )
 
-    over_channels(width, step)
-
-
-def gate_kernel(gate_long, rim_long, short, mixed, _, gate_feat, mixed_out):
-    width = gate_long.shape[1]
+    over_channels(width, step, unrolled=True)
+
+
+def modal_tables(state, decays, leads, lanes):
+    modes = decays.shape[0]
+    starts = [leads[mode, :, lanes] * state[mode : mode + 1, lanes] for mode in range(modes)]
+    return starts, [decays[mode, :, lanes] for mode in range(modes)]
+
+
+def near_kernel(
+    state, decays, leads, local, gate_long, rim_long, short, mixed, _,
+    out, gate_feat, mixed_out, sent,
+):
+    rows, width = local.shape
+    copy = pltpu.make_async_copy(mixed, mixed_out, sent)
+    copy.start()
 
     def step(here, base):
         gates = jnp.concatenate(
             [pltpu.roll(rim_long[:, here], 6, 0), gate_long[:, here].astype(F32)], 0
         )
         gate_feat[:, here] = shifted_filter(gates, short[0, :, here])[TILE:]
-        mixed_out[:, here] = mixed[:, here]
-
-    over_channels(width, step)
-
-
-def finish_kernel(state, decays, leads, local, gate_feat, out, held_out, sent):
-    rows, width = local.shape
-    modes = decays.shape[0]
+        for lanes in lane_tiles(base):
+
+            def emit(i, total):
+                part = slice(i * TILE, (i + 1) * TILE)
+                out[part, lanes] = gate_feat[part, lanes] * (local[part, lanes] + total)
+
+            response(*modal_tables(state, decays, leads, lanes), rows // TILE, emit)
+
+    over_channels(width, step, unrolled=True)
+    copy.wait()
+
+
+def finish_kernel(count, place, state, decays, leads, near, gate_feat, out, held_out, sent):
+    rows, width = near.shape
+    group, radix = list(stages(count))[-1] if count > 1 else (1, 1)
+    later = (place[0] // group) % radix > 0
     copies = []
     for chunk in range(width // PART):
-        for tile in range(PART // LANES):
-            lanes = slice(chunk * PART + tile * LANES, chunk * PART + (tile + 1) * LANES)
-            starts = [
-                leads[mode, :, lanes] * state[mode : mode + 1, lanes] for mode in range(modes)
-            ]
-            steps = [decays[mode, :, lanes] for mode in range(modes)]
-            held = []
-
-            def emit(i, total):
-                part = slice(i * TILE, (i + 1) * TILE)
-                held.append(gate_feat[part, lanes] * (local[part, lanes] + total))
-                if i % 2 == 1:
-                    held_out[(i - 1) * TILE : (i + 1) * TILE, lanes] = jnp.concatenate(
-                        held[-2:], 0
-                    ).astype(BF16)
-
-            response(starts, steps, rows // TILE, emit)
         here = pl.ds(chunk * PART, PART)
+
+        @pl.when(later)
+        def _():
+            for tile in range(PART // LANES):
+                lanes = slice(chunk * PART + tile * LANES, chunk * PART + (tile + 1) * LANES)
+                held = []
+
+                def emit(i, total):
+                    part = slice(i * TILE, (i + 1) * TILE)
+                    held.append(near[part, lanes] + gate_feat[part, lanes] * total)
+                    if i % 2 == 1:
+                        held_out[(i - 1) * TILE : (i + 1) * TILE, lanes] = jnp.concatenate(
+                            held[-2:], 0
+                        ).astype(BF16)
+
+                response(*modal_tables(state, decays, leads, lanes), rows // TILE, emit)
+
+        @pl.when(jnp.logical_not(later))
+        def _():
+            held_out[:, here] = near[:, here].astype(BF16)
+
         copy = pltpu.make_async_copy(held_out.at[:, here], out.at[:, here], sent.at[chunk])
         copy.start()
         copies.append(copy)
@@ -512,21 +541,21 @@
 
 def carried_state(state, weights, beside):
     count = lax.axis_size("ctx")
-    incoming = jnp.zeros_like(state)
-    sent = incoming
+    known = incoming = jnp.zeros_like(state)
+    sent = state
     at = 0
     for group, radix in stages(count):
+        known = known + incoming
         if group > 1 and group * radix == count:
             state = state + beside
         sent = state.astype(BF16)
         got = [state]
         for turn in range(1, radix):
             got.append(exchanged(sent, "ctx", turn * group).astype(F32))
-        for turn in range(radix):
-            incoming = incoming + weights[at + 2 * turn] * got[turn]
+        incoming = sum(weights[at + 2 * turn] * got[turn] for turn in range(radix))
         state = sum(weights[at + 2 * turn + 1] * got[turn] for turn in range(radix))
         at += 2 * radix
-    return incoming, sent
+    return known, incoming, sent
 
 
 def body(
@@ -555,6 +584,7 @@
         in_hbm(value)
         for value in (key_medium, value_medium, gate_medium, gate_long, key_long, short_medium)
     ]
+    place = lax.axis_index("ctx").astype(jnp.int32).reshape(1)
     pack = call(
         pack_kernel, "pack", [FAR] * 6, arr((EARLY, width), BF16),
         [
@@ -566,7 +596,6 @@
 
     skip_row = skip_medium[None]
     mode_weight = residues * jnp.sqrt(-jnp.expm1(-2.0 * decay_rates))
-    place = lax.axis_index("ctx").astype(jnp.int32).reshape(1)
     turns = sum(2 * radix for _, radix in stages(count)) or 1
     long_hat, carry, leads, decays = call(
         lambda *refs: impulse_kernel(count, *refs), "impulse",
@@ -577,7 +606,7 @@
         ],
         [pltpu.VMEM((rows, WIDTH), F32)],
         flops=2000 * rows * width, moved=10 * rows * width,
-    )(place, decay_rates, mode_weight, split_rows)
+    )(place, decay_rates, mode_weight, exact_rows)
 
     conv_early, gate_early, mixed_late, squares_late, key_feat, taps_hat, heads = call(
         own_kernel, "own", [KEPT] * 12,
@@ -629,16 +658,19 @@
         local_kernel, "local", [KEPT] * 5, [arr((rows, width), F32), arr((1, width), F32)],
         flops=2000 * rows * width, moved=14 * rows * width,
     )(product_long, long_hat, skip_long[None], exact_rows, backward)
-    incoming, last_sent = carried_state(state, carry, done)
-    gate_feat, mixed_out = call(
-        gate_kernel, "gate", [KEPT] * 5, [arr((rows, width), F32), arr((rows, width), BF16)],
+    known, incoming, last_sent = carried_state(state, carry, done)
+    near, gate_feat, mixed_out = call(
+        near_kernel, "near", [KEPT] * 9,
+        [arr((rows, width), F32), arr((rows, width), F32), arr((rows, width), BF16)],
+        [pltpu.SemaphoreType.DMA], out_specs=[KEPT, KEPT, FAR],
         flops=1000 * rows * width, moved=14 * rows * width,
-    )(gate_long, rim_long, short_long, mixed_medium, last_sent)
+    )(known, decays, leads, local, gate_long, rim_long, short_long, mixed_medium, last_sent)
     mixed_long = call(
-        finish_kernel, "finish", [KEPT] * 5, arr((rows, width), BF16),
+        lambda *refs: finish_kernel(count, *refs), "finish", [SCALAR] + [KEPT] * 5,
+        arr((rows, width), BF16),
         [pltpu.VMEM((rows, width), BF16), pltpu.SemaphoreType.DMA((width // PART,))], out_specs=FAR,
         flops=100 * rows * width, moved=8 * rows * width,
-    )(incoming, decays, leads, local, gate_feat)
+    )(place, incoming, decays, leads, near, gate_feat)
     return (mixed_out, mixed_long)
 
 

time: 47.2 us -> 45.8 us (0.970)
  Pallas kernels: 25.7 us -> 24.6 us
  waiting for transfers between devices: 5.09 us -> 4.32 us
    ppermute x7, waiting for transfers between devices: 3.01 us -> 1.88 us  [exchanged(): lax.ppermute(value, axis, [(source, source ^ flip) for source in range(co...]
    pallas_call x1, Pallas kernels: 4.16 us -> 3.62 us  [body(): call(lambda *refs: impulse_kernel(count, *refs), 'impulse', [SCALAR] + [K...]
  transfers between devices with their start and end apart: 8 -> 8, of which waited for: 6 -> 5; matrix products, arithmetic and copies ran while one was open for 0% -> 0% of each run, Pallas kernels for 32% -> 37%
where the time goes in v2:
time: 45.8 us; the launch traced here: 45.3 us
  Pallas kernels  24.6 us (54%)
  starting transfers between devices  14.8 us (32%)
  waiting for transfers between devices  4.32 us (9%)
  between operations  1.14 us (2%)
    ppermute x7, starting transfers between devices, exchanged(): lax.ppermute(value, axis, [(source, source ^ flip) for source in range(co...  9.94 us
    pallas_call x1, Pallas kernels, body(): call(own_kernel, 'own', [KEPT] * 12, [arr((EARLY, width), F32), arr((EARL...  6.15 us
    ppermute x1, starting transfers between devices, passed_along(): lax.ppermute(value, axis, [(source, source + steps) for source in range(c...  4.91 us
    pallas_call x1, Pallas kernels, body(): call(lambda *refs: impulse_kernel(count, *refs), 'impulse', [SCALAR] + [K...  3.62 us
    pallas_call x1, Pallas kernels, body(): call(near_kernel, 'near', [KEPT] * 9, [arr((rows, width), F32), arr((rows...  3.62 us
    pallas_call x1, Pallas kernels, body(): call(lambda *refs: state_kernel(all_width, *refs), 'state', [KEPT] * 4, [...  3.18 us
    ppermute x1, waiting for transfers between devices, passed_along(): lax.ppermute(value, axis, [(source, source + steps) for source in range(c...  2.44 us
    pallas_call x1, Pallas kernels, body(): call(pack_kernel, 'pack', [FAR] * 6, arr((EARLY, width), BF16), [pltpu.VM...  2.29 us
  transfers between devices with their start and end apart: 8, of which 5 were waited for; matrix products, arithmetic and copies ran while one was open for 0% of the time, Pallas kernels for 37%

profile of v2, /device:TPU:0, one launch (start us, length us, event | category | flops | bytes accessed | tf_op | source)
XLA Modules:
  0.0 45.3 jit_solution(5309172298804056040)
XLA Ops:
  0.7 2.3 %pack.1 = bf16[144,2048]{1,0:T(8,128)(2,1)S(1)} custom-call(bf16[256,2048]{1,0:T(8,128)(2,1)} %key.3, bf16[256,2048]{1,0:T(8,128)(2,1)} %value.4, bf16[256,2048]{1,0:T(8,128)(2,1)} %gate.3, bf16[256,2048]{1,0:T(8,128)(2,1)} %gate_long.3, bf16[256,2048]{1,0:T(8,128)(2,1)} %key_long.3, f32[3,3,2048]{2,1,0:T(4,128)} %short.7), custom_call_target="tpu_custom_call" | custom-call | tf_op jit(solution)/shard_map/pack/pallas_call | solution.py:588
  3.0 4.9 %collective-permute-start = (bf16[144,2048]{1,0:T(8,128)(2,1)S(1)}, bf16[144,2048]{1,0:T(8,128)(2,1)S(1)}, u32[]{:S(2)}, u32[]{:S(2)}) collective-permute-start(bf16[144,2048]{1,0:T(8,128)(2,1)S(1)} %pack.1), channel_id=1, source_target_pairs={{0,4},{4,8},{8,12},{12,16},{16,20},{20,24},{24,28},{1,5},{5,9},{9,... | collective-permute-start | bytes 1769480 | tf_op jit(solution)/shard_map/ppermute | solution.py:513
  8.0 0.1 sqrt_multiply_fusion.refs_2_
  8.1 3.6 %impulse.1 = (f32[2,256,2048]{2,1,0:T(8,128)S(1)}, f32[12,16,2048]{2,1,0:T(8,128)S(1)}, f32[16,8,2048]{2,1,0:T(8,128)S(1)}, f32[16,8,2048]{2,1,0:T(8,128)S(1)}) custom-call(s32[1]{0:T(128)} %bitcast.refs_0_, f32[16,2048]{1,0:T(8,128)S(1)} %copy-done.10, f32[16,2048]{1,0:T(8,128)S(1)} %sqrt_multiply_fusion.refs_2_, bf16[256,256]{1,0:T(8,128)(2,1)S(1)} %copy-done.5), custom_call_target="tpu_custom_call" | custom-call | flops 1048576000 | bytes 5242880 | tf_op jit(solution)/shard_map/impulse/pallas_call | solution.py:600
  11.9 6.1 %own.1 = (f32[144,2048]{1,0:T(8,128)S(1)}, f32[144,2048]{1,0:T(8,128)S(1)}, bf16[112,2048]{1,0:T(8,128)(2,1)S(1)}, f32[112,128]{1,0:T(8,128)S(1)}, f32[256,2048]...) custom-call(bf16[256,2048]{1,0:T(8,128)(2,1)S(1)} %copy-done.3, bf16[256,2048]{1,0:T(8,128)(2,1)S(1)} %copy-done.1, ...), custom_call_target="tpu_custom_call" | custom-call | flops 1048576000 | bytes 5242880 | tf_op jit(solution)/shard_map/own/pallas_call | solution.py:611
  18.0 2.4 %collective-permute-done.halo = bf16[144,2048]{1,0:T(8,128)(2,1)S(1)} collective-permute-done((bf16[144,2048]{1,0:T(8,128)(2,1)S(1)}, bf16[144,2048]{1,0:T(8,128)(2,1)S(1)}, u32[]{:S(2)}, u32[]{:S(2)}) %collective-permute-start) | collective-permute-done | bytes 589856 | tf_op jit(solution)/shard_map/ppermute | solution.py:513
  20.5 1.4 %medium.1 = (bf16[256,2048]{1,0:T(8,128)(2,1)S(1)}, f32[8,2048]{1,0:T(8,128)S(1)}, f32[8,264]{1,0:T(8,128)S(1)}, f32[8,2048]{1,0:T(8,128)S(1)}) custom-call(bf16[144,2048]{1,0:T(8,128)(2,1)S(1)} %collective-permute-done.halo, f32[40,2048]{1,0:T(8,128)S(1)} %get-tuple-element.27.heads, f32[3,3,2048]{2,1,0:T(4,128)S(1)} %copy-done.7, f32[1,2048]{1,0:T(1,128)S(1)} %bitcast.38, ...), custom_call_target="tpu_custom_call" | custom-call | flops 524288000 | bytes 5242880 | tf_op jit(solution)/shard_map/medium/pallas_call | solution.py:624
  21.9 0.1 collective-permute-start.3
  22.0 1.5 %collective-permute-start.2 = (f32[8,264]{1,0:T(8,128)S(1)}, f32[8,264]{1,0:T(8,128)S(1)}, u32[]{:S(2)}, u32[]{:S(2)}) collective-permute-start(f32[8,264]{1,0:T(8,128)S(1)} %get-tuple-element.33), channel_id=1, source_target_pairs={{0,2},{1,3},{2,0},{3,1},{4,6},{5,7},{6,4},{7,5},{8,10},{9,11},{10,... | collective-permute-start | bytes 25352 | tf_op jit(solution)/shard_map/ppermute | solution.py:518
  23.5 0.3 collective-permute-start.1
  23.8 1.0 %value.5 = (f32[3,256,2048]{2,1,0:T(8,128)S(1)}, f32[16,8,2048]{2,1,0:T(8,128)S(1)}) custom-call(bf16[256,2048]{1,0:T(8,128)(2,1)S(1)} %get-tuple-element.34.mixed, f32[8,2048]{1,0:T(8,128)S(1)} %get-tuple-element.35.mixed_rim, f32[1,2048]{1,0:T(1,128)S(1)} %bitcast.39, f32[256,2048]{1,0:T(8,128)S(1)} %get-tuple-element.36.key_feat, ...), custom_call_target="tpu_custom_call" | custom-call | flops 524288000 | bytes 5242880 | tf_op jit(solution)/shard_map/value/pallas_call | solution.py:642
  24.9 0.3 collective-permute-done.3
  25.2 0.5 %collective-permute-done.2 = f32[8,264]{1,0:T(8,128)S(1)} collective-permute-done((f32[8,264]{1,0:T(8,128)S(1)}, f32[8,264]{1,0:T(8,128)S(1)}, u32[]{:S(2)}, u32[]{:S(2)}) %collective-permute-start.2) | collective-permute-done | bytes 8480 | tf_op jit(solution)/shard_map/ppermute | solution.py:518
  25.8 3.2 %state.1 = (bf16[256,2048]{1,0:T(8,128)(2,1)S(1)}, f32[16,2048]{1,0:T(8,128)S(1)}) custom-call(f32[8,264]{1,0:T(8,128)S(1)} %add_add_fusion.refs_0_, f32[3,256,2048]{2,1,0:T(8,128)S(1)} %get-tuple-element.38.refs_1_, f32[16,8,2048]{2,1,0:T(8,128)S(1)} %get-tuple-element.39.refs_2_, f32[16,8,2048]{2,1,0:T(8,128)S(1)} %get-tuple-element.40.refs_3_.decays.refs_2_), custom_call_target="tpu_custom_call" | custom-call | flops 52428800 | bytes 5242880 | tf_op jit(solution)/shard_map/state/pallas_call | solution.py:650
  29.0 3.6 %collective-permute-start.6 = (bf16[16,2048]{1,0:T(8,128)(2,1)S(1)}, bf16[16,2048]{1,0:T(8,128)(2,1)S(1)}, u32[]{:S(2)}, u32[]{:S(2)}) collective-permute-start(bf16[16,2048]{1,0:T(8,128)(2,1)S(1)} %convert_element_type.18), channel_id=1, source_target_pairs={{0,12},{4,8},{8,4},{12,0},{16,28},{20,24},{24,20},{28,16},{1,13},{... | collective-permute-start | bytes 196616 | tf_op jit(solution)/shard_map/ppermute | solution.py:518
  32.5 0.4 collective-permute-start.5
  33.0 1.0 %collective-permute-start.4 = (bf16[16,2048]{1,0:T(8,128)(2,1)S(1)}, bf16[16,2048]{1,0:T(8,128)(2,1)S(1)}, u32[]{:S(2)}, u32[]{:S(2)}) collective-permute-start(bf16[16,2048]{1,0:T(8,128)(2,1)S(1)} %convert_element_type.18), channel_id=1, source_target_pairs={{0,4},{4,0},{8,12},{12,8},{16,20},{20,16},{24,28},{28,24},{1,5},{5... | collective-permute-start | bytes 196616 | tf_op jit(solution)/shard_map/ppermute | solution.py:518
  33.9 2.2 %local.1 = (f32[256,2048]{1,0:T(8,128)S(1)}, f32[1,2048]{1,0:T(1,128)S(1)}) custom-call(bf16[256,2048]{1,0:T(8,128)(2,1)S(1)} %get-tuple-element.43.product, f32[2,256,2048]{2,1,0:T(8,128)S(1)} %get-tuple-element.44.long_hat, f32[1,2048]{1,0:T(1,128)S(1)} %bitcast.40, bf16[256,256]{1,0:T(8,128)(2,1)S(1)} %copy-done.5, bf16[256,256]{1,0:T(8,128)(2,1)S(1)} %copy-done.9), custom_call_target="tpu_custom_call" | custom-call | flops 1048576000 | bytes 7340032 | tf_op jit(solution)/shard_map/local/pallas_call | solution.py:657
  36.2 0.6 %collective-permute-done.5 = bf16[16,2048]{1,0:T(8,128)(2,1)S(1)} collective-permute-done((bf16[16,2048]{1,0:T(8,128)(2,1)S(1)}, bf16[16,2048]{1,0:T(8,128)(2,1)S(1)}, u32[]{:S(2)}, u32[]{:S(2)}) %collective-permute-start.5) | collective-permute-done | bytes 65568 | tf_op jit(solution)/shard_map/ppermute | solution.py:518
  36.8 0.4 collective-permute-done.4
  37.2 0.1 fusion.8
  37.3 3.0 %collective-permute-start.7 = (bf16[16,2048]{1,0:T(8,128)(2,1)S(1)}, bf16[16,2048]{1,0:T(8,128)(2,1)S(1)}, u32[]{:S(2)}, u32[]{:S(2)}) collective-permute-start(bf16[16,2048]{1,0:T(8,128)(2,1)S(1)} %get-tuple-element.50._), channel_id=1, source_target_pairs={{0,16},{4,20},{8,24},{12,28},{16,0},{20,4},{24,8},{28,12},{1,17},{... | collective-permute-start | bytes 196616 | tf_op jit(solution)/shard_map/ppermute | solution.py:518
  40.4 3.6 %near.1 = (f32[256,2048]{1,0:T(8,128)S(1)}, f32[256,2048]{1,0:T(8,128)S(1)}, bf16[256,2048]{1,0:T(8,128)(2,1)}) custom-call(f32[16,2048]{1,0:T(8,128)S(1)} %get-tuple-element.52.state, f32[16,8,2048]{2,1,0:T(8,128)S(1)} %get-tuple-element.40.refs_3_.decays.refs_2_, f32[16,8,2048]{2,1,0:T(8,128)S(1)} %get-tuple-element.42.leads.refs_3_, ...), custom_call_target="tpu_custom_call" | custom-call | flops 524288000 | bytes 7340032 | tf_op jit(solution)/shard_map/near/pallas_call | solution.py:662
  44.1 1.0 %finish.1 = bf16[256,2048]{1,0:T(8,128)(2,1)} custom-call(s32[1]{0:T(128)} %bitcast.refs_0_, f32[16,2048]{1,0:T(8,128)S(1)} %fusion.7.refs_1_, f32[16,8,2048]{2,1,0:T(8,128)S(1)} %get-tuple-element.40.refs_3_.decays.refs_2_, f32[16,8,2048]{2,1,0:T(8,128)S(1)} %get-tuple-element.42.leads.refs_3_, f32[256,2048]{1,0:T(8,128)S(1)} %get-tuple-element.48.refs_4_, ...), custom_call_target="tpu_custom_call" | custom-call | flops 52428800 | bytes 4194304 | tf_op jit(solution)/shard_map/finish/pallas_call | solution.py:668
  (40 shorter events, 0.1 us)
Async XLA Ops:
  0.6 7.5 %copy-start.5 = (bf16[256,256]{1,0:T(8,128)(2,1)S(1)}, bf16[256,256]{1,0:T(8,128)(2,1)}, u32[]{:S(2)}) copy-start(bf16[256,256]{1,0:T(8,128)(2,1)} %constant.16.clone.refs_3_.exact_rows) | copy-start | bytes 393220
  0.6 7.3 %copy-start.10 = (f32[16,2048]{1,0:T(8,128)S(1)}, f32[16,2048]{1,0:T(8,128)}, u32[]{:S(2)}) copy-start(f32[16,2048]{1,0:T(8,128)} %rates.1) | copy-start | bytes 393220
  0.7 7.3 %copy-start.16 = (f32[16,2048]{1,0:T(8,128)S(1)}, f32[16,2048]{1,0:T(8,128)}, u32[]{:S(2)}) copy-start(f32[16,2048]{1,0:T(8,128)} %param.28) | copy-start | bytes 393220
  0.7 11.1 %copy-start.6 = (f32[128,2048]{1,0:T(8,128)S(1)}, f32[128,2048]{1,0:T(8,128)}, u32[]{:S(2)}) copy-start(f32[128,2048]{1,0:T(8,128)} %taps.1) | copy-start | bytes 3145732
  0.7 11.1 %copy-start.7 = (f32[3,3,2048]{2,1,0:T(4,128)S(1)}, f32[3,3,2048]{2,1,0:T(4,128)}, u32[]{:S(2)}) copy-start(f32[3,3,2048]{2,1,0:T(4,128)} %short.7) | copy-start | bytes 221188
  0.7 11.1 %copy-start.8 = (f32[3,3,2048]{2,1,0:T(4,128)S(1)}, f32[3,3,2048]{2,1,0:T(4,128)}, u32[]{:S(2)}) copy-start(f32[3,3,2048]{2,1,0:T(4,128)} %short.9) | copy-start | bytes 221188
  0.7 11.1 %copy-start.9 = (bf16[256,256]{1,0:T(8,128)(2,1)S(1)}, bf16[256,256]{1,0:T(8,128)(2,1)}, u32[]{:S(2)}) copy-start(bf16[256,256]{1,0:T(8,128)(2,1)} %constant.18.clone.backward) | copy-start | bytes 393220
  0.7 11.1 %copy-start.11 = (bf16[256,384]{1,0:T(8,128)(2,1)S(1)}, bf16[256,384]{1,0:T(8,128)(2,1)}, u32[]{:S(2)}) copy-start(bf16[256,384]{1,0:T(8,128)(2,1)} %constant.17.clone.split_rows) | copy-start | bytes 589828
  3.0 17.4 %collective-permute-start = (bf16[144,2048]{1,0:T(8,128)(2,1)S(1)}, bf16[144,2048]{1,0:T(8,128)(2,1)S(1)}, u32[]{:S(2)}, u32[]{:S(2)}) collective-permute-start(bf16[144,2048]{1,0:T(8,128)(2,1)S(1)} %pack.1), channel_id=1, source_target_pairs={{0,4},{4,8},{8,12},{12,16},{16,20},{20,24},{24,28},{1,5},{5,9},{9,... | collective-permute-start | bytes 1769480 | tf_op jit(solution)/shard_map/ppermute | solution.py:513
  8.0 3.9 %copy-start.1 = (bf16[256,2048]{1,0:T(8,128)(2,1)S(1)}, bf16[256,2048]{1,0:T(8,128)(2,1)}, u32[]{:S(2)}) copy-start(bf16[256,2048]{1,0:T(8,128)(2,1)} %key.3) | copy-start | bytes 3145732
  8.0 3.8 %copy-start.2 = (bf16[256,2048]{1,0:T(8,128)(2,1)S(1)}, bf16[256,2048]{1,0:T(8,128)(2,1)}, u32[]{:S(2)}) copy-start(bf16[256,2048]{1,0:T(8,128)(2,1)} %value.4) | copy-start | bytes 3145732
  8.0 3.8 %copy-start.3 = (bf16[256,2048]{1,0:T(8,128)(2,1)S(1)}, bf16[256,2048]{1,0:T(8,128)(2,1)}, u32[]{:S(2)}) copy-start(bf16[256,2048]{1,0:T(8,128)(2,1)} %gate.3) | copy-start | bytes 3145732
  8.0 3.8 %copy-start.4 = (bf16[256,2048]{1,0:T(8,128)(2,1)S(1)}, bf16[256,2048]{1,0:T(8,128)(2,1)}, u32[]{:S(2)}) copy-start(bf16[256,2048]{1,0:T(8,128)(2,1)} %key_long.3) | copy-start | bytes 3145732
  8.0 3.8 %copy-start.13 = (f32[2048]{0:T(1024)S(1)}, f32[2048]{0:T(1024)}, u32[]{:S(2)}) copy-start(f32[2048]{0:T(1024)} %param.22) | copy-start | bytes 24580
  11.9 8.6 %copy-start.12 = (bf16[320,256]{1,0:T(8,128)(2,1)S(1)}, bf16[320,256]{1,0:T(8,128)(2,1)}, u32[]{:S(2)}) copy-start(bf16[320,256]{1,0:T(8,128)(2,1)} %constant.19.clone.backward) | copy-start | bytes 491524
  21.9 3.3 %collective-permute-start.3 = (f32[8,264]{1,0:T(8,128)S(1)}, f32[8,264]{1,0:T(8,128)S(1)}, u32[]{:S(2)}, u32[]{:S(2)}) collective-permute-start(f32[8,264]{1,0:T(8,128)S(1)} %get-tuple-element.33), channel_id=1, source_target_pairs={{0,3},{1,2},{2,1},{3,0},{4,7},{5,6},{6,5},{7,4},{8,11},{9,10},{10,... | collective-permute-start | bytes 25352 | tf_op jit(solution)/shard_map/ppermute | solution.py:518
  22.0 3.7 %collective-permute-start.2 = (f32[8,264]{1,0:T(8,128)S(1)}, f32[8,264]{1,0:T(8,128)S(1)}, u32[]{:S(2)}, u32[]{:S(2)}) collective-permute-start(f32[8,264]{1,0:T(8,128)S(1)} %get-tuple-element.33), channel_id=1, source_target_pairs={{0,2},{1,3},{2,0},{3,1},{4,6},{5,7},{6,4},{7,5},{8,10},{9,11},{10,... | collective-permute-start | bytes 25352 | tf_op jit(solution)/shard_map/ppermute | solution.py:518
  23.5 2.2 %collective-permute-start.1 = (f32[8,264]{1,0:T(8,128)S(1)}, f32[8,264]{1,0:T(8,128)S(1)}, u32[]{:S(2)}, u32[]{:S(2)}) collective-permute-start(f32[8,264]{1,0:T(8,128)S(1)} %get-tuple-element.33), channel_id=1, source_target_pairs={{0,1},{1,0},{2,3},{3,2},{4,5},{5,4},{6,7},{7,6},{8,9},{9,8},{10,11... | collective-permute-start | bytes 25352 | tf_op jit(solution)/shard_map/ppermute | solution.py:518
  25.7 8.2 %copy-start.15 = (f32[2048]{0:T(1024)S(1)}, f32[2048]{0:T(1024)}, u32[]{:S(2)}) copy-start(f32[2048]{0:T(1024)} %param.29) | copy-start | bytes 24580
  29.0 7.2 %collective-permute-start.6 = (bf16[16,2048]{1,0:T(8,128)(2,1)S(1)}, bf16[16,2048]{1,0:T(8,128)(2,1)S(1)}, u32[]{:S(2)}, u32[]{:S(2)}) collective-permute-start(bf16[16,2048]{1,0:T(8,128)(2,1)S(1)} %convert_element_type.18), channel_id=1, source_target_pairs={{0,12},{4,8},{8,4},{12,0},{16,28},{20,24},{24,20},{28,16},{1,13},{... | collective-permute-start | bytes 196616 | tf_op jit(solution)/shard_map/ppermute | solution.py:518
  32.5 4.3 %collective-permute-start.5 = (bf16[16,2048]{1,0:T(8,128)(2,1)S(1)}, bf16[16,2048]{1,0:T(8,128)(2,1)S(1)}, u32[]{:S(2)}, u32[]{:S(2)}) collective-permute-start(bf16[16,2048]{1,0:T(8,128)(2,1)S(1)} %convert_element_type.18), channel_id=1, source_target_pairs={{0,8},{4,12},{8,0},{12,4},{16,24},{20,28},{24,16},{28,20},{1,9},{5... | collective-permute-start | bytes 196616 | tf_op jit(solution)/shard_map/ppermute | solution.py:518
  33.0 4.3 %collective-permute-start.4 = (bf16[16,2048]{1,0:T(8,128)(2,1)S(1)}, bf16[16,2048]{1,0:T(8,128)(2,1)S(1)}, u32[]{:S(2)}, u32[]{:S(2)}) collective-permute-start(bf16[16,2048]{1,0:T(8,128)(2,1)S(1)} %convert_element_type.18), channel_id=1, source_target_pairs={{0,4},{4,0},{8,12},{12,8},{16,20},{20,16},{24,28},{28,24},{1,5},{5... | collective-permute-start | bytes 196616 | tf_op jit(solution)/shard_map/ppermute | solution.py:518
  36.2 4.2 %copy-start = (bf16[256,2048]{1,0:T(8,128)(2,1)S(1)}, bf16[256,2048]{1,0:T(8,128)(2,1)}, u32[]{:S(2)}) copy-start(bf16[256,2048]{1,0:T(8,128)(2,1)} %gate_long.3) | copy-start | bytes 3145732
  37.3 6.7 %collective-permute-start.7 = (bf16[16,2048]{1,0:T(8,128)(2,1)S(1)}, bf16[16,2048]{1,0:T(8,128)(2,1)S(1)}, u32[]{:S(2)}, u32[]{:S(2)}) collective-permute-start(bf16[16,2048]{1,0:T(8,128)(2,1)S(1)} %get-tuple-element.50._), channel_id=1, source_target_pairs={{0,16},{4,20},{8,24},{12,28},{16,0},{20,4},{24,8},{28,12},{1,17},{... | collective-permute-start | bytes 196616 | tf_op jit(solution)/shard_map/ppermute | solution.py:518
  (1 other events, 3.4 us)

commit v3 on v2

--- a/solution.py
+++ b/solution.py
@@ -19,6 +19,7 @@
 
 RIM = 2 * TILE
 EARLY = BLOCK + RIM
+TURN = EARLY + RIM
 
 
 def split_np(values):
@@ -125,8 +126,34 @@
     return total
 
 
+def row_sums(partial):
+    return lax.dot_general(
+        jnp.ones((TILE, LANES), F32),
+        partial,
+        (((1,), (1,)), ((), ())),
+        precision=lax.Precision.HIGHEST,
+        preferred_element_type=F32,
+    )
+
+
+def norm_factors(squares, all_width):
+    factor = lax.rsqrt(squares / all_width + 1e-06)
+    high, rest = split(factor)
+    low = (factor - high.astype(F32) - rest.astype(F32)).astype(BF16)
+    row = rows_of(factor.shape)
+    stack = jnp.where(row == 0, high.astype(F32), jnp.where(row == 1, rest.astype(F32), 0.0))
+    stack = jnp.where(row == 2, low.astype(F32), stack)
+    stack = jnp.concatenate([stack, jnp.zeros_like(stack)], 0).astype(BF16)
+    return lax.dot_general(
+        stack,
+        jnp.ones((RIM, LANES), BF16),
+        (((0,), (0,)), ((), ())),
+        preferred_element_type=F32,
+    )
+
+
 def pack_kernel(
-    key, value, gate, gate_long, key_long, short, out, tops, ends, taps, arrived
+    _, key, value, gate, gate_long, key_long, short, out, tops, ends, taps, arrived
 ):
     rows, width = key.shape
     copies = []
@@ -150,26 +177,26 @@
         here = pl.ds(chunk * WIDTH, WIDTH)
         for copy in copies[chunk]:
             copy.wait()
-        key_part, value_part = tops[0, :, here].astype(F32), tops[1, :, here].astype(F32)
-        product = ahead_filter(key_part, taps[0, :, here]) * ahead_filter(
-            value_part, taps[1, :, here]
-        )
-        row = rows_of((TILE, WIDTH))
-        key_end, value_end = key_part[-TILE:], value_part[-TILE:]
-        gate_end, gate_long_end, key_long_end = (
-            ends[i, :, here].astype(F32)[TILE:] for i in range(3)
-        )
-        first = jnp.where(
-            row < 2,
-            pltpu.roll(key_end, 2, 0),
-            jnp.where(row < 4, pltpu.roll(value_end, 4, 0), gate_end),
-        )
-        second = jnp.where(
-            row < 2,
-            pltpu.roll(gate_long_end, 2, 0),
-            jnp.where(row < 4, pltpu.roll(key_long_end, 4, 0), product[TILE:RIM]),
-        )
-        out[:, here] = jnp.concatenate([first, second, product[RIM:]], 0).astype(BF16)
+        for lanes in lane_tiles(chunk * WIDTH):
+            key_part, value_part = tops[0, :, lanes].astype(F32), tops[1, :, lanes].astype(F32)
+            product = ahead_filter(key_part, taps[0, :, lanes]) * ahead_filter(
+                value_part, taps[1, :, lanes]
+            )
+            row = rows_of((TILE, LANES))
+            gate_end, gate_long_end, key_long_end = (
+                ends[i, :, lanes].astype(F32)[TILE:] for i in range(3)
+            )
+            first = jnp.where(
+                row < 2,
+                pltpu.roll(key_part[-TILE:], 2, 0),
+                jnp.where(row < 4, pltpu.roll(value_part[-TILE:], 4, 0), gate_end),
+            )
+            second = jnp.where(
+                row < 2,
+                pltpu.roll(gate_long_end, 2, 0),
+                jnp.where(row < 4, pltpu.roll(key_long_end, 4, 0), product[TILE:RIM]),
+            )
+            out[:, lanes] = jnp.concatenate([first, second, product[RIM:]], 0).astype(BF16)
 
 
 def mode_tables(rates, mode, lanes, offset, sign):
@@ -196,7 +223,9 @@
     return [pl.ds(pl.multiple_of(start, LANES), LANES) for start in starts]
 
 
-def impulse_kernel(count, place, rates, weights, exact_rows, long_hat, carry, leads, decays, impulse):
+def impulse_kernel(
+    count, place, rates, weights, exact_rows, _, long_hat, carry, leads, decays, tails, impulse
+):
     modes, width = rates.shape
     rows = impulse.shape[0]
     for i, weight in enumerate(carry_weights(place[0], count, rows, rates[...])):
@@ -210,6 +239,7 @@
                 start = lead * weights[mode : mode + 1, lanes]
                 leads[mode, :, lanes] = start * jnp.exp(-rates[mode : mode + 1, lanes])
                 decays[mode, :, lanes] = decay
+                tails[mode, :, lanes] = mode_tables(rates, mode, lanes, TILE - 1.0, -1.0)[0]
                 starts.append(start)
                 steps.append(decay)
 
@@ -230,20 +260,18 @@
 
 
 def own_kernel(
-    gate, key, value, key_long, short, short_long, skip, taps, split_rows, exact_rows, backward, _,
-    conv_early, gate_early, mixed_late, squares_late, key_feat, taps_hat, heads,
+    gate, key, value, short, skip, taps, split_rows, exact_rows, backward, _,
+    conv_early, gate_early, mixed_late, squares_late, taps_hat, heads, sums,
 ):
     rows, width = gate.shape
-    squares_late[...] = jnp.zeros(squares_late.shape, F32)
+    sums[...] = jnp.zeros(sums.shape, F32)
 
     def step(here, base):
         hat = forward_split(split_rows[...], taps[:, here])
         taps_hat[:, here] = hat
-        keys, values, gates, keys_long = (
-            ref[:, here].astype(F32) for ref in (key, value, gate, key_long)
-        )
+        keys, values, gates = (ref[:, here].astype(F32) for ref in (key, value, gate))
         heads[:, here] = jnp.concatenate(
-            [part[:TILE] for part in (keys, values, gates, keys_long)]
+            [part[:TILE] for part in (keys, values, gates)]
             + [taps[BLOCK - TILE :, here]],
             0,
         )
@@ -268,15 +296,15 @@
         mixed = (feat[EARLY:] * total[EARLY:]).astype(BF16)
         mixed_late[:, here] = mixed
         kept = mixed.astype(F32)
-        squares_late[...] = squares_late[...] + lane_parts(kept * kept)
-        key_feat[:, here] = shifted_filter(keys_long, short_long[1, :, here])
+        sums[...] = sums[...] + lane_parts(kept * kept)
 
     over_channels(width, step)
+    squares_late[...] = row_sums(sums[...])
 
 
 def medium_kernel(
     halo, heads, short, skip, taps_hat, exact_rows, backward,
-    conv_early, gate_early, mixed_late, squares_late,
+    conv_early, gate_early, mixed_late, _, __,
     mixed, mixed_rim, squares, rim_long, total,
 ):
     width = halo.shape[1]
@@ -287,8 +315,8 @@
         rim, rim_late = halo_part[:TILE], halo_part[TILE:RIM]
         rim_long[:, here] = rim_late
         row = rows_of((TILE, WIDTH))
-        key_part, value_part, gate_part, _, tail = (
-            heads[i * TILE : (i + 1) * TILE, here] for i in range(5)
+        key_part, value_part, gate_part, tail = (
+            heads[i * TILE : (i + 1) * TILE, here] for i in range(4)
         )
         keys = jnp.where(row >= 6, pltpu.roll(key_part, 6, 0), pltpu.roll(rim, 4, 0))
         values = jnp.where(row >= 6, pltpu.roll(value_part, 6, 0), pltpu.roll(rim, 2, 0))
@@ -319,54 +347,68 @@
         total[...] = total[...] + lane_parts(kept * kept)
 
     over_channels(width, step, unrolled=True)
-    squares[...] = lax.dot_general(
-        jnp.ones((TILE, LANES), F32),
-        jnp.concatenate([total[...], squares_late[...]], 0),
-        (((1,), (1,)), ((), ())),
-        precision=lax.Precision.HIGHEST,
-        preferred_element_type=F32,
-    )
-
-
-def value_kernel(mixed, mixed_rim, gain, key_feat, heads, rim_long, short, rates, parts, tails):
+    squares[...] = row_sums(total[...])
+
+
+def late_kernel(
+    all_width, squares, mixed_late, key_long, gain, short, decays, tails, product_out, state
+):
+    rows, width = key_long.shape
+    modes = decays.shape[0]
+    factors = norm_factors(squares[...], all_width)
+
+    def step(here, base):
+        for lanes in lane_tiles(base):
+            frame = mixed_late[:, lanes].astype(F32) * factors
+            feat = shifted_filter(frame, short[2, :, lanes] * gain[:, lanes])
+            keys = shifted_filter(key_long[EARLY:, lanes].astype(F32), short[1, :, lanes])
+            product = (keys * feat)[TURN - EARLY :]
+            product_out[:, lanes] = product.astype(BF16)
+            held = [product[:TILE]] * modes
+            steps = [decays[mode, :, lanes] for mode in range(modes)]
+            for i in range(TILE, rows - TURN, TILE):
+                held = [old * decay + product[i : i + TILE] for old, decay in zip(held, steps)]
+            for mode in range(modes):
+                state[mode : mode + 1, lanes] = sublane_sum(held[mode] * tails[mode, :, lanes])
+
+    over_channels(width, step, unrolled=True)
+
+
+def value_kernel(
+    mixed, mixed_rim, gain, key_long, rim_long, short, rates, tails, parts, tails_far
+):
     rows, width = mixed.shape
     modes = rates.shape[0]
 
     def step(here, base):
-        frame = jnp.concatenate([mixed_rim[:, here], mixed[:, here].astype(F32)], 0)
+        frame = jnp.concatenate([mixed_rim[:, here], mixed[:TURN, here].astype(F32)], 0)
         keys = shifted_filter(
             jnp.concatenate(
-                [pltpu.roll(rim_long[:, here], 4, 0), heads[3 * TILE : 4 * TILE, here]], 0
+                [pltpu.roll(rim_long[:, here], 4, 0), key_long[:TURN, here].astype(F32)], 0
             ),
             short[1, :, here],
         )[TILE:]
-        keys = jnp.concatenate([keys, key_feat[TILE:, here]], 0)
         weights = short[2, :, here] * gain[:, here]
         for j in range(3):
             moved = frame if j == 0 else pltpu.roll(frame, j, 0)
             parts[j, :, here] = keys * (weights[j : j + 1] * moved[TILE:])
-        for lanes in lane_tiles(base):
-            for mode in range(modes):
-                tails[mode, :, lanes] = mode_tables(rates, mode, lanes, TILE - 1.0, -1.0)[0]
+        for mode in range(modes):
+            tails_far[mode, :, here] = tails[mode, :, here] * jnp.exp(
+                (TURN - rows) * rates[mode : mode + 1, here]
+            )
 
     over_channels(width, step, unrolled=True)
 
 
-def state_kernel(all_width, squares, parts, tails, decays, product_out, state, factors):
-    rows, width = product_out.shape
+def state_kernel(
+    all_width, squares, squares_late, parts, tails_far, decays, state_late,
+    product_out, state, factors,
+):
+    width = product_out.shape[1]
     modes = decays.shape[0]
-    factor = lax.rsqrt(squares[...] / all_width + 1e-06)
-    high, rest = split(factor)
-    low = (factor - high.astype(F32) - rest.astype(F32)).astype(BF16)
-    row = rows_of(factor.shape)
-    stack = jnp.where(row == 0, high.astype(F32), jnp.where(row == 1, rest.astype(F32), 0.0))
-    stack = jnp.where(row == 2, low.astype(F32), stack)
-    stack = jnp.concatenate([stack, jnp.zeros_like(stack)], 0).astype(BF16)
-    inverse = lax.dot_general(
-        stack,
-        jnp.ones((RIM, LANES), BF16),
-        (((0,), (0,)), ((), ())),
-        preferred_element_type=F32,
+    inverse = norm_factors(squares[...], all_width)
+    inverse = jnp.concatenate(
+        [inverse, norm_factors(squares_late[...], all_width)[: TURN - EARLY]], 0
     )
     factors[0] = inverse[TILE:]
     factors[1] = pltpu.roll(inverse, 1, 0)[TILE:]
@@ -376,7 +418,7 @@
         for lanes in lane_tiles(base):
             steps = [decays[mode, :, lanes] for mode in range(modes)]
             held = None
-            for i in range(0, rows, 2 * TILE):
+            for i in range(0, TURN, 2 * TILE):
                 part = slice(i, i + 2 * TILE)
                 product = (
                     parts[0, part, lanes] * factors[0, part]
@@ -390,27 +432,28 @@
                     else:
                         held = [old * decay + piece for old, decay in zip(held, steps)]
             for mode in range(modes):
-                state[mode : mode + 1, lanes] = sublane_sum(held[mode] * tails[mode, :, lanes])
+                state[mode : mode + 1, lanes] = state_late[mode : mode + 1, lanes] + sublane_sum(
+                    held[mode] * tails_far[mode, :, lanes]
+                )
 
     over_channels(width, step, unrolled=True)
 
 
-def local_kernel(product, long_hat, skip, exact_rows, backward, out, done):
-    rows, width = product.shape
+def local_kernel(early, late, long_hat, skip, exact_rows, backward, out, done):
+    rows, width = out.shape
     done[...] = jnp.zeros(done.shape, F32)
 
     def step(here, base):
         spectra = []
+        product = jnp.concatenate([early[:, here].astype(F32), late[:, here].astype(F32)], 0)
         for block in range(rows // BLOCK):
             part = slice(block * BLOCK, (block + 1) * BLOCK)
-            piece = product[part, here]
-            spectra.append(forward_exact(exact_rows[...], piece))
+            piece = product[part]
+            spectra.append(forward_exact(exact_rows[...], piece.astype(BF16)))
             total = times(long_hat[0, :, here], spectra[block])
             for lag in range(1, block + 1):
                 total = total + times(long_hat[lag, :, here], spectra[block - lag])
-            out[part, here] = backward_exact(backward[...], total) + skip[:, here] * piece.astype(
-                F32
-            )
+            out[part, here] = backward_exact(backward[...], total) + skip[:, here] * piece
 
     over_channels(width, step, unrolled=True)
 
@@ -423,11 +466,11 @@
 
 def near_kernel(
     state, decays, leads, local, gate_long, rim_long, short, mixed, _,
-    out, gate_feat, mixed_out, sent,
+    near, gate_feat, mixed_out, out, held_out, sent,
 ):
     rows, width = local.shape
-    copy = pltpu.make_async_copy(mixed, mixed_out, sent)
-    copy.start()
+    copies = [pltpu.make_async_copy(mixed, mixed_out, sent.at[width // WIDTH])]
+    copies[0].start()
 
     def step(here, base):
         gates = jnp.concatenate(
@@ -436,26 +479,38 @@
         gate_feat[:, here] = shifted_filter(gates, short[0, :, here])[TILE:]
         for lanes in lane_tiles(base):
 
+            held = []
+
             def emit(i, total):
                 part = slice(i * TILE, (i + 1) * TILE)
-                out[part, lanes] = gate_feat[part, lanes] * (local[part, lanes] + total)
+                held.append(gate_feat[part, lanes] * (local[part, lanes] + total))
+                near[part, lanes] = held[-1]
+                if i % 2 == 1:
+                    held_out[(i - 1) * TILE : (i + 1) * TILE, lanes] = jnp.concatenate(
+                        held[-2:], 0
+                    ).astype(BF16)
 
             response(*modal_tables(state, decays, leads, lanes), rows // TILE, emit)
+        copy = pltpu.make_async_copy(
+            held_out.at[:, here], out.at[:, here], sent.at[base // WIDTH]
+        )
+        copy.start()
+        copies.append(copy)
 
     over_channels(width, step, unrolled=True)
-    copy.wait()
-
-
-def finish_kernel(count, place, state, decays, leads, near, gate_feat, out, held_out, sent):
+    for copy in copies:
+        copy.wait()
+
+
+def finish_kernel(count, place, state, decays, leads, near, gate_feat, _, out, held_out, sent):
     rows, width = near.shape
     group, radix = list(stages(count))[-1] if count > 1 else (1, 1)
-    later = (place[0] // group) % radix > 0
-    copies = []
-    for chunk in range(width // PART):
-        here = pl.ds(chunk * PART, PART)
-
-        @pl.when(later)
-        def _():
+
+    @pl.when((place[0] // group) % radix > 0)
+    def _():
+        copies = []
+        for chunk in range(width // PART):
+            here = pl.ds(chunk * PART, PART)
             for tile in range(PART // LANES):
                 lanes = slice(chunk * PART + tile * LANES, chunk * PART + (tile + 1) * LANES)
                 held = []
@@ -469,16 +524,11 @@
                         ).astype(BF16)
 
                 response(*modal_tables(state, decays, leads, lanes), rows // TILE, emit)
-
-        @pl.when(jnp.logical_not(later))
-        def _():
-            held_out[:, here] = near[:, here].astype(BF16)
-
-        copy = pltpu.make_async_copy(held_out.at[:, here], out.at[:, here], sent.at[chunk])
-        copy.start()
-        copies.append(copy)
-    for copy in copies:
-        copy.wait()
+            copy = pltpu.make_async_copy(held_out.at[:, here], out.at[:, here], sent.at[chunk])
+            copy.start()
+            copies.append(copy)
+        for copy in copies:
+            copy.wait()
 
 
 SCALAR = pl.BlockSpec(memory_space=pltpu.SMEM)
@@ -487,13 +537,14 @@
 MIB = 1024 * 1024
 
 
-def call(kernel, name, in_specs, out_shape, scratch=(), flops=0, moved=0, room=12, out_specs=None):
+def call(kernel, name, in_specs, out_shape, scratch=(), flops=0, moved=0, room=12, out_specs=None, aliases=None):
     return pl.pallas_call(
         kernel,
         in_specs=in_specs,
         out_specs=out_specs or jax.tree.map(lambda _: KEPT, out_shape),
         out_shape=out_shape,
         scratch_shapes=list(scratch),
+        input_output_aliases=aliases or {},
         compiler_params=pltpu.CompilerParams(vmem_limit_bytes=room * MIB),
         name=name,
         cost_estimate=pl.CostEstimate(flops=flops, bytes_accessed=moved, transcendentals=0),
@@ -516,6 +567,13 @@
 def exchanged(value, axis, flip):
     count = lax.axis_size(axis)
     return lax.ppermute(value, axis, [(source, source ^ flip) for source in range(count)])
+
+
+def sum_over(value, axis):
+    total = value
+    for part in [exchanged(value, axis, turn) for turn in range(1, lax.axis_size(axis))]:
+        total = total + part
+    return total
 
 
 def stages(count):
@@ -576,7 +634,6 @@
     rows, width = gate_medium.shape
     modes = decay_rates.shape[0]
     blocks = rows // BLOCK
-    frame = rows + TILE
     count = lax.axis_size("ctx")
     all_width = width * lax.axis_size("ch")
     exact_rows, split_rows, backward, backward_late = (jnp.asarray(m) for m in transforms())
@@ -586,91 +643,99 @@
     ]
     place = lax.axis_index("ctx").astype(jnp.int32).reshape(1)
     pack = call(
-        pack_kernel, "pack", [FAR] * 6, arr((EARLY, width), BF16),
+        pack_kernel, "pack", [SCALAR] + [FAR] * 6, arr((EARLY, width), BF16),
         [
             pltpu.VMEM((2, EARLY, width), BF16), pltpu.VMEM((3, RIM, width), BF16),
             pltpu.VMEM((2, 3, width), F32), pltpu.SemaphoreType.DMA((width // WIDTH, 6)),
         ],
-    )(*far)
+    )(place, *far)
     halo = passed_along(pack, "ctx", 1)
 
     skip_row = skip_medium[None]
     mode_weight = residues * jnp.sqrt(-jnp.expm1(-2.0 * decay_rates))
     turns = sum(2 * radix for _, radix in stages(count)) or 1
-    long_hat, carry, leads, decays = call(
+    conv_early, gate_early, mixed_late, squares_late, taps_hat, heads = call(
+        own_kernel, "own", [KEPT] * 10,
+        [
+            arr((EARLY, width), F32), arr((EARLY, width), F32),
+            arr((rows - EARLY, width), BF16), arr((TILE, rows - EARLY), F32),
+            arr((2 * BLOCK, width), F32), arr((4 * TILE, width), F32),
+        ],
+        [pltpu.VMEM((rows - EARLY, LANES), F32)],
+        flops=2000 * rows * width, moved=10 * rows * width, room=16,
+    )(
+        gate_medium, key_medium, value_medium, short_medium, skip_row, filter_medium, split_rows,
+        exact_rows, backward, pack,
+    )
+
+    table = arr((modes, TILE, width), F32)
+    long_hat, carry, leads, decays, tails = call(
         lambda *refs: impulse_kernel(count, *refs), "impulse",
-        [SCALAR] + [KEPT] * 3,
+        [SCALAR] + [KEPT] * 4,
         [
             arr((blocks, 2 * BLOCK, width), F32), arr((turns, modes, width), F32),
-            arr((modes, TILE, width), F32), arr((modes, TILE, width), F32),
+            table, table, table,
         ],
         [pltpu.VMEM((rows, WIDTH), F32)],
         flops=2000 * rows * width, moved=10 * rows * width,
-    )(place, decay_rates, mode_weight, exact_rows)
-
-    conv_early, gate_early, mixed_late, squares_late, key_feat, taps_hat, heads = call(
-        own_kernel, "own", [KEPT] * 12,
+    )(place, decay_rates, mode_weight, exact_rows, squares_late)
+
+    total_late = sum_over(squares_late, "ch")
+    product_late, state_late = call(
+        lambda *refs: late_kernel(all_width, *refs), "late", [KEPT] * 7,
+        [arr((rows - TURN, width), BF16), arr((modes, width), F32)],
+        flops=100 * rows * width, moved=10 * rows * width,
+    )(total_late, mixed_late, key_long, norm_gain[None], short_long, decays, tails)
+
+    mixed_medium, mixed_rim, squares, rim_long = call(
+        medium_kernel, "medium", [KEPT] * 12,
         [
-            arr((EARLY, width), F32), arr((EARLY, width), F32),
-            arr((rows - EARLY, width), BF16), arr((rows - EARLY, LANES), F32),
-            arr((rows, width), F32), arr((2 * BLOCK, width), F32), arr((5 * TILE, width), F32),
-        ],
-        flops=2000 * rows * width, moved=10 * rows * width, room=16,
-    )(
-        gate_medium, key_medium, value_medium, key_long, short_medium, short_long, skip_row,
-        filter_medium, split_rows, exact_rows, backward, carry,
-    )
-
-    mixed_medium, mixed_rim, squares, rim_long = call(
-        medium_kernel, "medium", [KEPT] * 11,
-        [
-            arr((rows, width), BF16), arr((TILE, width), F32), arr((TILE, frame), F32),
+            arr((rows, width), BF16), arr((TILE, width), F32), arr((TILE, EARLY + TILE), F32),
             arr((TILE, width), F32),
         ],
         [pltpu.VMEM((EARLY + TILE, LANES), F32)],
         flops=1000 * rows * width, moved=10 * rows * width,
     )(
         halo, heads, short_medium, skip_row, taps_hat, exact_rows, backward_late,
-        conv_early, gate_early, mixed_late, squares_late,
-    )
-
-    parts = [exchanged(squares, "ch", turn) for turn in range(1, lax.axis_size("ch"))]
-    total_squares = squares
-    for part in parts:
-        total_squares = total_squares + part
-
-    long_parts, tails = call(
-        value_kernel, "value", [KEPT] * 8,
-        [arr((3, rows, width), F32), arr((modes, TILE, width), F32)],
+        conv_early, gate_early, mixed_late, state_late, carry,
+    )
+
+    total_squares = sum_over(squares, "ch")
+    long_parts, tails_far = call(
+        value_kernel, "value", [KEPT] * 8, [arr((3, TURN, width), F32), table],
         flops=1000 * rows * width, moved=10 * rows * width,
     )(
-        mixed_medium, mixed_rim, norm_gain[None], key_feat, heads, rim_long, short_long,
-        decay_rates,
-    )
-    product_long, state = call(
-        lambda *refs: state_kernel(all_width, *refs), "state", [KEPT] * 4,
-        [arr((rows, width), BF16), arr((modes, width), F32)],
-        [pltpu.VMEM((3, rows, LANES), F32)],
+        mixed_medium, mixed_rim, norm_gain[None], key_long, rim_long, short_long, decay_rates, tails
+    )
+    product_early, state = call(
+        lambda *refs: state_kernel(all_width, *refs), "state", [KEPT] * 6,
+        [arr((TURN, width), BF16), arr((modes, width), F32)],
+        [pltpu.VMEM((3, TURN, LANES), F32)],
         flops=100 * rows * width, moved=10 * rows * width,
-    )(total_squares, long_parts, tails, decays)
+    )(total_squares, total_late, long_parts, tails_far, decays, state_late)
 
     local, done = call(
-        local_kernel, "local", [KEPT] * 5, [arr((rows, width), F32), arr((1, width), F32)],
+        local_kernel, "local", [KEPT] * 6, [arr((rows, width), F32), arr((1, width), F32)],
         flops=2000 * rows * width, moved=14 * rows * width,
-    )(product_long, long_hat, skip_long[None], exact_rows, backward)
+    )(product_early, product_late, long_hat, skip_long[None], exact_rows, backward)
     known, incoming, last_sent = carried_state(state, carry, done)
-    near, gate_feat, mixed_out = call(
+    near, gate_feat, mixed_out, mixed_long = call(
         near_kernel, "near", [KEPT] * 9,
-        [arr((rows, width), F32), arr((rows, width), F32), arr((rows, width), BF16)],
-        [pltpu.SemaphoreType.DMA], out_specs=[KEPT, KEPT, FAR],
+        [
+            arr((rows, width), F32), arr((rows, width), F32), arr((rows, width), BF16),
+            arr((rows, width), BF16),
+        ],
+        [pltpu.VMEM((rows, width), BF16), pltpu.SemaphoreType.DMA((width // WIDTH + 1,))],
+        out_specs=[KEPT, KEPT, FAR, FAR],
         flops=1000 * rows * width, moved=14 * rows * width,
     )(known, decays, leads, local, gate_long, rim_long, short_long, mixed_medium, last_sent)
     mixed_long = call(
-        lambda *refs: finish_kernel(count, *refs), "finish", [SCALAR] + [KEPT] * 5,
+        lambda *refs: finish_kernel(count, *refs), "finish", [SCALAR] + [KEPT] * 5 + [FAR],
         arr((rows, width), BF16),
-        [pltpu.VMEM((rows, width), BF16), pltpu.SemaphoreType.DMA((width // PART,))], out_specs=FAR,
+        [pltpu.VMEM((rows, width), BF16), pltpu.SemaphoreType.DMA((width // PART,))],
+        out_specs=FAR, aliases={6: 0},
         flops=100 * rows * width, moved=8 * rows * width,
-    )(place, incoming, decays, leads, near, gate_feat)
+    )(place, incoming, decays, leads, near, gate_feat, mixed_long)
     return (mixed_out, mixed_long)
 
 

time: 45.8 us -> 44.3 us (0.967)
  waiting for transfers between devices: 4.32 us -> 3.12 us
    ppermute x1, waiting for transfers between devices: 2.44 us -> 0.01 us  [passed_along(): lax.ppermute(value, axis, [(source, source + steps) for source in range(c...]
    ppermute x7 -> x10, waiting for transfers between devices: 1.88 us -> 3.11 us  [exchanged(): lax.ppermute(value, axis, [(source, source ^ flip) for source in range(co...]
    pallas_call x1, Pallas kernels: 3.62 us -> 4.71 us  [body(): call(near_kernel, 'near', [KEPT] * 9, [arr((rows, width), F32), arr((rows...]
    pallas_call x1, Pallas kernels: 1.05 us -> 0.06 us  [body(): call(lambda *refs: finish_kernel(count, *refs), 'finish', [SCALAR] + [KEP...]
    pallas_call x6 -> x7, Pallas kernels: 16.3 us -> 15.7 us  [the longest x1 4.76 us: body(): call(own_kernel, 'own', [KEPT] * 10, [arr((EARLY, width), F32), arr((EARL...]
    ppermute x7 -> x10, starting transfers between devices: 9.94 us -> 10.2 us  [exchanged(): lax.ppermute(value, axis, [(source, source ^ flip) for source in range(co...]
  transfers between devices with their start and end apart: 8 -> 11, of which waited for: 5 -> 4; matrix products, arithmetic and copies ran while one was open for 0% -> 0% of each run, Pallas kernels for 37% -> 42%
where the time goes in v3:
time: 44.3 us; the launch traced here: 44.1 us
  Pallas kernels  24.4 us (55%)
  starting transfers between devices  15.1 us (34%)
  waiting for transfers between devices  3.12 us (7%)
  between operations  1.17 us (3%)
    ppermute x10, starting transfers between devices, exchanged(): lax.ppermute(value, axis, [(source, source ^ flip) for source in range(co...  10.2 us
    ppermute x1, starting transfers between devices, passed_along(): lax.ppermute(value, axis, [(source, source + steps) for source in range(c...  4.91 us
    pallas_call x1, Pallas kernels, body(): call(own_kernel, 'own', [KEPT] * 10, [arr((EARLY, width), F32), arr((EARL...  4.76 us
    pallas_call x1, Pallas kernels, body(): call(near_kernel, 'near', [KEPT] * 9, [arr((rows, width), F32), arr((rows...  4.71 us
    pallas_call x1, Pallas kernels, body(): call(lambda *refs: impulse_kernel(count, *refs), 'impulse', [SCALAR] + [K...  3.97 us
    ppermute x10, waiting for transfers between devices, exchanged(): lax.ppermute(value, axis, [(source, source ^ flip) for source in range(co...  3.11 us
    pallas_call x1, Pallas kernels, body(): call(local_kernel, 'local', [KEPT] * 6, [arr((rows, width), F32), arr((1,...  2.23 us
    pallas_call x1, Pallas kernels, body(): call(pack_kernel, 'pack', [SCALAR] + [FAR] * 6, arr((EARLY, width), BF16)...  2.18 us
  transfers between devices with their start and end apart: 11, of which 4 were waited for; matrix products, arithmetic and copies ran while one was open for 0% of the time, Pallas kernels for 42%

profile of v3, /device:TPU:0, one launch (start us, length us, event | category | flops | bytes accessed | tf_op | source)
XLA Modules:
  0.0 44.1 jit_solution(17258234768196618610)
XLA Ops:
  0.7 2.2 %pack.1._ = bf16[144,2048]{1,0:T(8,128)(2,1)S(1)} custom-call(s32[1]{0:T(128)} %bitcast._.refs_0_, bf16[256,2048]{1,0:T(8,128)(2,1)} %key.3, bf16[256,2048]{1,0:T(8,128)(2,1)} %value.4, bf16[256,2048]{1,0:T(8,128)(2,1)} %gate.3, bf16[256,2048]{1,0:T(8,128)(2,1)} %gate_long.3, bf16[256,2048]{1,0:T(8,128)(2,1)} %key_long.3, f32[3,3,2048]{2,1,0:T(4,128)} %short.7), custom_call_target="tpu_custom_call" | custom-call | tf_op jit(solution)/shard_map/pack/pallas_call | solution.py:645
  2.9 4.9 %collective-permute-start = (bf16[144,2048]{1,0:T(8,128)(2,1)S(1)}, bf16[144,2048]{1,0:T(8,128)(2,1)S(1)}, u32[]{:S(2)}, u32[]{:S(2)}) collective-permute-start(bf16[144,2048]{1,0:T(8,128)(2,1)S(1)} %pack.1._), channel_id=1, source_target_pairs={{0,4},{4,8},{8,12},{12,16},{16,20},{20,24},{24,28},{1,5},{5,9},{9,... | collective-permute-start | bytes 1769480 | tf_op jit(solution)/shard_map/ppermute | solution.py:564
  8.0 4.8 %own.1 = (f32[144,2048]{1,0:T(8,128)S(1)}, f32[144,2048]{1,0:T(8,128)S(1)}, bf16[112,2048]{1,0:T(8,128)(2,1)S(1)}, f32[8,112]{1,0:T(8,128)S(1)}, f32[256,2048]{1,0:T(8,128)S(1)}, /*index=5*/f32[32,2048]{1,0:T(8,128)S(1)}) custom-call(bf16[256,2048]{1,0:T(8,128)(2,1)S(1)} %copy-done.4, bf16[256,2048]{1,0:T(8,128)(2,1)S(1)} %copy-done.2, ...), custom_call_target="tpu_custom_call" | custom-call | flops 1048576000 | bytes 5242880 | tf_op jit(solution)/shard_map/own/pallas_call | solution.py:657
  12.7 0.7 %collective-permute-start.3 = (f32[8,112]{1,0:T(8,128)S(1)}, f32[8,112]{1,0:T(8,128)S(1)}, u32[]{:S(2)}, u32[]{:S(2)}) collective-permute-start(f32[8,112]{1,0:T(8,128)S(1)} %get-tuple-element.29.refs_4_), channel_id=1, source_target_pairs={{0,3},{1,2},{2,1},{3,0},{4,7},{5,6},{6,5},{7,4},{8,11},{9,10},{10,... | collective-permute-start | bytes 10760 | tf_op jit(solution)/shard_map/ppermute | solution.py:569
  13.4 0.9 %collective-permute-start.2 = (f32[8,112]{1,0:T(8,128)S(1)}, f32[8,112]{1,0:T(8,128)S(1)}, u32[]{:S(2)}, u32[]{:S(2)}) collective-permute-start(f32[8,112]{1,0:T(8,128)S(1)} %get-tuple-element.29.refs_4_), channel_id=1, source_target_pairs={{0,2},{1,3},{2,0},{3,1},{4,6},{5,7},{6,4},{7,5},{8,10},{9,11},{10,... | collective-permute-start | bytes 10760 | tf_op jit(solution)/shard_map/ppermute | solution.py:569
  14.3 0.3 collective-permute-start.1
  14.6 0.1 sqrt_multiply_fusion.refs_2_
  14.7 4.0 %impulse.1 = (f32[2,256,2048]{2,1,0:T(8,128)S(1)}, f32[12,16,2048]{2,1,0:T(8,128)S(1)}, f32[16,8,2048]{2,1,0:T(8,128)S(1)}, f32[16,8,2048]{2,1,0:T(8,128)S(1)}, f32[16,8,2048]{2,1,0:T(8,128)S(1)}) custom-call(s32[1]{0:T(128)} %bitcast._.refs_0_, f32[16,2048]{1,0:T(8,128)S(1)} %copy-done.9, f32[16,2048]{1,0:T(8,128)S(1)} %sqrt_multiply_fusion.refs_2_, ...), custom_call_target="tpu_custom_call" | custom-call | flops 1048576000 | bytes 5242880 | tf_op jit(solution)/shard_map/impulse/pallas_call | solution.py:672
  18.8 1.8 %late.1 = (bf16[96,2048]{1,0:T(8,128)(2,1)S(1)}, f32[16,2048]{1,0:T(8,128)S(1)}) custom-call(f32[8,112]{1,0:T(8,128)S(1)} %add_add_fusion.1.refs_0_.refs_1_, bf16[112,2048]{1,0:T(8,128)(2,1)S(1)} %get-tuple-element.35.refs_1_.mixed_late, bf16[256,2048]{1,0:T(8,128)(2,1)S(1)} %copy-done, f32[1,2048]{1,0:T(1,128)S(1)} %bitcast.39, ...), custom_call_target="tpu_custom_call" | custom-call | flops 52428800 | bytes 5242880 | tf_op jit(solution)/shard_map/late/pallas_call | solution.py:684
  20.6 1.4 %medium.1 = (bf16[256,2048]{1,0:T(8,128)(2,1)S(1)}, f32[8,2048]{1,0:T(8,128)S(1)}, f32[8,152]{1,0:T(8,128)S(1)}, f32[8,2048]{1,0:T(8,128)S(1)}) custom-call(bf16[144,2048]{1,0:T(8,128)(2,1)S(1)} %collective-permute-done.halo, f32[32,2048]{1,0:T(8,128)S(1)} %get-tuple-element.31.heads, f32[3,3,2048]{2,1,0:T(4,128)S(1)} %copy-done.8, f32[1,2048]{1,0:T(1,128)S(1)} %bitcast.38, ...), custom_call_target="tpu_custom_call" | custom-call | flops 524288000 | bytes 5242880 | tf_op jit(solution)/shard_map/medium/pallas_call | solution.py:690
  22.1 1.1 %collective-permute-start.6 = (f32[8,152]{1,0:T(8,128)S(1)}, f32[8,152]{1,0:T(8,128)S(1)}, u32[]{:S(2)}, u32[]{:S(2)}) collective-permute-start(f32[8,152]{1,0:T(8,128)S(1)} %get-tuple-element.39), channel_id=1, source_target_pairs={{0,3},{1,2},{2,1},{3,0},{4,7},{5,6},{6,5},{7,4},{8,11},{9,10},{10,... | collective-permute-start | bytes 14600 | tf_op jit(solution)/shard_map/ppermute | solution.py:569
  23.2 0.7 %collective-permute-start.5 = (f32[8,152]{1,0:T(8,128)S(1)}, f32[8,152]{1,0:T(8,128)S(1)}, u32[]{:S(2)}, u32[]{:S(2)}) collective-permute-start(f32[8,152]{1,0:T(8,128)S(1)} %get-tuple-element.39), channel_id=1, source_target_pairs={{0,2},{1,3},{2,0},{3,1},{4,6},{5,7},{6,4},{7,5},{8,10},{9,11},{10,... | collective-permute-start | bytes 14600 | tf_op jit(solution)/shard_map/ppermute | solution.py:569
  24.0 1.1 %value.5 = (f32[3,160,2048]{2,1,0:T(8,128)S(1)}, f32[16,8,2048]{2,1,0:T(8,128)S(1)}) custom-call(bf16[256,2048]{1,0:T(8,128)(2,1)S(1)} %get-tuple-element.40.mixed, f32[8,2048]{1,0:T(8,128)S(1)} %get-tuple-element.41.mixed_rim, f32[1,2048]{1,0:T(1,128)S(1)} %bitcast.40, bf16[256,2048]{1,0:T(8,128)(2,1)S(1)} %copy-done, ...), custom_call_target="tpu_custom_call" | custom-call | flops 524288000 | bytes 5242880 | tf_op jit(solution)/shard_map/value/pallas_call | solution.py:704
  25.2 1.7 %collective-permute-done.5 = f32[8,152]{1,0:T(8,128)S(1)} collective-permute-done((f32[8,152]{1,0:T(8,128)S(1)}, f32[8,152]{1,0:T(8,128)S(1)}, u32[]{:S(2)}, u32[]{:S(2)}) %collective-permute-start.5) | collective-permute-done | bytes 4896 | tf_op jit(solution)/shard_map/ppermute | solution.py:569
  26.9 2.1 %state.1 = (bf16[160,2048]{1,0:T(8,128)(2,1)S(1)}, f32[16,2048]{1,0:T(8,128)S(1)}) custom-call(f32[8,152]{1,0:T(8,128)S(1)} %add_add_fusion.refs_0_, f32[8,112]{1,0:T(8,128)S(1)} %add_add_fusion.1.refs_0_.refs_1_, f32[3,160,2048]{2,1,0:T(8,128)S(1)} %get-tuple-element.43.refs_2_, f32[16,8,2048]{2,1,0:T(8,128)S(1)} %get-tuple-element.44.refs_3_, ...), custom_call_target="tpu_custom_call" | custom-call | flops 52428800 | bytes 5242880 | tf_op jit(solution)/shard_map/state/pallas_call | solution.py:710
  29.0 2.6 %collective-permute-start.9 = (bf16[16,2048]{1,0:T(8,128)(2,1)S(1)}, bf16[16,2048]{1,0:T(8,128)(2,1)S(1)}, u32[]{:S(2)}, u32[]{:S(2)}) collective-permute-start(bf16[16,2048]{1,0:T(8,128)(2,1)S(1)} %convert_element_type.18), channel_id=1, source_target_pairs={{0,12},{4,8},{8,4},{12,0},{16,28},{20,24},{24,20},{28,16},{1,13},{... | collective-permute-start | bytes 196616 | tf_op jit(solution)/shard_map/ppermute | solution.py:569
  31.6 0.4 collective-permute-start.8
  32.0 0.7 %collective-permute-start.7 = (bf16[16,2048]{1,0:T(8,128)(2,1)S(1)}, bf16[16,2048]{1,0:T(8,128)(2,1)S(1)}, u32[]{:S(2)}, u32[]{:S(2)}) collective-permute-start(bf16[16,2048]{1,0:T(8,128)(2,1)S(1)} %convert_element_type.18), channel_id=1, source_target_pairs={{0,4},{4,0},{8,12},{12,8},{16,20},{20,16},{24,28},{28,24},{1,5},{5... | collective-permute-start | bytes 196616 | tf_op jit(solution)/shard_map/ppermute | solution.py:569
  32.7 2.2 %local.1 = (f32[256,2048]{1,0:T(8,128)S(1)}, f32[1,2048]{1,0:T(1,128)S(1)}) custom-call(bf16[160,2048]{1,0:T(8,128)(2,1)S(1)} %get-tuple-element.47.early, bf16[96,2048]{1,0:T(8,128)(2,1)S(1)} %get-tuple-element.48.late, f32[2,256,2048]{2,1,0:T(8,128)S(1)} %get-tuple-element.49.long_hat, f32[1,2048]{1,0:T(1,128)S(1)} %bitcast.41, ...), custom_call_target="tpu_custom_call" | custom-call | flops 1048576000 | bytes 7340032 | tf_op jit(solution)/shard_map/local/pallas_call | solution.py:717
  34.9 0.9 %collective-permute-done.8 = bf16[16,2048]{1,0:T(8,128)(2,1)S(1)} collective-permute-done((bf16[16,2048]{1,0:T(8,128)(2,1)S(1)}, bf16[16,2048]{1,0:T(8,128)(2,1)S(1)}, u32[]{:S(2)}, u32[]{:S(2)}) %collective-permute-start.8) | collective-permute-done | bytes 65568 | tf_op jit(solution)/shard_map/ppermute | solution.py:569
  35.9 0.4 collective-permute-done.7
  36.3 0.1 fusion.8
  36.4 2.7 %collective-permute-start.10 = (bf16[16,2048]{1,0:T(8,128)(2,1)S(1)}, bf16[16,2048]{1,0:T(8,128)(2,1)S(1)}, u32[]{:S(2)}, u32[]{:S(2)}) collective-permute-start(bf16[16,2048]{1,0:T(8,128)(2,1)S(1)} %get-tuple-element.56._), channel_id=1, source_target_pairs={{0,16},{4,20},{8,24},{12,28},{16,0},{20,4},{24,8},{28,12},{1,17},{... | collective-permute-start | bytes 196616 | tf_op jit(solution)/shard_map/ppermute | solution.py:569
  39.1 4.7 %near.1 = (f32[256,2048]{1,0:T(8,128)S(1)}, f32[256,2048]{1,0:T(8,128)S(1)}, bf16[256,2048]{1,0:T(8,128)(2,1)}, bf16[256,2048]{1,0:T(8,128)(2,1)}) custom-call(f32[16,2048]{1,0:T(8,128)S(1)} %get-tuple-element.58.state, f32[16,8,2048]{2,1,0:T(8,128)S(1)} %get-tuple-element.36.refs_5_.refs_4_.decays.refs_2_, ...), custom_call_target="tpu_custom_call" | custom-call | flops 524288000 | bytes 7340032 | tf_op jit(solution)/shard_map/near/pallas_call | solution.py:722
  (48 shorter events, 0.3 us)
Async XLA Ops:
  0.6 7.2 %copy-start.2 = (bf16[256,2048]{1,0:T(8,128)(2,1)S(1)}, bf16[256,2048]{1,0:T(8,128)(2,1)}, u32[]{:S(2)}) copy-start(bf16[256,2048]{1,0:T(8,128)(2,1)} %key.3) | copy-start | bytes 3145732
  0.6 7.2 %copy-start.3 = (bf16[256,2048]{1,0:T(8,128)(2,1)S(1)}, bf16[256,2048]{1,0:T(8,128)(2,1)}, u32[]{:S(2)}) copy-start(bf16[256,2048]{1,0:T(8,128)(2,1)} %value.4) | copy-start | bytes 3145732
  0.7 7.2 %copy-start.4 = (bf16[256,2048]{1,0:T(8,128)(2,1)S(1)}, bf16[256,2048]{1,0:T(8,128)(2,1)}, u32[]{:S(2)}) copy-start(bf16[256,2048]{1,0:T(8,128)(2,1)} %gate.3) | copy-start | bytes 3145732
  0.7 7.2 %copy-start.5 = (bf16[256,256]{1,0:T(8,128)(2,1)S(1)}, bf16[256,256]{1,0:T(8,128)(2,1)}, u32[]{:S(2)}) copy-start(bf16[256,256]{1,0:T(8,128)(2,1)} %constant.16.clone.exact_rows.refs_3_) | copy-start | bytes 393220
  0.7 7.2 %copy-start.6 = (f32[128,2048]{1,0:T(8,128)S(1)}, f32[128,2048]{1,0:T(8,128)}, u32[]{:S(2)}) copy-start(f32[128,2048]{1,0:T(8,128)} %taps.1) | copy-start | bytes 3145732
  0.7 7.2 %copy-start.8 = (f32[3,3,2048]{2,1,0:T(4,128)S(1)}, f32[3,3,2048]{2,1,0:T(4,128)}, u32[]{:S(2)}) copy-start(f32[3,3,2048]{2,1,0:T(4,128)} %short.7) | copy-start | bytes 221188
  0.7 7.2 %copy-start.10 = (bf16[256,256]{1,0:T(8,128)(2,1)S(1)}, bf16[256,256]{1,0:T(8,128)(2,1)}, u32[]{:S(2)}) copy-start(bf16[256,256]{1,0:T(8,128)(2,1)} %constant.18.clone.backward) | copy-start | bytes 393220
  0.7 7.2 %copy-start.11 = (bf16[256,384]{1,0:T(8,128)(2,1)S(1)}, bf16[256,384]{1,0:T(8,128)(2,1)}, u32[]{:S(2)}) copy-start(bf16[256,384]{1,0:T(8,128)(2,1)} %constant.17.clone.split_rows) | copy-start | bytes 589828
  0.7 7.2 %copy-start.13 = (f32[2048]{0:T(1024)S(1)}, f32[2048]{0:T(1024)}, u32[]{:S(2)}) copy-start(f32[2048]{0:T(1024)} %param.22) | copy-start | bytes 24580
  2.9 17.7 %collective-permute-start = (bf16[144,2048]{1,0:T(8,128)(2,1)S(1)}, bf16[144,2048]{1,0:T(8,128)(2,1)S(1)}, u32[]{:S(2)}, u32[]{:S(2)}) collective-permute-start(bf16[144,2048]{1,0:T(8,128)(2,1)S(1)} %pack.1._), channel_id=1, source_target_pairs={{0,4},{4,8},{8,12},{12,16},{16,20},{20,24},{24,28},{1,5},{5,9},{9,... | collective-permute-start | bytes 1769480 | tf_op jit(solution)/shard_map/ppermute | solution.py:564
  7.9 6.7 %copy-start.9 = (f32[16,2048]{1,0:T(8,128)S(1)}, f32[16,2048]{1,0:T(8,128)}, u32[]{:S(2)}) copy-start(f32[16,2048]{1,0:T(8,128)} %rates.1) | copy-start | bytes 393220
  7.9 6.7 %copy-start.16 = (f32[16,2048]{1,0:T(8,128)S(1)}, f32[16,2048]{1,0:T(8,128)}, u32[]{:S(2)}) copy-start(f32[16,2048]{1,0:T(8,128)} %param.28) | copy-start | bytes 393220
  12.7 6.0 %copy-start.7 = (f32[3,3,2048]{2,1,0:T(4,128)S(1)}, f32[3,3,2048]{2,1,0:T(4,128)}, u32[]{:S(2)}) copy-start(f32[3,3,2048]{2,1,0:T(4,128)} %short.9) | copy-start | bytes 221188
  12.7 6.1 %copy-start.14 = (f32[2048]{0:T(1024)S(1)}, f32[2048]{0:T(1024)}, u32[]{:S(2)}) copy-start(f32[2048]{0:T(1024)} %param.23) | copy-start | bytes 24580
  12.7 6.0 %collective-permute-start.3 = (f32[8,112]{1,0:T(8,128)S(1)}, f32[8,112]{1,0:T(8,128)S(1)}, u32[]{:S(2)}, u32[]{:S(2)}) collective-permute-start(f32[8,112]{1,0:T(8,128)S(1)} %get-tuple-element.29.refs_4_), channel_id=1, source_target_pairs={{0,3},{1,2},{2,1},{3,0},{4,7},{5,6},{6,5},{7,4},{8,11},{9,10},{10,... | collective-permute-start | bytes 10760 | tf_op jit(solution)/shard_map/ppermute | solution.py:569
  13.4 5.3 %collective-permute-start.2 = (f32[8,112]{1,0:T(8,128)S(1)}, f32[8,112]{1,0:T(8,128)S(1)}, u32[]{:S(2)}, u32[]{:S(2)}) collective-permute-start(f32[8,112]{1,0:T(8,128)S(1)} %get-tuple-element.29.refs_4_), channel_id=1, source_target_pairs={{0,2},{1,3},{2,0},{3,1},{4,6},{5,7},{6,4},{7,5},{8,10},{9,11},{10,... | collective-permute-start | bytes 10760 | tf_op jit(solution)/shard_map/ppermute | solution.py:569
  14.3 4.4 %collective-permute-start.1 = (f32[8,112]{1,0:T(8,128)S(1)}, f32[8,112]{1,0:T(8,128)S(1)}, u32[]{:S(2)}, u32[]{:S(2)}) collective-permute-start(f32[8,112]{1,0:T(8,128)S(1)} %get-tuple-element.29.refs_4_), channel_id=1, source_target_pairs={{0,1},{1,0},{2,3},{3,2},{4,5},{5,4},{6,7},{7,6},{8,9},{9,8},{10,11... | collective-permute-start | bytes 10760 | tf_op jit(solution)/shard_map/ppermute | solution.py:569
  22.1 3.1 %collective-permute-start.6 = (f32[8,152]{1,0:T(8,128)S(1)}, f32[8,152]{1,0:T(8,128)S(1)}, u32[]{:S(2)}, u32[]{:S(2)}) collective-permute-start(f32[8,152]{1,0:T(8,128)S(1)} %get-tuple-element.39), channel_id=1, source_target_pairs={{0,3},{1,2},{2,1},{3,0},{4,7},{5,6},{6,5},{7,4},{8,11},{9,10},{10,... | collective-permute-start | bytes 14600 | tf_op jit(solution)/shard_map/ppermute | solution.py:569
  23.2 3.7 %collective-permute-start.5 = (f32[8,152]{1,0:T(8,128)S(1)}, f32[8,152]{1,0:T(8,128)S(1)}, u32[]{:S(2)}, u32[]{:S(2)}) collective-permute-start(f32[8,152]{1,0:T(8,128)S(1)} %get-tuple-element.39), channel_id=1, source_target_pairs={{0,2},{1,3},{2,0},{3,1},{4,6},{5,7},{6,4},{7,5},{8,10},{9,11},{10,... | collective-permute-start | bytes 14600 | tf_op jit(solution)/shard_map/ppermute | solution.py:569
  23.9 2.9 %collective-permute-start.4 = (f32[8,152]{1,0:T(8,128)S(1)}, f32[8,152]{1,0:T(8,128)S(1)}, u32[]{:S(2)}, u32[]{:S(2)}) collective-permute-start(f32[8,152]{1,0:T(8,128)S(1)} %get-tuple-element.39), channel_id=1, source_target_pairs={{0,1},{1,0},{2,3},{3,2},{4,5},{5,4},{6,7},{7,6},{8,9},{9,8},{10,11... | collective-permute-start | bytes 14600 | tf_op jit(solution)/shard_map/ppermute | solution.py:569
  29.0 5.9 %collective-permute-start.9 = (bf16[16,2048]{1,0:T(8,128)(2,1)S(1)}, bf16[16,2048]{1,0:T(8,128)(2,1)S(1)}, u32[]{:S(2)}, u32[]{:S(2)}) collective-permute-start(bf16[16,2048]{1,0:T(8,128)(2,1)S(1)} %convert_element_type.18), channel_id=1, source_target_pairs={{0,12},{4,8},{8,4},{12,0},{16,28},{20,24},{24,20},{28,16},{1,13},{... | collective-permute-start | bytes 196616 | tf_op jit(solution)/shard_map/ppermute | solution.py:569
  31.6 4.3 %collective-permute-start.8 = (bf16[16,2048]{1,0:T(8,128)(2,1)S(1)}, bf16[16,2048]{1,0:T(8,128)(2,1)S(1)}, u32[]{:S(2)}, u32[]{:S(2)}) collective-permute-start(bf16[16,2048]{1,0:T(8,128)(2,1)S(1)} %convert_element_type.18), channel_id=1, source_target_pairs={{0,8},{4,12},{8,0},{12,4},{16,24},{20,28},{24,16},{28,20},{1,9},{5... | collective-permute-start | bytes 196616 | tf_op jit(solution)/shard_map/ppermute | solution.py:569
  32.0 4.3 %collective-permute-start.7 = (bf16[16,2048]{1,0:T(8,128)(2,1)S(1)}, bf16[16,2048]{1,0:T(8,128)(2,1)S(1)}, u32[]{:S(2)}, u32[]{:S(2)}) collective-permute-start(bf16[16,2048]{1,0:T(8,128)(2,1)S(1)} %convert_element_type.18), channel_id=1, source_target_pairs={{0,4},{4,0},{8,12},{12,8},{16,20},{20,16},{24,28},{28,24},{1,5},{5... | collective-permute-start | bytes 196616 | tf_op jit(solution)/shard_map/ppermute | solution.py:569
  36.4 7.5 %collective-permute-start.10 = (bf16[16,2048]{1,0:T(8,128)(2,1)S(1)}, bf16[16,2048]{1,0:T(8,128)(2,1)S(1)}, u32[]{:S(2)}, u32[]{:S(2)}) collective-permute-start(bf16[16,2048]{1,0:T(8,128)(2,1)S(1)} %get-tuple-element.56._), channel_id=1, source_target_pairs={{0,16},{4,20},{8,24},{12,28},{16,0},{20,4},{24,8},{28,12},{1,17},{... | collective-permute-start | bytes 196616 | tf_op jit(solution)/shard_map/ppermute | solution.py:569
  (4 other events, 18.0 us)

commit v4 on v3

--- a/solution.py
+++ b/solution.py
@@ -351,11 +351,13 @@
 
 
 def late_kernel(
-    all_width, squares, mixed_late, key_long, gain, short, decays, tails, product_out, state
+    all_width, squares, mixed_late, key_long, gain, short, decays, tails,
+    product_out, state, late_factors,
 ):
     rows, width = key_long.shape
     modes = decays.shape[0]
     factors = norm_factors(squares[...], all_width)
+    late_factors[...] = factors
 
     def step(here, base):
         for lanes in lane_tiles(base):
@@ -375,7 +377,8 @@
 
 
 def value_kernel(
-    mixed, mixed_rim, gain, key_long, rim_long, short, rates, tails, parts, tails_far
+    mixed, mixed_rim, gain, key_long, gate_long, rim_long, short, rates, tails,
+    parts, tails_far, gate_feat,
 ):
     rows, width = mixed.shape
     modes = rates.shape[0]
@@ -388,6 +391,10 @@
             ),
             short[1, :, here],
         )[TILE:]
+        gates = jnp.concatenate(
+            [pltpu.roll(rim_long[:, here], 6, 0), gate_long[:, here].astype(F32)], 0
+        )
+        gate_feat[:, here] = shifted_filter(gates, short[0, :, here])[TILE:]
         weights = short[2, :, here] * gain[:, here]
         for j in range(3):
             moved = frame if j == 0 else pltpu.roll(frame, j, 0)
@@ -401,14 +408,14 @@
 
 
 def state_kernel(
-    all_width, squares, squares_late, parts, tails_far, decays, state_late,
+    all_width, squares, late_factors, parts, tails_far, decays, state_late,
     product_out, state, factors,
 ):
     width = product_out.shape[1]
     modes = decays.shape[0]
     inverse = norm_factors(squares[...], all_width)
     inverse = jnp.concatenate(
-        [inverse, norm_factors(squares_late[...], all_width)[: TURN - EARLY]], 0
+        [inverse, late_factors[: TURN - EARLY]], 0
     )
     factors[0] = inverse[TILE:]
     factors[1] = pltpu.roll(inverse, 1, 0)[TILE:]
@@ -465,18 +472,14 @@
 
 
 def near_kernel(
-    state, decays, leads, local, gate_long, rim_long, short, mixed, _,
-    near, gate_feat, mixed_out, out, held_out, sent,
+    state, decays, leads, local, gate_feat, mixed, _,
+    near, mixed_out, out, held_out, sent,
 ):
     rows, width = local.shape
     copies = [pltpu.make_async_copy(mixed, mixed_out, sent.at[width // WIDTH])]
     copies[0].start()
 
     def step(here, base):
-        gates = jnp.concatenate(
-            [pltpu.roll(rim_long[:, here], 6, 0), gate_long[:, here].astype(F32)], 0
-        )
-        gate_feat[:, here] = shifted_filter(gates, short[0, :, here])[TILE:]
         for lanes in lane_tiles(base):
 
             held = []
@@ -681,9 +684,12 @@
     )(place, decay_rates, mode_weight, exact_rows, squares_late)
 
     total_late = sum_over(squares_late, "ch")
-    product_late, state_late = call(
+    product_late, state_late, late_factors = call(
         lambda *refs: late_kernel(all_width, *refs), "late", [KEPT] * 7,
-        [arr((rows - TURN, width), BF16), arr((modes, width), F32)],
+        [
+            arr((rows - TURN, width), BF16), arr((modes, width), F32),
+            arr((rows - EARLY, LANES), F32),
+        ],
         flops=100 * rows * width, moved=10 * rows * width,
     )(total_late, mixed_late, key_long, norm_gain[None], short_long, decays, tails)
 
@@ -701,34 +707,35 @@
     )
 
     total_squares = sum_over(squares, "ch")
-    long_parts, tails_far = call(
-        value_kernel, "value", [KEPT] * 8, [arr((3, TURN, width), F32), table],
+    long_parts, tails_far, gate_feat = call(
+        value_kernel, "value", [KEPT] * 9,
+        [arr((3, TURN, width), F32), table, arr((rows, width), F32)],
         flops=1000 * rows * width, moved=10 * rows * width,
     )(
-        mixed_medium, mixed_rim, norm_gain[None], key_long, rim_long, short_long, decay_rates, tails
+        mixed_medium, mixed_rim, norm_gain[None], key_long, gate_long, rim_long, short_long,
+        decay_rates, tails,
     )
     product_early, state = call(
         lambda *refs: state_kernel(all_width, *refs), "state", [KEPT] * 6,
         [arr((TURN, width), BF16), arr((modes, width), F32)],
         [pltpu.VMEM((3, TURN, LANES), F32)],
         flops=100 * rows * width, moved=10 * rows * width,
-    )(total_squares, total_late, long_parts, tails_far, decays, state_late)
+    )(total_squares, late_factors, long_parts, tails_far, decays, state_late)
 
     local, done = call(
         local_kernel, "local", [KEPT] * 6, [arr((rows, width), F32), arr((1, width), F32)],
         flops=2000 * rows * width, moved=14 * rows * width,
     )(product_early, product_late, long_hat, skip_long[None], exact_rows, backward)
     known, incoming, last_sent = carried_state(state, carry, done)
-    near, gate_feat, mixed_out, mixed_long = call(
-        near_kernel, "near", [KEPT] * 9,
+    near, mixed_out, mixed_long = call(
+        near_kernel, "near", [KEPT] * 7,
         [
-            arr((rows, width), F32), arr((rows, width), F32), arr((rows, width), BF16),
-            arr((rows, width), BF16),
+            arr((rows, width), F32), arr((rows, width), BF16), arr((rows, width), BF16),
         ],
         [pltpu.VMEM((rows, width), BF16), pltpu.SemaphoreType.DMA((width // WIDTH + 1,))],
-        out_specs=[KEPT, KEPT, FAR, FAR],
+        out_specs=[KEPT, FAR, FAR],
         flops=1000 * rows * width, moved=14 * rows * width,
-    )(known, decays, leads, local, gate_long, rim_long, short_long, mixed_medium, last_sent)
+    )(known, decays, leads, local, gate_feat, mixed_medium, last_sent)
     mixed_long = call(
         lambda *refs: finish_kernel(count, *refs), "finish", [SCALAR] + [KEPT] * 5 + [FAR],
         arr((rows, width), BF16),

time: 44.3 us -> 44.5 us (level)
  the two profiles are of different devices: /device:TPU:0 before, /device:TPU:24 now
where the time goes in v4:
time: 44.5 us; the launch traced here: 44.4 us
  Pallas kernels  27.7 us (62%)
  starting transfers between devices  11.2 us (25%)
  waiting for transfers between devices  3.88 us (9%)
  between operations  1.18 us (3%)
    ppermute x10, starting transfers between devices, exchanged(): lax.ppermute(value, axis, [(source, source ^ flip) for source in range(co...  7.81 us
    pallas_call x1, Pallas kernels, body(): call(own_kernel, 'own', [KEPT] * 10, [arr((EARLY, width), F32), arr((EARL...  4.83 us
    pallas_call x1, Pallas kernels, body(): call(lambda *refs: impulse_kernel(count, *refs), 'impulse', [SCALAR] + [K...  4 us
    pallas_call x1, Pallas kernels, body(): call(near_kernel, 'near', [KEPT] * 7, [arr((rows, width), F32), arr((rows...  3.74 us
    ppermute x1, starting transfers between devices, passed_along(): lax.ppermute(value, axis, [(source, source + steps) for source in range(c...  3.43 us
    pallas_call x1, Pallas kernels, body(): call(lambda *refs: finish_kernel(count, *refs), 'finish', [SCALAR] + [KEP...  3.13 us
    pallas_call x1, Pallas kernels, body(): call(local_kernel, 'local', [KEPT] * 6, [arr((rows, width), F32), arr((1,...  2.43 us
    ppermute x10, waiting for transfers between devices, exchanged(): lax.ppermute(value, axis, [(source, source ^ flip) for source in range(co...  2.32 us
  transfers between devices with their start and end apart: 11, of which 3 were waited for; matrix products, arithmetic and copies ran while one was open for 0% of the time, Pallas kernels for 42%

profile of v4, /device:TPU:24, one launch (start us, length us, event | category | flops | bytes accessed | tf_op | source)
XLA Modules:
  0.0 44.4 jit_solution(5354113146741205958)
XLA Ops:
  0.7 2.2 %pack.1._ = bf16[144,2048]{1,0:T(8,128)(2,1)S(1)} custom-call(s32[1]{0:T(128)} %bitcast._.refs_0_, bf16[256,2048]{1,0:T(8,128)(2,1)} %key.3, bf16[256,2048]{1,0:T(8,128)(2,1)} %value.4, bf16[256,2048]{1,0:T(8,128)(2,1)} %gate.3, bf16[256,2048]{1,0:T(8,128)(2,1)} %gate_long.3, bf16[256,2048]{1,0:T(8,128)(2,1)} %key_long.3, f32[3,3,2048]{2,1,0:T(4,128)} %short.6), custom_call_target="tpu_custom_call" | custom-call | tf_op jit(solution)/shard_map/pack/pallas_call | solution.py:648
  2.9 3.4 %collective-permute-start = (bf16[144,2048]{1,0:T(8,128)(2,1)S(1)}, bf16[144,2048]{1,0:T(8,128)(2,1)S(1)}, u32[]{:S(2)}, u32[]{:S(2)}) collective-permute-start(bf16[144,2048]{1,0:T(8,128)(2,1)S(1)} %pack.1._), channel_id=1, source_target_pairs={{0,4},{4,8},{8,12},{12,16},{16,20},{20,24},{24,28},{1,5},{5,9},{9,... | collective-permute-start | bytes 1769480 | tf_op jit(solution)/shard_map/ppermute | solution.py:567
  6.5 4.8 %own.1 = (f32[144,2048]{1,0:T(8,128)S(1)}, f32[144,2048]{1,0:T(8,128)S(1)}, bf16[112,2048]{1,0:T(8,128)(2,1)S(1)}, f32[8,112]{1,0:T(8,128)S(1)}, f32[256,2048]{1,0:T(8,128)S(1)}, /*index=5*/f32[32,2048]{1,0:T(8,128)S(1)}) custom-call(bf16[256,2048]{1,0:T(8,128)(2,1)S(1)} %copy-done.4, bf16[256,2048]{1,0:T(8,128)(2,1)S(1)} %copy-done.2, ...), custom_call_target="tpu_custom_call" | custom-call | flops 1048576000 | bytes 5242880 | tf_op jit(solution)/shard_map/own/pallas_call | solution.py:660
  11.3 0.7 %collective-permute-start.3 = (f32[8,112]{1,0:T(8,128)S(1)}, f32[8,112]{1,0:T(8,128)S(1)}, u32[]{:S(2)}, u32[]{:S(2)}) collective-permute-start(f32[8,112]{1,0:T(8,128)S(1)} %get-tuple-element.30.refs_4_), channel_id=1, source_target_pairs={{0,3},{1,2},{2,1},{3,0},{4,7},{5,6},{6,5},{7,4},{8,11},{9,10},{10,... | collective-permute-start | bytes 10760 | tf_op jit(solution)/shard_map/ppermute | solution.py:572
  12.0 0.9 %collective-permute-start.2 = (f32[8,112]{1,0:T(8,128)S(1)}, f32[8,112]{1,0:T(8,128)S(1)}, u32[]{:S(2)}, u32[]{:S(2)}) collective-permute-start(f32[8,112]{1,0:T(8,128)S(1)} %get-tuple-element.30.refs_4_), channel_id=1, source_target_pairs={{0,2},{1,3},{2,0},{3,1},{4,6},{5,7},{6,4},{7,5},{8,10},{9,11},{10,... | collective-permute-start | bytes 10760 | tf_op jit(solution)/shard_map/ppermute | solution.py:572
  12.9 0.3 collective-permute-start.1
  13.3 4.0 %impulse.1 = (f32[2,256,2048]{2,1,0:T(8,128)S(1)}, f32[12,16,2048]{2,1,0:T(8,128)S(1)}, f32[16,8,2048]{2,1,0:T(8,128)S(1)}, f32[16,8,2048]{2,1,0:T(8,128)S(1)}, f32[16,8,2048]{2,1,0:T(8,128)S(1)}) custom-call(s32[1]{0:T(128)} %bitcast._.refs_0_, f32[16,2048]{1,0:T(8,128)S(1)} %copy-done.8, f32[16,2048]{1,0:T(8,128)S(1)} %sqrt_multiply_fusion.refs_2_, ...), custom_call_target="tpu_custom_call" | custom-call | flops 1048576000 | bytes 5242880 | tf_op jit(solution)/shard_map/impulse/pallas_call | solution.py:675
  17.4 1.8 %late.1 = (bf16[96,2048]{1,0:T(8,128)(2,1)S(1)}, f32[16,2048]{1,0:T(8,128)S(1)}, f32[112,128]{1,0:T(8,128)S(1)}) custom-call(f32[8,112]{1,0:T(8,128)S(1)} %add_add_fusion.1.refs_0_, bf16[112,2048]{1,0:T(8,128)(2,1)S(1)} %get-tuple-element.36.refs_1_.mixed_late, bf16[256,2048]{1,0:T(8,128)(2,1)S(1)} %copy-done, f32[1,2048]{1,0:T(1,128)S(1)} %bitcast.39, ...), custom_call_target="tpu_custom_call" | custom-call | flops 52428800 | bytes 5242880 | tf_op jit(solution)/shard_map/late/pallas_call | solution.py:687
  19.2 1.6 %collective-permute-done.halo = bf16[144,2048]{1,0:T(8,128)(2,1)S(1)} collective-permute-done((bf16[144,2048]{1,0:T(8,128)(2,1)S(1)}, bf16[144,2048]{1,0:T(8,128)(2,1)S(1)}, u32[]{:S(2)}, u32[]{:S(2)}) %collective-permute-start) | collective-permute-done | bytes 589856 | tf_op jit(solution)/shard_map/ppermute | solution.py:567
  20.8 1.5 %medium.1 = (bf16[256,2048]{1,0:T(8,128)(2,1)S(1)}, f32[8,2048]{1,0:T(8,128)S(1)}, f32[8,152]{1,0:T(8,128)S(1)}, f32[8,2048]{1,0:T(8,128)S(1)}) custom-call(bf16[144,2048]{1,0:T(8,128)(2,1)S(1)} %collective-permute-done.halo, f32[32,2048]{1,0:T(8,128)S(1)} %get-tuple-element.32.heads, f32[3,3,2048]{2,1,0:T(4,128)S(1)} %copy-done.7, f32[1,2048]{1,0:T(1,128)S(1)} %bitcast.38, ...), custom_call_target="tpu_custom_call" | custom-call | flops 524288000 | bytes 5242880 | tf_op jit(solution)/shard_map/medium/pallas_call | solution.py:696
  22.4 1.5 %collective-permute-start.5 = (f32[8,152]{1,0:T(8,128)S(1)}, f32[8,152]{1,0:T(8,128)S(1)}, u32[]{:S(2)}, u32[]{:S(2)}) collective-permute-start(f32[8,152]{1,0:T(8,128)S(1)} %get-tuple-element.40), channel_id=1, source_target_pairs={{0,2},{1,3},{2,0},{3,1},{4,6},{5,7},{6,4},{7,5},{8,10},{9,11},{10,... | collective-permute-start | bytes 14600 | tf_op jit(solution)/shard_map/ppermute | solution.py:572
  23.9 0.3 collective-permute-start.4
  24.2 1.9 %value.5 = (f32[3,160,2048]{2,1,0:T(8,128)S(1)}, f32[16,8,2048]{2,1,0:T(8,128)S(1)}, f32[256,2048]{1,0:T(8,128)S(1)}) custom-call(bf16[256,2048]{1,0:T(8,128)(2,1)S(1)} %get-tuple-element.42.mixed, f32[8,2048]{1,0:T(8,128)S(1)} %get-tuple-element.43.mixed_rim, f32[1,2048]{1,0:T(1,128)S(1)} %bitcast.40, bf16[256,2048]{1,0:T(8,128)(2,1)S(1)} %copy-done, ...), custom_call_target="tpu_custom_call" | custom-call | flops 524288000 | bytes 5242880 | tf_op jit(solution)/shard_map/value/pallas_call | solution.py:710
  26.2 2.2 %state.1 = (bf16[160,2048]{1,0:T(8,128)(2,1)S(1)}, f32[16,2048]{1,0:T(8,128)S(1)}) custom-call(f32[8,152]{1,0:T(8,128)S(1)} %add_add_fusion.refs_0_, f32[112,128]{1,0:T(8,128)S(1)} %get-tuple-element.41.refs_1_, f32[3,160,2048]{2,1,0:T(8,128)S(1)} %get-tuple-element.45.refs_2_, f32[16,8,2048]{2,1,0:T(8,128)S(1)} %get-tuple-element.46.refs_3_, ...), custom_call_target="tpu_custom_call" | custom-call | flops 52428800 | bytes 5242880 | tf_op jit(solution)/shard_map/state/pallas_call | solution.py:718
  28.4 0.9 %collective-permute-start.9 = (bf16[16,2048]{1,0:T(8,128)(2,1)S(1)}, bf16[16,2048]{1,0:T(8,128)(2,1)S(1)}, u32[]{:S(2)}, u32[]{:S(2)}) collective-permute-start(bf16[16,2048]{1,0:T(8,128)(2,1)S(1)} %convert_element_type.18), channel_id=1, source_target_pairs={{0,12},{4,8},{8,4},{12,0},{16,28},{20,24},{24,20},{28,16},{1,13},{... | collective-permute-start | bytes 196616 | tf_op jit(solution)/shard_map/ppermute | solution.py:572
  29.2 1.3 %collective-permute-start.8 = (bf16[16,2048]{1,0:T(8,128)(2,1)S(1)}, bf16[16,2048]{1,0:T(8,128)(2,1)S(1)}, u32[]{:S(2)}, u32[]{:S(2)}) collective-permute-start(bf16[16,2048]{1,0:T(8,128)(2,1)S(1)} %convert_element_type.18), channel_id=1, source_target_pairs={{0,8},{4,12},{8,0},{12,4},{16,24},{20,28},{24,16},{28,20},{1,9},{5... | collective-permute-start | bytes 196616 | tf_op jit(solution)/shard_map/ppermute | solution.py:572
  30.5 1.4 %collective-permute-start.7 = (bf16[16,2048]{1,0:T(8,128)(2,1)S(1)}, bf16[16,2048]{1,0:T(8,128)(2,1)S(1)}, u32[]{:S(2)}, u32[]{:S(2)}) collective-permute-start(bf16[16,2048]{1,0:T(8,128)(2,1)S(1)} %convert_element_type.18), channel_id=1, source_target_pairs={{0,4},{4,0},{8,12},{12,8},{16,20},{20,16},{24,28},{28,24},{1,5},{5... | collective-permute-start | bytes 196616 | tf_op jit(solution)/shard_map/ppermute | solution.py:572
  31.9 2.4 %local.1 = (f32[256,2048]{1,0:T(8,128)S(1)}, f32[1,2048]{1,0:T(1,128)S(1)}) custom-call(bf16[160,2048]{1,0:T(8,128)(2,1)S(1)} %get-tuple-element.49.early, bf16[96,2048]{1,0:T(8,128)(2,1)S(1)} %get-tuple-element.50.late, f32[2,256,2048]{2,1,0:T(8,128)S(1)} %get-tuple-element.51.long_hat, f32[1,2048]{1,0:T(1,128)S(1)} %bitcast.41, ...), custom_call_target="tpu_custom_call" | custom-call | flops 1048576000 | bytes 7340032 | tf_op jit(solution)/shard_map/local/pallas_call | solution.py:725
  34.4 0.6 %collective-permute-done.7 = bf16[16,2048]{1,0:T(8,128)(2,1)S(1)} collective-permute-done((bf16[16,2048]{1,0:T(8,128)(2,1)S(1)}, bf16[16,2048]{1,0:T(8,128)(2,1)S(1)}, u32[]{:S(2)}, u32[]{:S(2)}) %collective-permute-start.7) | collective-permute-done | bytes 65568 | tf_op jit(solution)/shard_map/ppermute | solution.py:572
  35.0 0.1 fusion.8
  35.1 0.5 %collective-permute-start.10 = (bf16[16,2048]{1,0:T(8,128)(2,1)S(1)}, bf16[16,2048]{1,0:T(8,128)(2,1)S(1)}, u32[]{:S(2)}, u32[]{:S(2)}) collective-permute-start(bf16[16,2048]{1,0:T(8,128)(2,1)S(1)} %get-tuple-element.58._), channel_id=1, source_target_pairs={{0,16},{4,20},{8,24},{12,28},{16,0},{20,4},{24,8},{28,12},{1,17},{... | collective-permute-start | bytes 196616 | tf_op jit(solution)/shard_map/ppermute | solution.py:572
  35.6 3.7 %near.1 = (f32[256,2048]{1,0:T(8,128)S(1)}, bf16[256,2048]{1,0:T(8,128)(2,1)}, bf16[256,2048]{1,0:T(8,128)(2,1)}) custom-call(f32[16,2048]{1,0:T(8,128)S(1)} %get-tuple-element.60.state, f32[16,8,2048]{2,1,0:T(8,128)S(1)} %get-tuple-element.37.refs_5_.refs_4_.decays.refs_2_, f32[16,8,2048]{2,1,0:T(8,128)S(1)} %get-tuple-element.48.leads.refs_3_, ...), custom_call_target="tpu_custom_call" | custom-call | flops 524288000 | bytes 7340032 | tf_op jit(solution)/shard_map/near/pallas_call | solution.py:730
  39.3 1.7 %collective-permute-done.10 = bf16[16,2048]{1,0:T(8,128)(2,1)S(1)} collective-permute-done((bf16[16,2048]{1,0:T(8,128)(2,1)S(1)}, bf16[16,2048]{1,0:T(8,128)(2,1)S(1)}, u32[]{:S(2)}, u32[]{:S(2)}) %collective-permute-start.10) | collective-permute-done | bytes 65568 | tf_op jit(solution)/shard_map/ppermute | solution.py:572
  41.0 3.1 %finish.1 = bf16[256,2048]{1,0:T(8,128)(2,1)} custom-call(s32[1]{0:T(128)} %bitcast._.refs_0_, f32[16,2048]{1,0:T(8,128)S(1)} %fusion.7.refs_1_, f32[16,8,2048]{2,1,0:T(8,128)S(1)} %get-tuple-element.37.refs_5_.refs_4_.decays.refs_2_, f32[16,8,2048]{2,1,0:T(8,128)S(1)} %get-tuple-element.48.leads.refs_3_, ...), custom_call_target="tpu_custom_call", output_to_operand_aliasing={{}: (6, {})} | custom-call | flops 52428800 | bytes 4194304 | tf_op jit(solution)/shard_map/finish/pallas_call | solution.py:739
  (48 shorter events, 0.3 us)
Async XLA Ops:
  0.6 5.7 %copy-start.2 = (bf16[256,2048]{1,0:T(8,128)(2,1)S(1)}, bf16[256,2048]{1,0:T(8,128)(2,1)}, u32[]{:S(2)}) copy-start(bf16[256,2048]{1,0:T(8,128)(2,1)} %key.3) | copy-start | bytes 3145732
  0.6 5.7 %copy-start.3 = (bf16[256,2048]{1,0:T(8,128)(2,1)S(1)}, bf16[256,2048]{1,0:T(8,128)(2,1)}, u32[]{:S(2)}) copy-start(bf16[256,2048]{1,0:T(8,128)(2,1)} %value.4) | copy-start | bytes 3145732
  0.7 5.7 %copy-start.4 = (bf16[256,2048]{1,0:T(8,128)(2,1)S(1)}, bf16[256,2048]{1,0:T(8,128)(2,1)}, u32[]{:S(2)}) copy-start(bf16[256,2048]{1,0:T(8,128)(2,1)} %gate.3) | copy-start | bytes 3145732
  0.7 5.7 %copy-start.5 = (bf16[256,256]{1,0:T(8,128)(2,1)S(1)}, bf16[256,256]{1,0:T(8,128)(2,1)}, u32[]{:S(2)}) copy-start(bf16[256,256]{1,0:T(8,128)(2,1)} %constant.16.clone.exact_rows.refs_3_) | copy-start | bytes 393220
  0.7 5.7 %copy-start.6 = (f32[128,2048]{1,0:T(8,128)S(1)}, f32[128,2048]{1,0:T(8,128)}, u32[]{:S(2)}) copy-start(f32[128,2048]{1,0:T(8,128)} %taps.1) | copy-start | bytes 3145732
  0.7 5.7 %copy-start.7 = (f32[3,3,2048]{2,1,0:T(4,128)S(1)}, f32[3,3,2048]{2,1,0:T(4,128)}, u32[]{:S(2)}) copy-start(f32[3,3,2048]{2,1,0:T(4,128)} %short.6) | copy-start | bytes 221188
  0.7 5.7 %copy-start.9 = (bf16[256,256]{1,0:T(8,128)(2,1)S(1)}, bf16[256,256]{1,0:T(8,128)(2,1)}, u32[]{:S(2)}) copy-start(bf16[256,256]{1,0:T(8,128)(2,1)} %constant.18.clone.backward) | copy-start | bytes 393220
  2.9 17.9 %collective-permute-start = (bf16[144,2048]{1,0:T(8,128)(2,1)S(1)}, bf16[144,2048]{1,0:T(8,128)(2,1)S(1)}, u32[]{:S(2)}, u32[]{:S(2)}) collective-permute-start(bf16[144,2048]{1,0:T(8,128)(2,1)S(1)} %pack.1._), channel_id=1, source_target_pairs={{0,4},{4,8},{8,12},{12,16},{16,20},{20,24},{24,28},{1,5},{5,9},{9,... | collective-permute-start | bytes 1769480 | tf_op jit(solution)/shard_map/ppermute | solution.py:567
  6.4 6.8 %copy-start.8 = (f32[16,2048]{1,0:T(8,128)S(1)}, f32[16,2048]{1,0:T(8,128)}, u32[]{:S(2)}) copy-start(f32[16,2048]{1,0:T(8,128)} %rates.1) | copy-start | bytes 393220
  6.5 6.7 %copy-start.16 = (f32[16,2048]{1,0:T(8,128)S(1)}, f32[16,2048]{1,0:T(8,128)}, u32[]{:S(2)}) copy-start(f32[16,2048]{1,0:T(8,128)} %param.28) | copy-start | bytes 393220
  11.3 6.1 %copy-start = (bf16[256,2048]{1,0:T(8,128)(2,1)S(1)}, bf16[256,2048]{1,0:T(8,128)(2,1)}, u32[]{:S(2)}) copy-start(bf16[256,2048]{1,0:T(8,128)(2,1)} %key_long.3) | copy-start | bytes 3145732
  11.3 6.1 %copy-start.10 = (f32[3,3,2048]{2,1,0:T(4,128)S(1)}, f32[3,3,2048]{2,1,0:T(4,128)}, u32[]{:S(2)}) copy-start(f32[3,3,2048]{2,1,0:T(4,128)} %short.7) | copy-start | bytes 221188
  11.3 6.1 %copy-start.14 = (f32[2048]{0:T(1024)S(1)}, f32[2048]{0:T(1024)}, u32[]{:S(2)}) copy-start(f32[2048]{0:T(1024)} %param.23) | copy-start | bytes 24580
  11.3 6.0 %collective-permute-start.3 = (f32[8,112]{1,0:T(8,128)S(1)}, f32[8,112]{1,0:T(8,128)S(1)}, u32[]{:S(2)}, u32[]{:S(2)}) collective-permute-start(f32[8,112]{1,0:T(8,128)S(1)} %get-tuple-element.30.refs_4_), channel_id=1, source_target_pairs={{0,3},{1,2},{2,1},{3,0},{4,7},{5,6},{6,5},{7,4},{8,11},{9,10},{10,... | collective-permute-start | bytes 10760 | tf_op jit(solution)/shard_map/ppermute | solution.py:572
  12.0 5.3 %collective-permute-start.2 = (f32[8,112]{1,0:T(8,128)S(1)}, f32[8,112]{1,0:T(8,128)S(1)}, u32[]{:S(2)}, u32[]{:S(2)}) collective-permute-start(f32[8,112]{1,0:T(8,128)S(1)} %get-tuple-element.30.refs_4_), channel_id=1, source_target_pairs={{0,2},{1,3},{2,0},{3,1},{4,6},{5,7},{6,4},{7,5},{8,10},{9,11},{10,... | collective-permute-start | bytes 10760 | tf_op jit(solution)/shard_map/ppermute | solution.py:572
  12.9 4.4 %collective-permute-start.1 = (f32[8,112]{1,0:T(8,128)S(1)}, f32[8,112]{1,0:T(8,128)S(1)}, u32[]{:S(2)}, u32[]{:S(2)}) collective-permute-start(f32[8,112]{1,0:T(8,128)S(1)} %get-tuple-element.30.refs_4_), channel_id=1, source_target_pairs={{0,1},{1,0},{2,3},{3,2},{4,5},{5,4},{6,7},{7,6},{8,9},{9,8},{10,11... | collective-permute-start | bytes 10760 | tf_op jit(solution)/shard_map/ppermute | solution.py:572
  22.3 3.8 %collective-permute-start.6 = (f32[8,152]{1,0:T(8,128)S(1)}, f32[8,152]{1,0:T(8,128)S(1)}, u32[]{:S(2)}, u32[]{:S(2)}) collective-permute-start(f32[8,152]{1,0:T(8,128)S(1)} %get-tuple-element.40), channel_id=1, source_target_pairs={{0,3},{1,2},{2,1},{3,0},{4,7},{5,6},{6,5},{7,4},{8,11},{9,10},{10,... | collective-permute-start | bytes 14600 | tf_op jit(solution)/shard_map/ppermute | solution.py:572
  22.4 3.8 %collective-permute-start.5 = (f32[8,152]{1,0:T(8,128)S(1)}, f32[8,152]{1,0:T(8,128)S(1)}, u32[]{:S(2)}, u32[]{:S(2)}) collective-permute-start(f32[8,152]{1,0:T(8,128)S(1)} %get-tuple-element.40), channel_id=1, source_target_pairs={{0,2},{1,3},{2,0},{3,1},{4,6},{5,7},{6,4},{7,5},{8,10},{9,11},{10,... | collective-permute-start | bytes 14600 | tf_op jit(solution)/shard_map/ppermute | solution.py:572
  23.9 2.3 %collective-permute-start.4 = (f32[8,152]{1,0:T(8,128)S(1)}, f32[8,152]{1,0:T(8,128)S(1)}, u32[]{:S(2)}, u32[]{:S(2)}) collective-permute-start(f32[8,152]{1,0:T(8,128)S(1)} %get-tuple-element.40), channel_id=1, source_target_pairs={{0,1},{1,0},{2,3},{3,2},{4,5},{5,4},{6,7},{7,6},{8,9},{9,8},{10,11... | collective-permute-start | bytes 14600 | tf_op jit(solution)/shard_map/ppermute | solution.py:572
  26.2 5.8 %copy-start.15 = (f32[2048]{0:T(1024)S(1)}, f32[2048]{0:T(1024)}, u32[]{:S(2)}) copy-start(f32[2048]{0:T(1024)} %param.29) | copy-start | bytes 24580
  28.4 6.0 %collective-permute-start.9 = (bf16[16,2048]{1,0:T(8,128)(2,1)S(1)}, bf16[16,2048]{1,0:T(8,128)(2,1)S(1)}, u32[]{:S(2)}, u32[]{:S(2)}) collective-permute-start(bf16[16,2048]{1,0:T(8,128)(2,1)S(1)} %convert_element_type.18), channel_id=1, source_target_pairs={{0,12},{4,8},{8,4},{12,0},{16,28},{20,24},{24,20},{28,16},{1,13},{... | collective-permute-start | bytes 196616 | tf_op jit(solution)/shard_map/ppermute | solution.py:572
  29.2 5.1 %collective-permute-start.8 = (bf16[16,2048]{1,0:T(8,128)(2,1)S(1)}, bf16[16,2048]{1,0:T(8,128)(2,1)S(1)}, u32[]{:S(2)}, u32[]{:S(2)}) collective-permute-start(bf16[16,2048]{1,0:T(8,128)(2,1)S(1)} %convert_element_type.18), channel_id=1, source_target_pairs={{0,8},{4,12},{8,0},{12,4},{16,24},{20,28},{24,16},{28,20},{1,9},{5... | collective-permute-start | bytes 196616 | tf_op jit(solution)/shard_map/ppermute | solution.py:572
  30.5 4.5 %collective-permute-start.7 = (bf16[16,2048]{1,0:T(8,128)(2,1)S(1)}, bf16[16,2048]{1,0:T(8,128)(2,1)S(1)}, u32[]{:S(2)}, u32[]{:S(2)}) collective-permute-start(bf16[16,2048]{1,0:T(8,128)(2,1)S(1)} %convert_element_type.18), channel_id=1, source_target_pairs={{0,4},{4,0},{8,12},{12,8},{16,20},{20,16},{24,28},{28,24},{1,5},{5... | collective-permute-start | bytes 196616 | tf_op jit(solution)/shard_map/ppermute | solution.py:572
  35.1 5.9 %collective-permute-start.10 = (bf16[16,2048]{1,0:T(8,128)(2,1)S(1)}, bf16[16,2048]{1,0:T(8,128)(2,1)S(1)}, u32[]{:S(2)}, u32[]{:S(2)}) collective-permute-start(bf16[16,2048]{1,0:T(8,128)(2,1)S(1)} %get-tuple-element.58._), channel_id=1, source_target_pairs={{0,16},{4,20},{8,24},{12,28},{16,0},{20,4},{24,8},{28,12},{1,17},{... | collective-permute-start | bytes 196616 | tf_op jit(solution)/shard_map/ppermute | solution.py:572
  (4 other events, 18.3 us)

commit v5 on v4

--- a/solution.py
+++ b/solution.py
@@ -44,7 +44,7 @@
     angle = angles(times)
     late = np.concatenate([np.cos(angle), -np.sin(angle)], 0).T / BLOCK
     late = late * ((times >= BLOCK - 4) & (times < 2 * BLOCK - 1))[:, None]
-    return exact_rows, split_rows, backward, np.concatenate(split_np(late), 0)
+    return exact_rows, split_rows, backward, split_np(late)[0]
 
 
 def dot(a, b):
@@ -325,7 +325,7 @@
         end = jnp.where(row >= 6, start, halo_part[-TILE:])
         window = jnp.concatenate([halo_part[RIM:-TILE], end], 0).astype(BF16)
         spectrum = times(taps_hat[:, here], forward_exact(exact_rows[...], window))
-        late = backward_exact(backward[...], spectrum)
+        late = dot(backward[...], spectrum.astype(BF16))
         tap_a, tap_b, tap_c = (tail[i : i + 1] for i in (7, 6, 5))
         far_a, far_b, far_c = (rim_late[i : i + 1] for i in (5, 6, 7))
         skip_part = skip[:, here]

time: 44.5 us -> 44.4 us (level)
  no operation moved by 1% of the time
where the time goes in v5:
time: 44.4 us; the launch traced here: 44.3 us
  Pallas kernels  27.7 us (62%)
  starting transfers between devices  11.3 us (25%)
  waiting for transfers between devices  3.82 us (9%)
  between operations  1.18 us (3%)
    ppermute x10, starting transfers between devices, exchanged(): lax.ppermute(value, axis, [(source, source ^ flip) for source in range(co...  7.84 us
    pallas_call x1, Pallas kernels, body(): call(own_kernel, 'own', [KEPT] * 10, [arr((EARLY, width), F32), arr((EARL...  4.85 us
    pallas_call x1, Pallas kernels, body(): call(lambda *refs: impulse_kernel(count, *refs), 'impulse', [SCALAR] + [K...  4 us
    pallas_call x1, Pallas kernels, body(): call(near_kernel, 'near', [KEPT] * 7, [arr((rows, width), F32), arr((rows...  3.74 us
    ppermute x1, starting transfers between devices, passed_along(): lax.ppermute(value, axis, [(source, source + steps) for source in range(c...  3.43 us
    pallas_call x1, Pallas kernels, body(): call(lambda *refs: finish_kernel(count, *refs), 'finish', [SCALAR] + [KEP...  3.13 us
    pallas_call x1, Pallas kernels, body(): call(local_kernel, 'local', [KEPT] * 6, [arr((rows, width), F32), arr((1,...  2.46 us
    ppermute x10, waiting for transfers between devices, exchanged(): lax.ppermute(value, axis, [(source, source ^ flip) for source in range(co...  2.29 us
  transfers between devices with their start and end apart: 11, of which 3 were waited for; matrix products, arithmetic and copies ran while one was open for 0% of the time, Pallas kernels for 42%

profile of v5, /device:TPU:24, one launch (start us, length us, event | category | flops | bytes accessed | tf_op | source)
XLA Modules:
  0.0 44.3 jit_solution(6567450222335905679)
XLA Ops:
  0.7 2.2 %pack.1._ = bf16[144,2048]{1,0:T(8,128)(2,1)S(1)} custom-call(s32[1]{0:T(128)} %bitcast._.refs_0_, bf16[256,2048]{1,0:T(8,128)(2,1)} %key.3, bf16[256,2048]{1,0:T(8,128)(2,1)} %value.4, bf16[256,2048]{1,0:T(8,128)(2,1)} %gate.3, bf16[256,2048]{1,0:T(8,128)(2,1)} %gate_long.3, bf16[256,2048]{1,0:T(8,128)(2,1)} %key_long.3, f32[3,3,2048]{2,1,0:T(4,128)} %short.6), custom_call_target="tpu_custom_call" | custom-call | tf_op jit(solution)/shard_map/pack/pallas_call | solution.py:648
  2.9 3.4 %collective-permute-start = (bf16[144,2048]{1,0:T(8,128)(2,1)S(1)}, bf16[144,2048]{1,0:T(8,128)(2,1)S(1)}, u32[]{:S(2)}, u32[]{:S(2)}) collective-permute-start(bf16[144,2048]{1,0:T(8,128)(2,1)S(1)} %pack.1._), channel_id=1, source_target_pairs={{0,4},{4,8},{8,12},{12,16},{16,20},{20,24},{24,28},{1,5},{5,9},{9,... | collective-permute-start | bytes 1769480 | tf_op jit(solution)/shard_map/ppermute | solution.py:567
  6.5 4.9 %own.1 = (f32[144,2048]{1,0:T(8,128)S(1)}, f32[144,2048]{1,0:T(8,128)S(1)}, bf16[112,2048]{1,0:T(8,128)(2,1)S(1)}, f32[8,112]{1,0:T(8,128)S(1)}, f32[256,2048]{1,0:T(8,128)S(1)}, /*index=5*/f32[32,2048]{1,0:T(8,128)S(1)}) custom-call(bf16[256,2048]{1,0:T(8,128)(2,1)S(1)} %copy-done.4, bf16[256,2048]{1,0:T(8,128)(2,1)S(1)} %copy-done.2, ...), custom_call_target="tpu_custom_call" | custom-call | flops 1048576000 | bytes 5242880 | tf_op jit(solution)/shard_map/own/pallas_call | solution.py:660
  11.3 0.7 %collective-permute-start.3 = (f32[8,112]{1,0:T(8,128)S(1)}, f32[8,112]{1,0:T(8,128)S(1)}, u32[]{:S(2)}, u32[]{:S(2)}) collective-permute-start(f32[8,112]{1,0:T(8,128)S(1)} %get-tuple-element.30.refs_4_), channel_id=1, source_target_pairs={{0,3},{1,2},{2,1},{3,0},{4,7},{5,6},{6,5},{7,4},{8,11},{9,10},{10,... | collective-permute-start | bytes 10760 | tf_op jit(solution)/shard_map/ppermute | solution.py:572
  12.0 0.9 %collective-permute-start.2 = (f32[8,112]{1,0:T(8,128)S(1)}, f32[8,112]{1,0:T(8,128)S(1)}, u32[]{:S(2)}, u32[]{:S(2)}) collective-permute-start(f32[8,112]{1,0:T(8,128)S(1)} %get-tuple-element.30.refs_4_), channel_id=1, source_target_pairs={{0,2},{1,3},{2,0},{3,1},{4,6},{5,7},{6,4},{7,5},{8,10},{9,11},{10,... | collective-permute-start | bytes 10760 | tf_op jit(solution)/shard_map/ppermute | solution.py:572
  12.9 0.3 collective-permute-start.1
  13.3 4.0 %impulse.1 = (f32[2,256,2048]{2,1,0:T(8,128)S(1)}, f32[12,16,2048]{2,1,0:T(8,128)S(1)}, f32[16,8,2048]{2,1,0:T(8,128)S(1)}, f32[16,8,2048]{2,1,0:T(8,128)S(1)}, f32[16,8,2048]{2,1,0:T(8,128)S(1)}) custom-call(s32[1]{0:T(128)} %bitcast._.refs_0_, f32[16,2048]{1,0:T(8,128)S(1)} %copy-done.8, f32[16,2048]{1,0:T(8,128)S(1)} %sqrt_multiply_fusion.refs_2_, ...), custom_call_target="tpu_custom_call" | custom-call | flops 1048576000 | bytes 5242880 | tf_op jit(solution)/shard_map/impulse/pallas_call | solution.py:675
  17.4 1.8 %late.1 = (bf16[96,2048]{1,0:T(8,128)(2,1)S(1)}, f32[16,2048]{1,0:T(8,128)S(1)}, f32[112,128]{1,0:T(8,128)S(1)}) custom-call(f32[8,112]{1,0:T(8,128)S(1)} %add_add_fusion.1.refs_0_, bf16[112,2048]{1,0:T(8,128)(2,1)S(1)} %get-tuple-element.36.refs_1_.mixed_late, bf16[256,2048]{1,0:T(8,128)(2,1)S(1)} %copy-done, f32[1,2048]{1,0:T(1,128)S(1)} %bitcast.39, ...), custom_call_target="tpu_custom_call" | custom-call | flops 52428800 | bytes 5242880 | tf_op jit(solution)/shard_map/late/pallas_call | solution.py:687
  19.2 1.5 %collective-permute-done.halo = bf16[144,2048]{1,0:T(8,128)(2,1)S(1)} collective-permute-done((bf16[144,2048]{1,0:T(8,128)(2,1)S(1)}, bf16[144,2048]{1,0:T(8,128)(2,1)S(1)}, u32[]{:S(2)}, u32[]{:S(2)}) %collective-permute-start) | collective-permute-done | bytes 589856 | tf_op jit(solution)/shard_map/ppermute | solution.py:567
  20.8 1.4 %medium.1 = (bf16[256,2048]{1,0:T(8,128)(2,1)S(1)}, f32[8,2048]{1,0:T(8,128)S(1)}, f32[8,152]{1,0:T(8,128)S(1)}, f32[8,2048]{1,0:T(8,128)S(1)}) custom-call(bf16[144,2048]{1,0:T(8,128)(2,1)S(1)} %collective-permute-done.halo, f32[32,2048]{1,0:T(8,128)S(1)} %get-tuple-element.32.heads, f32[3,3,2048]{2,1,0:T(4,128)S(1)} %copy-done.7, f32[1,2048]{1,0:T(1,128)S(1)} %bitcast.38, ...), custom_call_target="tpu_custom_call" | custom-call | flops 524288000 | bytes 5242880 | tf_op jit(solution)/shard_map/medium/pallas_call | solution.py:696
  22.3 1.5 %collective-permute-start.5 = (f32[8,152]{1,0:T(8,128)S(1)}, f32[8,152]{1,0:T(8,128)S(1)}, u32[]{:S(2)}, u32[]{:S(2)}) collective-permute-start(f32[8,152]{1,0:T(8,128)S(1)} %get-tuple-element.40), channel_id=1, source_target_pairs={{0,2},{1,3},{2,0},{3,1},{4,6},{5,7},{6,4},{7,5},{8,10},{9,11},{10,... | collective-permute-start | bytes 14600 | tf_op jit(solution)/shard_map/ppermute | solution.py:572
  23.8 0.3 collective-permute-start.4
  24.1 1.9 %value.5 = (f32[3,160,2048]{2,1,0:T(8,128)S(1)}, f32[16,8,2048]{2,1,0:T(8,128)S(1)}, f32[256,2048]{1,0:T(8,128)S(1)}) custom-call(bf16[256,2048]{1,0:T(8,128)(2,1)S(1)} %get-tuple-element.42.mixed, f32[8,2048]{1,0:T(8,128)S(1)} %get-tuple-element.43.mixed_rim, f32[1,2048]{1,0:T(1,128)S(1)} %bitcast.40, bf16[256,2048]{1,0:T(8,128)(2,1)S(1)} %copy-done, ...), custom_call_target="tpu_custom_call" | custom-call | flops 524288000 | bytes 5242880 | tf_op jit(solution)/shard_map/value/pallas_call | solution.py:710
  26.1 2.2 %state.1 = (bf16[160,2048]{1,0:T(8,128)(2,1)S(1)}, f32[16,2048]{1,0:T(8,128)S(1)}) custom-call(f32[8,152]{1,0:T(8,128)S(1)} %add_add_fusion.refs_0_, f32[112,128]{1,0:T(8,128)S(1)} %get-tuple-element.41.refs_1_, f32[3,160,2048]{2,1,0:T(8,128)S(1)} %get-tuple-element.45.refs_2_, f32[16,8,2048]{2,1,0:T(8,128)S(1)} %get-tuple-element.46.refs_3_, ...), custom_call_target="tpu_custom_call" | custom-call | flops 52428800 | bytes 5242880 | tf_op jit(solution)/shard_map/state/pallas_call | solution.py:718
  28.3 0.9 %collective-permute-start.9 = (bf16[16,2048]{1,0:T(8,128)(2,1)S(1)}, bf16[16,2048]{1,0:T(8,128)(2,1)S(1)}, u32[]{:S(2)}, u32[]{:S(2)}) collective-permute-start(bf16[16,2048]{1,0:T(8,128)(2,1)S(1)} %convert_element_type.18), channel_id=1, source_target_pairs={{0,12},{4,8},{8,4},{12,0},{16,28},{20,24},{24,20},{28,16},{1,13},{... | collective-permute-start | bytes 196616 | tf_op jit(solution)/shard_map/ppermute | solution.py:572
  29.2 1.2 %collective-permute-start.8 = (bf16[16,2048]{1,0:T(8,128)(2,1)S(1)}, bf16[16,2048]{1,0:T(8,128)(2,1)S(1)}, u32[]{:S(2)}, u32[]{:S(2)}) collective-permute-start(bf16[16,2048]{1,0:T(8,128)(2,1)S(1)} %convert_element_type.18), channel_id=1, source_target_pairs={{0,8},{4,12},{8,0},{12,4},{16,24},{20,28},{24,16},{28,20},{1,9},{5... | collective-permute-start | bytes 196616 | tf_op jit(solution)/shard_map/ppermute | solution.py:572
  30.4 1.4 %collective-permute-start.7 = (bf16[16,2048]{1,0:T(8,128)(2,1)S(1)}, bf16[16,2048]{1,0:T(8,128)(2,1)S(1)}, u32[]{:S(2)}, u32[]{:S(2)}) collective-permute-start(bf16[16,2048]{1,0:T(8,128)(2,1)S(1)} %convert_element_type.18), channel_id=1, source_target_pairs={{0,4},{4,0},{8,12},{12,8},{16,20},{20,16},{24,28},{28,24},{1,5},{5... | collective-permute-start | bytes 196616 | tf_op jit(solution)/shard_map/ppermute | solution.py:572
  31.8 2.5 %local.1 = (f32[256,2048]{1,0:T(8,128)S(1)}, f32[1,2048]{1,0:T(1,128)S(1)}) custom-call(bf16[160,2048]{1,0:T(8,128)(2,1)S(1)} %get-tuple-element.49.early, bf16[96,2048]{1,0:T(8,128)(2,1)S(1)} %get-tuple-element.50.late, f32[2,256,2048]{2,1,0:T(8,128)S(1)} %get-tuple-element.51.long_hat, f32[1,2048]{1,0:T(1,128)S(1)} %bitcast.41, ...), custom_call_target="tpu_custom_call" | custom-call | flops 1048576000 | bytes 7340032 | tf_op jit(solution)/shard_map/local/pallas_call | solution.py:725
  34.3 0.6 %collective-permute-done.7 = bf16[16,2048]{1,0:T(8,128)(2,1)S(1)} collective-permute-done((bf16[16,2048]{1,0:T(8,128)(2,1)S(1)}, bf16[16,2048]{1,0:T(8,128)(2,1)S(1)}, u32[]{:S(2)}, u32[]{:S(2)}) %collective-permute-start.7) | collective-permute-done | bytes 65568 | tf_op jit(solution)/shard_map/ppermute | solution.py:572
  34.9 0.1 fusion.8
  35.0 0.5 %collective-permute-start.10 = (bf16[16,2048]{1,0:T(8,128)(2,1)S(1)}, bf16[16,2048]{1,0:T(8,128)(2,1)S(1)}, u32[]{:S(2)}, u32[]{:S(2)}) collective-permute-start(bf16[16,2048]{1,0:T(8,128)(2,1)S(1)} %get-tuple-element.58._), channel_id=1, source_target_pairs={{0,16},{4,20},{8,24},{12,28},{16,0},{20,4},{24,8},{28,12},{1,17},{... | collective-permute-start | bytes 196616 | tf_op jit(solution)/shard_map/ppermute | solution.py:572
  35.5 3.7 %near.1 = (f32[256,2048]{1,0:T(8,128)S(1)}, bf16[256,2048]{1,0:T(8,128)(2,1)}, bf16[256,2048]{1,0:T(8,128)(2,1)}) custom-call(f32[16,2048]{1,0:T(8,128)S(1)} %get-tuple-element.60.state, f32[16,8,2048]{2,1,0:T(8,128)S(1)} %get-tuple-element.37.refs_5_.refs_4_.decays.refs_2_, f32[16,8,2048]{2,1,0:T(8,128)S(1)} %get-tuple-element.48.leads.refs_3_, ...), custom_call_target="tpu_custom_call" | custom-call | flops 524288000 | bytes 7340032 | tf_op jit(solution)/shard_map/near/pallas_call | solution.py:730
  39.3 1.7 %collective-permute-done.10 = bf16[16,2048]{1,0:T(8,128)(2,1)S(1)} collective-permute-done((bf16[16,2048]{1,0:T(8,128)(2,1)S(1)}, bf16[16,2048]{1,0:T(8,128)(2,1)S(1)}, u32[]{:S(2)}, u32[]{:S(2)}) %collective-permute-start.10) | collective-permute-done | bytes 65568 | tf_op jit(solution)/shard_map/ppermute | solution.py:572
  41.0 3.1 %finish.1 = bf16[256,2048]{1,0:T(8,128)(2,1)} custom-call(s32[1]{0:T(128)} %bitcast._.refs_0_, f32[16,2048]{1,0:T(8,128)S(1)} %fusion.7.refs_1_, f32[16,8,2048]{2,1,0:T(8,128)S(1)} %get-tuple-element.37.refs_5_.refs_4_.decays.refs_2_, f32[16,8,2048]{2,1,0:T(8,128)S(1)} %get-tuple-element.48.leads.refs_3_, ...), custom_call_target="tpu_custom_call", output_to_operand_aliasing={{}: (6, {})} | custom-call | flops 52428800 | bytes 4194304 | tf_op jit(solution)/shard_map/finish/pallas_call | solution.py:739
  (48 shorter events, 0.3 us)
Async XLA Ops:
  0.6 5.7 %copy-start.2 = (bf16[256,2048]{1,0:T(8,128)(2,1)S(1)}, bf16[256,2048]{1,0:T(8,128)(2,1)}, u32[]{:S(2)}) copy-start(bf16[256,2048]{1,0:T(8,128)(2,1)} %key.3) | copy-start | bytes 3145732
  0.6 5.7 %copy-start.3 = (bf16[256,2048]{1,0:T(8,128)(2,1)S(1)}, bf16[256,2048]{1,0:T(8,128)(2,1)}, u32[]{:S(2)}) copy-start(bf16[256,2048]{1,0:T(8,128)(2,1)} %value.4) | copy-start | bytes 3145732
  0.7 5.7 %copy-start.4 = (bf16[256,2048]{1,0:T(8,128)(2,1)S(1)}, bf16[256,2048]{1,0:T(8,128)(2,1)}, u32[]{:S(2)}) copy-start(bf16[256,2048]{1,0:T(8,128)(2,1)} %gate.3) | copy-start | bytes 3145732
  0.7 5.7 %copy-start.5 = (bf16[256,256]{1,0:T(8,128)(2,1)S(1)}, bf16[256,256]{1,0:T(8,128)(2,1)}, u32[]{:S(2)}) copy-start(bf16[256,256]{1,0:T(8,128)(2,1)} %constant.16.clone.exact_rows.refs_3_) | copy-start | bytes 393220
  0.7 5.7 %copy-start.6 = (f32[128,2048]{1,0:T(8,128)S(1)}, f32[128,2048]{1,0:T(8,128)}, u32[]{:S(2)}) copy-start(f32[128,2048]{1,0:T(8,128)} %taps.1) | copy-start | bytes 3145732
  0.7 5.7 %copy-start.7 = (f32[3,3,2048]{2,1,0:T(4,128)S(1)}, f32[3,3,2048]{2,1,0:T(4,128)}, u32[]{:S(2)}) copy-start(f32[3,3,2048]{2,1,0:T(4,128)} %short.6) | copy-start | bytes 221188
  0.7 5.7 %copy-start.9 = (bf16[256,256]{1,0:T(8,128)(2,1)S(1)}, bf16[256,256]{1,0:T(8,128)(2,1)}, u32[]{:S(2)}) copy-start(bf16[256,256]{1,0:T(8,128)(2,1)} %constant.18.clone.backward) | copy-start | bytes 393220
  2.9 17.9 %collective-permute-start = (bf16[144,2048]{1,0:T(8,128)(2,1)S(1)}, bf16[144,2048]{1,0:T(8,128)(2,1)S(1)}, u32[]{:S(2)}, u32[]{:S(2)}) collective-permute-start(bf16[144,2048]{1,0:T(8,128)(2,1)S(1)} %pack.1._), channel_id=1, source_target_pairs={{0,4},{4,8},{8,12},{12,16},{16,20},{20,24},{24,28},{1,5},{5,9},{9,... | collective-permute-start | bytes 1769480 | tf_op jit(solution)/shard_map/ppermute | solution.py:567
  6.4 6.8 %copy-start.8 = (f32[16,2048]{1,0:T(8,128)S(1)}, f32[16,2048]{1,0:T(8,128)}, u32[]{:S(2)}) copy-start(f32[16,2048]{1,0:T(8,128)} %rates.1) | copy-start | bytes 393220
  6.5 6.8 %copy-start.16 = (f32[16,2048]{1,0:T(8,128)S(1)}, f32[16,2048]{1,0:T(8,128)}, u32[]{:S(2)}) copy-start(f32[16,2048]{1,0:T(8,128)} %param.28) | copy-start | bytes 393220
  11.3 6.1 %copy-start = (bf16[256,2048]{1,0:T(8,128)(2,1)S(1)}, bf16[256,2048]{1,0:T(8,128)(2,1)}, u32[]{:S(2)}) copy-start(bf16[256,2048]{1,0:T(8,128)(2,1)} %key_long.3) | copy-start | bytes 3145732
  11.3 6.1 %copy-start.10 = (f32[3,3,2048]{2,1,0:T(4,128)S(1)}, f32[3,3,2048]{2,1,0:T(4,128)}, u32[]{:S(2)}) copy-start(f32[3,3,2048]{2,1,0:T(4,128)} %short.7) | copy-start | bytes 221188
  11.3 6.1 %copy-start.14 = (f32[2048]{0:T(1024)S(1)}, f32[2048]{0:T(1024)}, u32[]{:S(2)}) copy-start(f32[2048]{0:T(1024)} %param.23) | copy-start | bytes 24580
  11.3 6.0 %collective-permute-start.3 = (f32[8,112]{1,0:T(8,128)S(1)}, f32[8,112]{1,0:T(8,128)S(1)}, u32[]{:S(2)}, u32[]{:S(2)}) collective-permute-start(f32[8,112]{1,0:T(8,128)S(1)} %get-tuple-element.30.refs_4_), channel_id=1, source_target_pairs={{0,3},{1,2},{2,1},{3,0},{4,7},{5,6},{6,5},{7,4},{8,11},{9,10},{10,... | collective-permute-start | bytes 10760 | tf_op jit(solution)/shard_map/ppermute | solution.py:572
  12.0 5.3 %collective-permute-start.2 = (f32[8,112]{1,0:T(8,128)S(1)}, f32[8,112]{1,0:T(8,128)S(1)}, u32[]{:S(2)}, u32[]{:S(2)}) collective-permute-start(f32[8,112]{1,0:T(8,128)S(1)} %get-tuple-element.30.refs_4_), channel_id=1, source_target_pairs={{0,2},{1,3},{2,0},{3,1},{4,6},{5,7},{6,4},{7,5},{8,10},{9,11},{10,... | collective-permute-start | bytes 10760 | tf_op jit(solution)/shard_map/ppermute | solution.py:572
  12.9 4.4 %collective-permute-start.1 = (f32[8,112]{1,0:T(8,128)S(1)}, f32[8,112]{1,0:T(8,128)S(1)}, u32[]{:S(2)}, u32[]{:S(2)}) collective-permute-start(f32[8,112]{1,0:T(8,128)S(1)} %get-tuple-element.30.refs_4_), channel_id=1, source_target_pairs={{0,1},{1,0},{2,3},{3,2},{4,5},{5,4},{6,7},{7,6},{8,9},{9,8},{10,11... | collective-permute-start | bytes 10760 | tf_op jit(solution)/shard_map/ppermute | solution.py:572
  22.2 3.8 %collective-permute-start.6 = (f32[8,152]{1,0:T(8,128)S(1)}, f32[8,152]{1,0:T(8,128)S(1)}, u32[]{:S(2)}, u32[]{:S(2)}) collective-permute-start(f32[8,152]{1,0:T(8,128)S(1)} %get-tuple-element.40), channel_id=1, source_target_pairs={{0,3},{1,2},{2,1},{3,0},{4,7},{5,6},{6,5},{7,4},{8,11},{9,10},{10,... | collective-permute-start | bytes 14600 | tf_op jit(solution)/shard_map/ppermute | solution.py:572
  22.3 3.7 %collective-permute-start.5 = (f32[8,152]{1,0:T(8,128)S(1)}, f32[8,152]{1,0:T(8,128)S(1)}, u32[]{:S(2)}, u32[]{:S(2)}) collective-permute-start(f32[8,152]{1,0:T(8,128)S(1)} %get-tuple-element.40), channel_id=1, source_target_pairs={{0,2},{1,3},{2,0},{3,1},{4,6},{5,7},{6,4},{7,5},{8,10},{9,11},{10,... | collective-permute-start | bytes 14600 | tf_op jit(solution)/shard_map/ppermute | solution.py:572
  23.8 2.3 %collective-permute-start.4 = (f32[8,152]{1,0:T(8,128)S(1)}, f32[8,152]{1,0:T(8,128)S(1)}, u32[]{:S(2)}, u32[]{:S(2)}) collective-permute-start(f32[8,152]{1,0:T(8,128)S(1)} %get-tuple-element.40), channel_id=1, source_target_pairs={{0,1},{1,0},{2,3},{3,2},{4,5},{5,4},{6,7},{7,6},{8,9},{9,8},{10,11... | collective-permute-start | bytes 14600 | tf_op jit(solution)/shard_map/ppermute | solution.py:572
  26.1 5.8 %copy-start.15 = (f32[2048]{0:T(1024)S(1)}, f32[2048]{0:T(1024)}, u32[]{:S(2)}) copy-start(f32[2048]{0:T(1024)} %param.29) | copy-start | bytes 24580
  28.3 6.0 %collective-permute-start.9 = (bf16[16,2048]{1,0:T(8,128)(2,1)S(1)}, bf16[16,2048]{1,0:T(8,128)(2,1)S(1)}, u32[]{:S(2)}, u32[]{:S(2)}) collective-permute-start(bf16[16,2048]{1,0:T(8,128)(2,1)S(1)} %convert_element_type.18), channel_id=1, source_target_pairs={{0,12},{4,8},{8,4},{12,0},{16,28},{20,24},{24,20},{28,16},{1,13},{... | collective-permute-start | bytes 196616 | tf_op jit(solution)/shard_map/ppermute | solution.py:572
  29.2 5.1 %collective-permute-start.8 = (bf16[16,2048]{1,0:T(8,128)(2,1)S(1)}, bf16[16,2048]{1,0:T(8,128)(2,1)S(1)}, u32[]{:S(2)}, u32[]{:S(2)}) collective-permute-start(bf16[16,2048]{1,0:T(8,128)(2,1)S(1)} %convert_element_type.18), channel_id=1, source_target_pairs={{0,8},{4,12},{8,0},{12,4},{16,24},{20,28},{24,16},{28,20},{1,9},{5... | collective-permute-start | bytes 196616 | tf_op jit(solution)/shard_map/ppermute | solution.py:572
  30.4 4.5 %collective-permute-start.7 = (bf16[16,2048]{1,0:T(8,128)(2,1)S(1)}, bf16[16,2048]{1,0:T(8,128)(2,1)S(1)}, u32[]{:S(2)}, u32[]{:S(2)}) collective-permute-start(bf16[16,2048]{1,0:T(8,128)(2,1)S(1)} %convert_element_type.18), channel_id=1, source_target_pairs={{0,4},{4,0},{8,12},{12,8},{16,20},{20,16},{24,28},{28,24},{1,5},{5... | collective-permute-start | bytes 196616 | tf_op jit(solution)/shard_map/ppermute | solution.py:572
  35.0 5.9 %collective-permute-start.10 = (bf16[16,2048]{1,0:T(8,128)(2,1)S(1)}, bf16[16,2048]{1,0:T(8,128)(2,1)S(1)}, u32[]{:S(2)}, u32[]{:S(2)}) collective-permute-start(bf16[16,2048]{1,0:T(8,128)(2,1)S(1)} %get-tuple-element.58._), channel_id=1, source_target_pairs={{0,16},{4,20},{8,24},{12,28},{16,0},{20,4},{24,8},{28,12},{1,17},{... | collective-permute-start | bytes 196616 | tf_op jit(solution)/shard_map/ppermute | solution.py:572
  (4 other events, 18.2 us)
